TPU v7x, 32 devices: a whole 2x2x4 slice. The times are simulated.
32 devices in a mesh: group: 2 (over x), expert: 8 (over z, y), dp: 2 (over core).
Axes of the slice: x: 2, y: 2, z: 4, core: 2. Of those that a mesh axis runs over, the one named last changes fastest.
Arguments:
- tokens: bfloat16 [4096, 3584], P(('group', 'expert', 'dp')), parts along dimension 0, may hold values from -6 to 6
- expert_ids: int32 [4096, 4], P(('group', 'expert', 'dp')), parts along dimension 0, may hold values from 0 to 7, as said below
- combine: float32 [4096, 4], P(('group', 'expert', 'dp')), parts along dimension 0, may hold values from 0.1 to 1
- hot_list: int32 [2], P('group'), parts along dimension 0, may hold values from 0 to 7, as said below
- in_weight: bfloat16 [8, 2, 3584, 1024], P('expert', None, None, 'dp'), may hold values from -0.09375 to 0.09375
- in_scale: float32 [8, 2, 28, 8], P('expert', None, None, 'dp'), may hold values from 0.5 to 2
- out_weight: bfloat16 [8, 1024, 3584], P('expert', 'dp'), may hold values from -0.1875 to 0.1875
- out_scale: float32 [8, 8, 28], P('expert', 'dp'), may hold values from 0.5 to 2
Outputs:
- mixed: bfloat16 [4096, 3584], P(('group', 'expert', 'dp')), parts along dimension 0
There are 2 independent parts, one for each index of `group`. A program takes and returns all parts, laid end to end along the dimension named above; an argument that names none is the same for every part. Nothing has to cross between parts.
Inputs may be any that keep to these rules, and one draw needn't show every extreme that they name: `expert_ids`: each row names 4 different experts. `hot_list`: one expert per group, a valid expert id.
All inputs are finite; a program needn't handle non-finite values.
Results may differ from a plain program's by a relative error of at most 0.008.
Values may be sent and summed in bfloat16 or wider, within the bound.
No kernel may reach another device: no remote copies, remote signals or barrier semaphores. Data moves between devices by JAX's collectives and lax.ppermute only.
A program may use at most 192 MiB of HBM per device.

v0:
```python
import jax
import jax.numpy as jnp
from jax import lax
from jax.sharding import PartitionSpec as P

QB = 128


def spread(array, axis, root):
    mine = lax.axis_index(axis) == root
    return lax.psum(jnp.where(mine, array, jnp.zeros_like(array)), axis)


def dequantize(raw_weight, raw_scale, tile_size):
    array_shape = raw_weight.shape
    tiled = raw_weight.astype(jnp.float32).reshape(
        array_shape[:-2]
        + (array_shape[-2] // tile_size, tile_size, array_shape[-1] // tile_size, tile_size)
    )
    return (tiled * raw_scale[..., :, None, :, None]).reshape(array_shape).astype(jnp.bfloat16)


def half_product(source_rows, gate_w, up_w, down_w):
    gate_value = jnp.dot(source_rows, gate_w, preferred_element_type=jnp.float32)
    up_value = jnp.dot(source_rows, up_w, preferred_element_type=jnp.float32)
    hidden = (jax.nn.silu(gate_value) * up_value).astype(jnp.bfloat16)
    return jnp.dot(hidden, down_w, preferred_element_type=jnp.float32)


def shards(tokens, expert_ids, combine, hot_list, in_weight, in_scale, out_weight, out_scale):
    owners = lax.axis_size("expert")
    halves = lax.axis_size("dp")
    tok_rows, feat_width = tokens.shape
    top_count = expert_ids.shape[1]
    capacity = tok_rows * top_count * 3 // (4 * owners)
    hot_expert = hot_list[0]
    flat_ids = expert_ids.reshape(-1)
    one_hot = (flat_ids[:, None] == jnp.arange(owners, dtype=jnp.int32)[None, :]).astype(jnp.int32)
    slot_rank = jnp.sum(jnp.cumsum(one_hot, axis=0) * one_hot, axis=1) - 1
    routed = (flat_ids != hot_expert) & (slot_rank < capacity)
    slot_index = jnp.where(routed, flat_ids * capacity + slot_rank, owners * capacity)
    picked = tokens[jnp.arange(flat_ids.shape[0]) // top_count]
    send_rows = (
        jnp.zeros((owners * capacity, feat_width), jnp.bfloat16)
        .at[slot_index]
        .set(picked, mode="drop")
    )
    send_rows = send_rows.reshape(owners, capacity, feat_width)
    local_in = dequantize(in_weight[0], in_scale[0], QB)
    local_out = dequantize(out_weight[0], out_scale[0], QB)
    doubled = jnp.repeat(send_rows, halves, axis=0)
    arrived = lax.all_to_all(doubled, ("expert", "dp"), split_axis=0, concat_axis=0, tiled=True)
    produced = half_product(
        arrived.reshape(-1, feat_width), local_in[0], local_in[1], local_out
    ).reshape(arrived.shape)
    returned = lax.all_to_all(produced, ("expert", "dp"), split_axis=0, concat_axis=0, tiled=True)
    stride_owner = halves * capacity
    shadow_in, shadow_out = (
        spread(local_in, "expert", hot_expert),
        spread(local_out, "expert", hot_expert),
    )
    pair_rows = lax.all_gather(tokens, "dp", axis=0, tiled=True)
    shadow_part = half_product(pair_rows, shadow_in[0], shadow_in[1], shadow_out).reshape(
        halves, tok_rows, feat_width
    )
    shadow_parts = lax.all_to_all(shadow_part, "dp", split_axis=0, concat_axis=0, tiled=True)
    shadow_full = jnp.sum(shadow_parts, axis=0).astype(jnp.bfloat16)
    flat_back = returned.reshape(-1, feat_width)
    routed_rows = routed.reshape(tok_rows, top_count)
    rank_rows = jnp.clip(slot_rank, 0, capacity - 1).reshape(tok_rows, top_count)
    summed = jnp.zeros((tok_rows, feat_width), jnp.float32)
    shadow_weight = jnp.zeros((tok_rows,), jnp.float32)
    for column in range(top_count):
        chosen = expert_ids[:, column]
        pair_weight = jnp.where(routed_rows[:, column], combine[:, column], 0.0)
        gathered = jnp.zeros((tok_rows, feat_width), jnp.float32)
        for half_index in range(halves):
            flat_index = chosen * stride_owner + half_index * capacity + rank_rows[:, column]
            gathered = gathered + flat_back[flat_index]
        part_rows = gathered.astype(jnp.bfloat16).astype(jnp.float32)
        summed = summed + pair_weight[:, None] * part_rows
        shadow_weight = shadow_weight + jnp.where(chosen == hot_expert, combine[:, column], 0.0)
    summed = summed + shadow_weight[:, None] * shadow_full.astype(jnp.float32)
    return summed.astype(jnp.bfloat16)


def solution(mesh):
    placed = (
        P(("group", "expert", "dp"), None),
        P(("group", "expert", "dp"), None),
        P(("group", "expert", "dp"), None),
        P("group"),
        P("expert", None, None, "dp"),
        P("expert", None, None, "dp"),
        P("expert", "dp", None),
        P("expert", "dp", None),
    )
    return jax.shard_map(
        shards,
        mesh=mesh,
        in_specs=placed,
        out_specs=P(("group", "expert", "dp"), None),
        check_vma=False,
    )
```

profile of v0, /device:TPU:13, one launch (start us, length us, event | category | flops | bytes accessed | tf_op | source)
XLA Modules:
  0.0 835.0 jit_solution(3448456251750113181)
XLA Ops:
  13.4 15.6 %scatter_custom_fusion = bf16[384,3584]{1,0:T(8,128)(2,1)S(1)} fusion(s32[512]{0:T(512)S(1)} %bitcast.128, bf16[128,3584]{1,0:T(8,128)(2,1)} %param.8, s32[1024]{0:T(1024)S(1)} %pad_clamp_fusion.8, bf16[]{:T(256)} %constant.25.clone.1), kind=kCustom, calls=%fused_computation.28 | custom fusion | bytes 2753024 | tf_op jit(solution)/shard_map/scatter | solution.py:46
  32.0 6.7 all-to-all-start
  38.8 7.1 mul.145
  45.9 17.9 %mul.146 = f32[2,3584,512]{2,1,0:T(8,128)} reshape(f32[2,28,128,4,128]{4,3,2,1,0:T(4,128)} %mul.145) | data formatting | bytes 29360128 | tf_op jit(solution)/shard_map/mul | solution.py:20
  73.8 6.7 fusion.2
  82.4 9.7 %broadcast_select_fusion = (bf16[2,3584,512]{2,1,0:T(8,128)(2,1)}, bf16[2,3584,512]{2,1,0:T(8,128)(2,1)}) fusion(pred[]{:T(512)S(6)} %eq.64, f32[2,3584,512]{2,1,0:T(8,128)S(1)} %copy-done, bf16[1,2,3584,512]{3,2,1,0:T(8,128)(2,1)} %param.12), kind=kLoop, calls=%fused_computation.15 | loop fusion | flops 14680064 | bytes 36700160 | tf_op jit(solution)/shard_map/jit(_where)/select_n | solution.py:11
  92.1 7.6 reshape.181
  99.8 7.0 multiply_convert_fusion
  106.7 138.1 %all-to-all-done = bf16[16,48,3584]{2,1,0:T(8,128)(2,1)} async-done(((bf16[16,48,3584]{2,1,0:T(8,128)(2,1)}), bf16[16,48,3584]{2,1,0:T(8,128)(2,1)}, u32[]{:S(2)}, u32[]{:S(2)}) %all-to-all-start) | async-done | bytes 5505056 | tf_op jit(solution)/shard_map/all_to_all | solution.py:52
  244.8 6.6 fusion.8
  263.1 228.3 %all-reduce.3.cloned.1.call-done = (bf16[512,3584]{0,1:T(8,128)(2,1)}, bf16[2,3584,512]{2,1,0:T(8,128)(2,1)}) async-done(((bf16[512,3584]{0,1:T(8,128)(2,1)}, bf16[2,3584,512]{2,1,0:T(8,128)(2,1)}), (bf16[512,3584]{0,1:T(8,128)(2,1)}, bf16[2,3584,512]{2,1,0:T(8,128)(2,1)})) %all-reduce.3.cloned.1.call-update) | async-done | bytes 11010064 | tf_op jit(solution)/shard_map/psum | solution.py:11
  495.3 9.0 %fusion.16 = f32[256,3584]{1,0:T(8,128)} fusion(bf16[512,3584]{0,1:T(8,128)(2,1)} %get-tuple-element.5, bf16[256,3584]{1,0:T(8,128)(2,1)S(1)} %copy-done.7, bf16[2,3584,512]{2,1,0:T(8,128)(2,1)} %get-tuple-element.6, f32[256,512]{0,1:T(8,128)S(1)} %fusion.12), kind=kOutput, calls=%fused_computation.41 | convolution fusion | flops 1879834624 | bytes 13369344 | tf_op jit(solution)/shard_map/dot_general | solution.py:27
  504.4 11.7 %all_to_all.15 = f32[2,128,3584]{2,1,0:T(8,128)} all-to-all(f32[2,128,3584]{2,1,0:T(8,128)} %bitcast.122), channel_id=1, replica_groups=mesh['group'=2,'expert'=8,'dp'=2] {'dp'}, dimensions={0} | all-to-all | bytes 7340032 | tf_op jit(solution)/shard_map/all_to_all | solution.py:66
  516.1 7.5 all-to-all-start.1
  526.6 235.3 %all-to-all-done.1 = f32[16,48,3584]{2,1,0:T(8,128)} async-done(((f32[16,48,3584]{2,1,0:T(8,128)}), f32[16,48,3584]{2,1,0:T(8,128)}, u32[]{:S(2)}, u32[]{:S(2)}) %all-to-all-start.1) | async-done | bytes 11010080 | tf_op jit(solution)/shard_map/all_to_all | solution.py:56
  762.0 6.2 gather_fusion.3
  768.2 7.3 gather_fusion.4
  775.5 7.4 gather_fusion.5
  782.9 7.3 gather_fusion.6
  790.2 7.4 gather_fusion.7
  797.5 7.3 gather_fusion.2
  804.9 7.3 gather_fusion.1
  812.2 7.6 gather_fusion
  819.7 7.6 add_convert_fusion
  (69 shorter events, 38.8 us)
Async XLA Ops:
  7.4 255.7 %all-gather.2.cloned.1.call-start = ((), (), s32[]{:S(2)}) async-start(), calls=%async_computation.3 | async-start | bytes 2752512 | tf_op jit(solution)/shard_map/all_gather | solution.py:62
  32.0 6.7 copy-start.4
  32.0 212.8 %all-to-all-start = ((bf16[16,48,3584]{2,1,0:T(8,128)(2,1)}), bf16[16,48,3584]{2,1,0:T(8,128)(2,1)}, u32[]{:S(2)}, u32[]{:S(2)}) async-start(bf16[16,48,3584]{2,1,0:T(8,128)(2,1)} %bitcast.118), calls=%async_computation | async-start | bytes 11010048 | tf_op jit(solution)/shard_map/all_to_all | solution.py:52
  38.7 452.8 %all-reduce.3.cloned.1.call-start = ((), (), s32[]{:S(2)}) async-start(), calls=%async_computation.4 | async-start | bytes 22020096 | tf_op jit(solution)/shard_map/psum | solution.py:11
  63.8 6.0 copy-start.5
  69.8 3.9 copy-start.1
  73.8 8.6 %copy-start = (f32[2,3584,512]{2,1,0:T(8,128)S(1)}, f32[2,3584,512]{2,1,0:T(8,128)}, u32[]{:S(2)}) copy-start(f32[2,3584,512]{2,1,0:T(8,128)} %mul.146) | copy-start | bytes 44040196
  99.7 151.6 %slice-start = ((s8[7340032]{0:T(1024)(128)(4,1)}), s8[3145728]{0:T(1024)(128)(4,1)S(1)}, s32[]{:S(2)}) async-start(s8[7340032]{0:T(1024)(128)(4,1)} %bitcast.120), calls=%async_computation.5 | async-start | bytes 6291456
  244.8 6.6 slice-start.1
  251.4 5.9 copy-start.2
  491.4 3.9 copy-start.7
  516.1 8.0 copy-start.3
  516.1 8.1 copy-start.6
  516.1 245.9 %all-to-all-start.1 = ((f32[16,48,3584]{2,1,0:T(8,128)}), f32[16,48,3584]{2,1,0:T(8,128)}, u32[]{:S(2)}, u32[]{:S(2)}) async-start(f32[16,48,3584]{2,1,0:T(8,128)} %fusion.3), calls=%async_computation.1 | async-start | bytes 22020096 | tf_op jit(solution)/shard_map/all_to_all | solution.py:56
Sparse Core Ops, SparseCore 0:
  9.7 12.0 all-gather.1
Sparse Core Ops, SparseCore 1:
  92.2 399.2 all-reduce.2
where the time goes:
time: 843 us; the launch traced here: 835 us
  waiting for transfers between devices  602 us (71%)
  local copies, waits for them, and re-layouts  123 us (15%)
  other arithmetic  36.2 us (4%)
  matrix products  31.1 us (4%)
  between operations  16 us (2%)
  starting transfers between devices  14.2 us (2%)
  blocking collectives  11.7 us (1%)
    all_to_all x1, waiting for transfers between devices, shards(): lax.all_to_all(produced, ('expert', 'dp'), split_axis=0, concat_axis=0, t...  235 us
    psum x1, waiting for transfers between devices, spread(): return lax.psum(jnp.where(mine, array, jnp.zeros_like(array)), axis)  228 us
    all_to_all x1, waiting for transfers between devices, shards(): lax.all_to_all(doubled, ('expert', 'dp'), split_axis=0, concat_axis=0, ti...  138 us
    gather x8, local copies, waits for them, and re-layouts, shards(): gathered = gathered + flat_back[flat_index]  57.8 us
    mul x5, local copies, waits for them, and re-layouts, dequantize(): tiled * raw_scale[..., :, None, :, None]  29.1 us
  transfers between devices with their start and end apart: 4, of which 3 were waited for; matrix products, arithmetic and copies ran while one was open for 13% of the time, Pallas kernels for 0%

commit v1 on v0

v1 whole, which is shorter than its diff:
```python
import functools

import jax
import jax.numpy as jnp
from jax import lax
from jax.experimental import pallas as pl
from jax.experimental.pallas import tpu as pltpu
from jax.sharding import PartitionSpec as P

QB = 128
TILE_F = 256
VMEM_LIMIT = 56 * 1024 * 1024


def ring_order(mesh):
    count = mesh.shape["expert"]
    rows = 2 if count == 8 else 1
    first = [i * rows for i in range(count // rows)]
    second = [i * rows + 1 for i in reversed(range(count // rows))] if rows == 2 else []
    return first + second


def dequantize(raw_weight, raw_scale):
    shape = raw_weight.shape
    tiled = raw_weight.astype(jnp.float32).reshape(
        shape[:-2] + (shape[-2] // QB, QB, shape[-1] // QB, QB)
    )
    return (tiled * raw_scale[..., :, None, :, None]).reshape(shape).astype(jnp.bfloat16)


def route_kernel(capacity, hot_ref, ids_ref, combine_ref, out_ref):
    rows, owners = out_ref.shape
    ids = ids_ref[...]
    combine = combine_ref[...]
    lane = lax.broadcasted_iota(jnp.int32, (rows, owners), 1)
    named = jnp.zeros((rows, owners), jnp.float32)
    weight = jnp.zeros((rows, owners), jnp.float32)
    for k in range(ids.shape[1]):
        here = ids[:, k : k + 1] == lane
        named = named + jnp.where(here, 1.0, 0.0)
        weight = weight + jnp.where(here, combine[:, k : k + 1], 0.0)
    later = lax.broadcasted_iota(jnp.int32, (rows, rows), 0)
    earlier = lax.broadcasted_iota(jnp.int32, (rows, rows), 1)
    before = jnp.where(earlier < later, 1.0, 0.0).astype(jnp.bfloat16)
    rank = jnp.dot(before, named.astype(jnp.bfloat16), preferred_element_type=jnp.float32)
    keep = (lane == hot_ref[0]) | (rank < capacity)
    out_ref[...] = jnp.where(keep, weight, 0.0)


def route(hot_list, expert_ids, combine, owners, capacity):
    rows = expert_ids.shape[0]
    return pl.pallas_call(
        functools.partial(route_kernel, capacity),
        out_shape=jax.ShapeDtypeStruct((rows, owners), jnp.float32),
        in_specs=[
            pl.BlockSpec(memory_space=pltpu.SMEM),
            pl.BlockSpec(memory_space=pltpu.VMEM),
            pl.BlockSpec(memory_space=pltpu.VMEM),
        ],
        out_specs=pl.BlockSpec(memory_space=pltpu.VMEM),
        name="route",
    )(hot_list, expert_ids, combine)


def expert_kernel(sizes, half_steps, where_ref, weight_ref, in_own, out_own, in_sib, out_sib, *refs):
    blocks = len(sizes)
    x_refs, o_refs = refs[:blocks], refs[blocks : 2 * blocks]
    rows, total = refs[2 * blocks :]
    step = pl.program_id(0)
    starts = [sum(sizes[:i]) for i in range(blocks)]

    @pl.when(step == 0)
    def _():
        for start, size, x_ref in zip(starts, sizes, x_refs):
            rows[start : start + size, :] = x_ref[...]

    def add(in_ref, out_ref, first):
        x = rows[...]
        gate = jnp.dot(x, in_ref[0], preferred_element_type=jnp.float32)
        up = jnp.dot(x, in_ref[1], preferred_element_type=jnp.float32)
        hidden = (gate / (1.0 + jnp.exp(-gate)) * up).astype(jnp.bfloat16)
        term = jnp.dot(hidden, out_ref[...], preferred_element_type=jnp.float32)

        @pl.when(step == 0)
        def _():
            total[...] = term

        @pl.when(step != 0)
        def _():
            total[...] += term

    @pl.when(step < half_steps)
    def _():
        add(in_own, out_own, True)

    @pl.when(step >= half_steps)
    def _():
        add(in_sib, out_sib, False)

    @pl.when(step == 2 * half_steps - 1)
    def _():
        lane = lax.broadcasted_iota(jnp.int32, (8, weight_ref.shape[1]), 1)[0:1]
        for i, (start, size, o_ref) in enumerate(zip(starts, sizes, o_refs)):
            at = pl.multiple_of(where_ref[1 + i], 8)
            table = weight_ref[pl.ds(at, size), :]
            weight = jnp.sum(jnp.where(lane == where_ref[0], table, 0.0), axis=1, keepdims=True)
            o_ref[...] = (total[start : start + size, :] * weight).astype(jnp.bfloat16)


def run_expert(blocks, where, weights, own, sib):
    in_own, out_own = own
    in_sib, out_sib = sib
    width, half = in_own.shape[1], in_own.shape[2]
    half_steps = half // TILE_F
    sizes = tuple(b.shape[0] for b in blocks)
    m = sum(sizes)
    last = half_steps - 1
    whole = pl.BlockSpec(memory_space=pltpu.VMEM)
    return pl.pallas_call(
        functools.partial(expert_kernel, sizes, half_steps),
        grid=(2 * half_steps,),
        out_shape=[jax.ShapeDtypeStruct(b.shape, jnp.bfloat16) for b in blocks],
        in_specs=[
            pl.BlockSpec(memory_space=pltpu.SMEM),
            whole,
            pl.BlockSpec((2, width, TILE_F), lambda j: (0, 0, jnp.minimum(j, last))),
            pl.BlockSpec((TILE_F, width), lambda j: (jnp.minimum(j, last), 0)),
            pl.BlockSpec((2, width, TILE_F), lambda j: (0, 0, jnp.maximum(j - half_steps, 0))),
            pl.BlockSpec((TILE_F, width), lambda j: (jnp.maximum(j - half_steps, 0), 0)),
        ]
        + [whole] * len(blocks),
        out_specs=[whole] * len(blocks),
        scratch_shapes=[
            pltpu.VMEM((m, width), jnp.bfloat16),
            pltpu.VMEM((m, width), jnp.float32),
        ],
        compiler_params=pltpu.CompilerParams(vmem_limit_bytes=VMEM_LIMIT),
        cost_estimate=pl.CostEstimate(
            flops=2 * m * width * half * 6, bytes_accessed=6 * width * half * 2, transcendentals=0
        ),
        name="expert",
    )(where, weights, in_own, out_own, in_sib, out_sib, *blocks)


def shards(order, tokens, expert_ids, combine, hot_list, in_weight, in_scale, out_weight, out_scale):
    owners = lax.axis_size("expert")
    halves = lax.axis_size("dp")
    tok_rows, width = tokens.shape
    capacity = tok_rows * expert_ids.shape[1] * 3 // (4 * owners)
    mine = lax.axis_index("expert")
    far = owners // 2
    mid = tok_rows // 2

    def shift(x, by):
        return lax.ppermute(
            x, "expert", [(order[i], order[(i + by) % owners]) for i in range(owners)]
        )

    def add(a, b):
        return (a.astype(jnp.float32) + b.astype(jnp.float32)).astype(jnp.bfloat16)

    place = [order.index(i) for i in range(owners)]
    at = jnp.array(place, jnp.int32)[mine]
    around = jnp.array(order, jnp.int32)

    def source(by):
        return around[(at + by) % owners] * tok_rows

    own = (dequantize(in_weight[0], in_scale[0]), dequantize(out_weight[0], out_scale[0]))
    swap = [(i, (i + 1) % halves) for i in range(halves)]
    sib = tuple(lax.ppermute(w, "dp", swap) for w in own)

    weights = lax.all_gather(
        route(hot_list, expert_ids, combine, owners, capacity), "expert", axis=0, tiled=True
    )

    done = {}

    def expert(keys, blocks, offsets):
        where = jnp.stack([mine.astype(jnp.int32)] + [o.astype(jnp.int32) for o in offsets])
        for key, out in zip(keys, run_expert(blocks, where, weights, own, sib)):
            done[key] = out

    ahead = behind = tokens
    waiting = [("0", tokens, source(0))]
    for s in range(1, far):
        behind = shift(behind, 1)
        ahead = shift(ahead, -1)
        waiting += [(-s, behind, source(-s)), (s, ahead, source(s))]
        expert(*zip(*waiting))
        waiting = []
    top = shift(behind[:mid], 1)
    bottom = shift(ahead[mid:], -1)
    expert(("top", "bottom"), (top, bottom), (source(far), source(far) + mid))

    to_right = shift(done["top"], 1)
    to_left = shift(done["bottom"], -1)
    empty = jnp.zeros((mid, width), jnp.bfloat16)
    to_right = jnp.concatenate([to_right, empty], axis=0)
    to_left = jnp.concatenate([empty, to_left], axis=0)
    for s in range(far - 1, 0, -1):
        to_right = shift(add(done[s], to_right), 1)
        to_left = shift(add(done[-s], to_left), -1)
    own_rows = done["0"].astype(jnp.float32)
    return (own_rows + to_right.astype(jnp.float32) + to_left.astype(jnp.float32)).astype(
        jnp.bfloat16
    )


def solution(mesh):
    placed = (
        P(("group", "expert", "dp"), None),
        P(("group", "expert", "dp"), None),
        P(("group", "expert", "dp"), None),
        P("group"),
        P("expert", None, None, "dp"),
        P("expert", None, None, "dp"),
        P("expert", "dp", None),
        P("expert", "dp", None),
    )
    return jax.shard_map(
        functools.partial(shards, ring_order(mesh)),
        mesh=mesh,
        in_specs=placed,
        out_specs=P(("group", "expert", "dp"), None),
        check_vma=False,
    )
```

time: 843 us -> 293 us (0.35)
  the two profiles are of different devices: /device:TPU:13 before, /device:TPU:0 now
where the time goes in v1:
time: 293 us; the launch traced here: 292 us
  waiting for transfers between devices  93.8 us (32%)
  Pallas kernels  65.6 us (22%)
  local copies, waits for them, and re-layouts  43.2 us (15%)
  blocking collectives  37.7 us (13%)
  other arithmetic  22.5 us (8%)
  starting transfers between devices  16.7 us (6%)
  between operations  12.5 us (4%)
    ppermute x16, waiting for transfers between devices, shift(): lax.ppermute(x, 'expert', [(order[i], order[(i + by) % owners]) for i in...  93.8 us
    pallas_call x4, Pallas kernels, run_expert(): pl.pallas_call(functools.partial(expert_kernel, sizes, half_steps), grid=...  63.8 us
    all_gather x1, blocking collectives, shards(): lax.all_gather(route(hot_list, expert_ids, combine, owners, capacity), 'e...  37.7 us
    mul x6, local copies, waits for them, and re-layouts, dequantize(): tiled * raw_scale[..., :, None, :, None]  34.9 us
    convert_element_type x2, other arithmetic, dequantize(): (tiled * raw_scale[..., :, None, :, None]).reshape(shape)  17.8 us
    ppermute x16, starting transfers between devices, shift(): lax.ppermute(x, 'expert', [(order[i], order[(i + by) % owners]) for i in...  16.2 us
    unnamed x45, local copies, waits for them, and re-layouts  6.96 us
  transfers between devices with their start and end apart: 18, of which 9 were waited for; matrix products, arithmetic and copies ran while one was open for 9% of the time, Pallas kernels for 18%

profile of v1, /device:TPU:0, one launch (start us, length us, event | category | flops | bytes accessed | tf_op | source)
XLA Modules:
  0.0 292.0 jit_solution(8119022445064217849)
XLA Ops:
  0.8 7.1 %mul.63 = f32[2,28,128,4,128]{4,3,2,1,0:T(4,128)} broadcast(f32[2,28,4]{2,1,0:T(8,128)S(1)} %copy.16), dimensions={0,1,3} | broadcast | bytes 14680960 | tf_op jit(solution)/shard_map/mul | solution.py:28
  7.9 17.5 %mul.64 = f32[2,3584,512]{2,1,0:T(8,128)} reshape(f32[2,28,128,4,128]{4,3,2,1,0:T(4,128)} %mul.63) | data formatting | bytes 29360128 | tf_op jit(solution)/shard_map/mul | solution.py:28
  25.4 10.7 %fusion.in_own = bf16[2,3584,512]{2,1,0:T(8,128)(2,1)} fusion(f32[2,3584,512]{2,1,0:T(8,128)} %mul.64, bf16[1,2,3584,512]{3,2,1,0:T(8,128)(2,1)} %param.14), kind=kLoop, calls=%fused_computation.1 | loop fusion | flops 11010048 | bytes 29360128 | tf_op jit(solution)/shard_map/convert_element_type | solution.py:28
  37.6 3.8 %copy.21 = f32[448,8,4,128]{3,1,2,0:T(8,128)} copy(f32[448,8,4,128]{3,2,1,0:T(4,128)S(1)} %bitcast.17) | data formatting | bytes 14680064
  41.5 8.4 %copy.18 = f32[512,3584]{1,0:T(8,128)} copy(f32[512,3584]{0,1:T(8,128)} %bitcast.18) | data formatting | bytes 14680064 | tf_op jit(solution)/shard_map/mul | solution.py:28
  49.9 7.1 %fusion.1.out_own = bf16[512,3584]{1,0:T(8,128)(2,1)} fusion(f32[512,3584]{1,0:T(8,128)} %copy.18, bf16[1,512,3584]{2,1,0:T(8,128)(2,1)} %param.16), kind=kLoop, calls=%fused_computation.4 | loop fusion | flops 5505024 | bytes 14680064 | tf_op jit(solution)/shard_map/convert_element_type | solution.py:28
  57.0 3.0 %collective-permute-start.2 = (bf16[128,3584]{1,0:T(8,128)(2,1)S(1)}, bf16[128,3584]{1,0:T(8,128)(2,1)S(1)}, u32[]{:S(2)}, u32[]{:S(2)}) collective-permute-start(bf16[128,3584]{1,0:T(8,128)(2,1)S(1)} %copy-done.17), channel_id=1, source_target_pairs={{0,4},{4,8},{8,12},{12,14},{14,10},{10,6},{6,2},{2,0},{1,5},{5,9},... | collective-permute-start | bytes 2752520 | tf_op jit(solution)/shard_map/ppermute | solution.py:155
  60.1 20.5 %collective-permute-done.2.refs_1_ = bf16[128,3584]{1,0:T(8,128)(2,1)S(1)} collective-permute-done((bf16[128,3584]{1,0:T(8,128)(2,1)S(1)}, bf16[128,3584]{1,0:T(8,128)(2,1)S(1)}, u32[]{:S(2)}, u32[]{:S(2)}) %collective-permute-start.2) | collective-permute-done | bytes 917536 | tf_op jit(solution)/shard_map/ppermute | solution.py:155
  80.5 1.8 collective-permute-start.4
  82.6 19.7 %collective-permute-done.4.refs_0_ = bf16[128,3584]{1,0:T(8,128)(2,1)S(1)} collective-permute-done((bf16[128,3584]{1,0:T(8,128)(2,1)S(1)}, bf16[128,3584]{1,0:T(8,128)(2,1)S(1)}, u32[]{:S(2)}, u32[]{:S(2)}) %collective-permute-start.4) | collective-permute-done | bytes 917536 | tf_op jit(solution)/shard_map/ppermute | solution.py:155
  102.3 1.5 collective-permute-start.6
  119.5 1.8 route.1
  121.3 1.9 collective-permute-done.6.refs_0_
  125.4 37.7 %all_gather.3.weight_ref = f32[1024,8]{1,0:T(8,128)} all-gather(f32[128,8]{1,0:T(8,128)S(1)} %copy-done.12), channel_id=1, replica_groups=mesh['group'=2,'expert'=8,'dp'=2] {'expert'}, dimensions={0}, use_global_device_ids=true | all-gather | bytes 36864 | tf_op jit(solution)/shard_map/all_gather | solution.py:173
  166.4 12.6 %expert.7 = (bf16[64,3584]{1,0:T(8,128)(2,1)}, bf16[64,3584]{1,0:T(8,128)(2,1)}) custom-call(s32[3]{0:T(128)} %pad_add_fusion.3.where_ref, f32[1024,8]{1,0:T(8,128)} %all_gather.3.weight_ref, bf16[2,3584,512]{2,1,0:T(8,128)(2,1)} %fusion.in_own, bf16[512,3584]{1,0:T(8,128)(2,1)} %fusion.1.out_own, bf16[2,3584,512]{2,1,0:T(8,128)(2,1)} %collective-permute-done.in_sib, ...), custom_call_target="tpu_custom_call" | custom-call | flops 2818572288 | bytes 22020096 | tf_op jit(solution)/shard_map/expert/pallas_call | solution.py:119
  179.1 2.0 collective-permute-start.10
  181.1 15.7 %expert.6 = (bf16[128,3584]{1,0:T(8,128)(2,1)}, bf16[128,3584]{1,0:T(8,128)(2,1)}) custom-call(s32[3]{0:T(128)} %pad_add_fusion.2.where_ref, f32[1024,8]{1,0:T(8,128)} %all_gather.3.weight_ref, bf16[2,3584,512]{2,1,0:T(8,128)(2,1)} %fusion.in_own, bf16[512,3584]{1,0:T(8,128)(2,1)} %fusion.1.out_own, bf16[2,3584,512]{2,1,0:T(8,128)(2,1)} %collective-permute-done.in_sib, ...), custom_call_target="tpu_custom_call" | custom-call | flops 5637144576 | bytes 22020096 | tf_op jit(solution)/shard_map/expert/pallas_call | solution.py:119
  196.8 19.6 %expert.4 = (bf16[128,3584]{1,0:T(8,128)(2,1)}, bf16[128,3584]{1,0:T(8,128)(2,1)}, bf16[128,3584]{1,0:T(8,128)(2,1)}) custom-call(s32[4]{0:T(128)} %pad_add_fusion.where_ref, f32[1024,8]{1,0:T(8,128)} %all_gather.3.weight_ref, bf16[2,3584,512]{2,1,0:T(8,128)(2,1)} %fusion.in_own, bf16[512,3584]{1,0:T(8,128)(2,1)} %fusion.1.out_own, ...), custom_call_target="tpu_custom_call" | custom-call | flops 8455716864 | bytes 22020096 | tf_op jit(solution)/shard_map/expert/pallas_call | solution.py:119
  216.4 15.9 %expert.5 = (bf16[128,3584]{1,0:T(8,128)(2,1)}, bf16[128,3584]{1,0:T(8,128)(2,1)}) custom-call(s32[3]{0:T(128)} %pad_add_fusion.1.where_ref, f32[1024,8]{1,0:T(8,128)} %all_gather.3.weight_ref, bf16[2,3584,512]{2,1,0:T(8,128)(2,1)} %fusion.in_own, bf16[512,3584]{1,0:T(8,128)(2,1)} %fusion.1.out_own, bf16[2,3584,512]{2,1,0:T(8,128)(2,1)} %collective-permute-done.in_sib, ...), custom_call_target="tpu_custom_call" | custom-call | flops 5637144576 | bytes 22020096 | tf_op jit(solution)/shard_map/expert/pallas_call | solution.py:119
  234.7 19.1 %collective-permute-done.15 = bf16[128,3584]{1,0:T(8,128)(2,1)S(1)} collective-permute-done((bf16[128,3584]{1,0:T(8,128)(2,1)S(1)}, bf16[128,3584]{1,0:T(8,128)(2,1)S(1)}, u32[]{:S(2)}, u32[]{:S(2)}) %collective-permute-start.15) | collective-permute-done | bytes 917536 | tf_op jit(solution)/shard_map/ppermute | solution.py:155
  254.9 1.5 collective-permute-start.12
  256.4 20.2 %collective-permute-done.16 = bf16[128,3584]{1,0:T(8,128)(2,1)S(1)} collective-permute-done((bf16[128,3584]{1,0:T(8,128)(2,1)S(1)}, bf16[128,3584]{1,0:T(8,128)(2,1)S(1)}, u32[]{:S(2)}, u32[]{:S(2)}) %collective-permute-start.16) | collective-permute-done | bytes 917536 | tf_op jit(solution)/shard_map/ppermute | solution.py:155
  277.3 1.8 collective-permute-start.13
  279.1 11.1 %collective-permute-done.17 = bf16[128,3584]{1,0:T(8,128)(2,1)S(1)} collective-permute-done((bf16[128,3584]{1,0:T(8,128)(2,1)S(1)}, bf16[128,3584]{1,0:T(8,128)(2,1)S(1)}, u32[]{:S(2)}, u32[]{:S(2)}) %collective-permute-start.17) | collective-permute-done | bytes 917536 | tf_op jit(solution)/shard_map/ppermute | solution.py:155
  (86 shorter events, 17.5 us)
Async XLA Ops:
  36.1 129.4 %collective-permute-start = (bf16[2,3584,512]{2,1,0:T(8,128)(2,1)}, bf16[2,3584,512]{2,1,0:T(8,128)(2,1)}, u32[]{:S(2)}, u32[]{:S(2)}) collective-permute-start(bf16[2,3584,512]{2,1,0:T(8,128)(2,1)} %fusion.in_own), channel_id=1, source_target_pairs={{0,1},{1,0},{2,3},{3,2},{4,5},{5,4},{6,7},{7,6},{8,9},{9,8},{10,11... | collective-permute-start | bytes 22020104 | tf_op jit(solution)/shard_map/ppermute | solution.py:171
  49.8 61.7 %copy-start.13 = (s32[8]{0:T(128)S(1)}, s32[8]{0:T(128)}, u32[]{:S(2)}) copy-start(s32[8]{0:T(128)} %constant.84.clone) | copy-start | bytes 100
  49.9 64.4 %copy-start.15 = (s32[128,4]{0,1:T(4,128)S(1)}, s32[128,4]{0,1:T(4,128)}, u32[]{:S(2)}) copy-start(s32[128,4]{0,1:T(4,128)} %param.11) | copy-start | bytes 6148
  49.9 65.1 %copy-start.16 = (f32[128,4]{0,1:T(4,128)S(1)}, f32[128,4]{0,1:T(4,128)}, u32[]{:S(2)}) copy-start(f32[128,4]{0,1:T(4,128)} %param.12) | copy-start | bytes 6148
  57.0 108.5 %collective-permute-start.1 = (bf16[512,3584]{1,0:T(8,128)(2,1)}, bf16[512,3584]{1,0:T(8,128)(2,1)}, u32[]{:S(2)}, u32[]{:S(2)}) collective-permute-start(bf16[512,3584]{1,0:T(8,128)(2,1)} %fusion.1.out_own), channel_id=1, source_target_pairs={{0,1},{1,0},{2,3},{3,2},{4,5},{5,4},{6,7},{7,6},{8,9},{9,8},{10,11... | collective-permute-start | bytes 11010056 | tf_op jit(solution)/shard_map/ppermute | solution.py:171
  57.0 23.5 %collective-permute-start.2 = (bf16[128,3584]{1,0:T(8,128)(2,1)S(1)}, bf16[128,3584]{1,0:T(8,128)(2,1)S(1)}, u32[]{:S(2)}, u32[]{:S(2)}) collective-permute-start(bf16[128,3584]{1,0:T(8,128)(2,1)S(1)} %copy-done.17), channel_id=1, source_target_pairs={{0,4},{4,8},{8,12},{12,14},{14,10},{10,6},{6,2},{2,0},{1,5},{5,9},... | collective-permute-start | bytes 2752520 | tf_op jit(solution)/shard_map/ppermute | solution.py:155
  60.1 22.3 %collective-permute-start.3 = (bf16[128,3584]{1,0:T(8,128)(2,1)S(1)}, bf16[128,3584]{1,0:T(8,128)(2,1)S(1)}, u32[]{:S(2)}, u32[]{:S(2)}) collective-permute-start(bf16[128,3584]{1,0:T(8,128)(2,1)S(1)} %copy-done.17), channel_id=1, source_target_pairs={{0,2},{4,0},{8,4},{12,8},{14,12},{10,14},{6,10},{2,6},{1,3},{5,1},... | collective-permute-start | bytes 2752520 | tf_op jit(solution)/shard_map/ppermute | solution.py:155
  80.5 21.7 %collective-permute-start.4 = (bf16[128,3584]{1,0:T(8,128)(2,1)S(1)}, bf16[128,3584]{1,0:T(8,128)(2,1)S(1)}, u32[]{:S(2)}, u32[]{:S(2)}) collective-permute-start(bf16[128,3584]{1,0:T(8,128)(2,1)S(1)} %collective-permute-done.2.refs_1_), channel_id=1, source_target_pairs={{0,4},{4,8},{8,12},{12,14},{14,10},{10,6},{6,2},{2,0},{1,5},{5,9},... | collective-permute-start | bytes 2752520 | tf_op jit(solution)/shard_map/ppermute | solution.py:155
  82.3 21.4 %collective-permute-start.5 = (bf16[128,3584]{1,0:T(8,128)(2,1)S(1)}, bf16[128,3584]{1,0:T(8,128)(2,1)}, u32[]{:S(2)}, u32[]{:S(2)}) collective-permute-start(bf16[128,3584]{1,0:T(8,128)(2,1)S(1)} %collective-permute-done.3.refs_2_), channel_id=1, source_target_pairs={{0,2},{4,0},{8,4},{12,8},{14,12},{10,14},{6,10},{2,6},{1,3},{5,1},... | collective-permute-start | bytes 2752520 | tf_op jit(solution)/shard_map/ppermute | solution.py:155
  102.3 76.7 %copy-start.9 = (bf16[128,3584]{1,0:T(8,128)(2,1)}, bf16[128,3584]{1,0:T(8,128)(2,1)S(1)}, u32[]{:S(2)}) copy-start(bf16[128,3584]{1,0:T(8,128)(2,1)S(1)} %collective-permute-done.4.refs_0_) | copy-start | bytes 2752516
  102.3 20.9 %collective-permute-start.6 = (bf16[128,3584]{1,0:T(8,128)(2,1)S(1)}, bf16[128,3584]{1,0:T(8,128)(2,1)S(1)}, u32[]{:S(2)}, u32[]{:S(2)}) collective-permute-start(bf16[128,3584]{1,0:T(8,128)(2,1)S(1)} %collective-permute-done.4.refs_0_), channel_id=1, source_target_pairs={{0,4},{4,8},{8,12},{12,14},{14,10},{10,6},{6,2},{2,0},{1,5},{5,9},... | collective-permute-start | bytes 2752520 | tf_op jit(solution)/shard_map/ppermute | solution.py:155
  103.8 20.7 %collective-permute-start.7 = (bf16[128,3584]{1,0:T(8,128)(2,1)}, bf16[128,3584]{1,0:T(8,128)(2,1)S(1)}, u32[]{:S(2)}, u32[]{:S(2)}) collective-permute-start(bf16[128,3584]{1,0:T(8,128)(2,1)} %collective-permute-done.5.refs_1_), channel_id=1, source_target_pairs={{0,2},{4,0},{8,4},{12,8},{14,12},{10,14},{6,10},{2,6},{1,3},{5,1},... | collective-permute-start | bytes 2752520 | tf_op jit(solution)/shard_map/ppermute | solution.py:155
  123.2 55.8 %copy-start = (bf16[128,3584]{1,0:T(8,128)(2,1)}, bf16[128,3584]{1,0:T(8,128)(2,1)S(1)}, u32[]{:S(2)}) copy-start(bf16[128,3584]{1,0:T(8,128)(2,1)S(1)} %collective-permute-done.6.refs_0_) | copy-start | bytes 2752516
  123.2 42.2 %collective-permute-start.8 = (bf16[64,3584]{1,0:T(8,128)(2,1)S(1)}, bf16[64,3584]{1,0:T(8,128)(2,1)S(1)}, u32[]{:S(2)}, u32[]{:S(2)}) collective-permute-start(bf16[64,3584]{1,0:T(8,128)(2,1)S(1)} %slice.8), channel_id=1, source_target_pairs={{0,4},{4,8},{8,12},{12,14},{14,10},{10,6},{6,2},{2,0},{1,5},{5,9},... | collective-permute-start | bytes 1376264 | tf_op jit(solution)/shard_map/ppermute | solution.py:155
  124.4 54.6 %copy-start.1 = (bf16[128,3584]{1,0:T(8,128)(2,1)}, bf16[128,3584]{1,0:T(8,128)(2,1)S(1)}, u32[]{:S(2)}) copy-start(bf16[128,3584]{1,0:T(8,128)(2,1)S(1)} %collective-permute-done.7.refs_1_) | copy-start | bytes 2752516
  124.5 41.0 %collective-permute-start.9 = (bf16[64,3584]{1,0:T(8,128)(2,1)S(1)}, bf16[64,3584]{1,0:T(8,128)(2,1)S(1)}, u32[]{:S(2)}, u32[]{:S(2)}) collective-permute-start(bf16[64,3584]{1,0:T(8,128)(2,1)S(1)} %slice.9), channel_id=1, source_target_pairs={{0,2},{4,0},{8,4},{12,8},{14,12},{10,14},{6,10},{2,6},{1,3},{5,1},... | collective-permute-start | bytes 1376264 | tf_op jit(solution)/shard_map/ppermute | solution.py:155
  179.0 53.3 %collective-permute-start.14 = (bf16[64,3584]{1,0:T(8,128)(2,1)}, bf16[64,3584]{1,0:T(8,128)(2,1)S(1)}, u32[]{:S(2)}, u32[]{:S(2)}) collective-permute-start(bf16[64,3584]{1,0:T(8,128)(2,1)} %get-tuple-element.22), channel_id=1, source_target_pairs={{0,2},{4,0},{8,4},{12,8},{14,12},{10,14},{6,10},{2,6},{1,3},{5,1},... | collective-permute-start | bytes 1376264 | tf_op jit(solution)/shard_map/ppermute | solution.py:155
  179.1 53.7 %collective-permute-start.10 = (bf16[64,3584]{1,0:T(8,128)(2,1)}, bf16[64,3584]{1,0:T(8,128)(2,1)S(1)}, u32[]{:S(2)}, u32[]{:S(2)}) collective-permute-start(bf16[64,3584]{1,0:T(8,128)(2,1)} %get-tuple-element.18), channel_id=1, source_target_pairs={{0,4},{4,8},{8,12},{12,14},{14,10},{10,6},{6,2},{2,0},{1,5},{5,9},... | collective-permute-start | bytes 1376264 | tf_op jit(solution)/shard_map/ppermute | solution.py:155
  232.5 21.4 %collective-permute-start.15 = (bf16[128,3584]{1,0:T(8,128)(2,1)S(1)}, bf16[128,3584]{1,0:T(8,128)(2,1)S(1)}, u32[]{:S(2)}, u32[]{:S(2)}) collective-permute-start(bf16[128,3584]{1,0:T(8,128)(2,1)S(1)} %add_convert_fusion.3), channel_id=1, source_target_pairs={{0,2},{4,0},{8,4},{12,8},{14,12},{10,14},{6,10},{2,6},{1,3},{5,1},... | collective-permute-start | bytes 2752520 | tf_op jit(solution)/shard_map/ppermute | solution.py:155
  233.6 21.1 %collective-permute-start.11 = (bf16[128,3584]{1,0:T(8,128)(2,1)S(1)}, bf16[128,3584]{1,0:T(8,128)(2,1)S(1)}, u32[]{:S(2)}, u32[]{:S(2)}) collective-permute-start(bf16[128,3584]{1,0:T(8,128)(2,1)S(1)} %add_convert_fusion.6), channel_id=1, source_target_pairs={{0,4},{4,8},{8,12},{12,14},{14,10},{10,6},{6,2},{2,0},{1,5},{5,9},... | collective-permute-start | bytes 2752520 | tf_op jit(solution)/shard_map/ppermute | solution.py:155
  254.0 22.5 %collective-permute-start.16 = (bf16[128,3584]{1,0:T(8,128)(2,1)S(1)}, bf16[128,3584]{1,0:T(8,128)(2,1)S(1)}, u32[]{:S(2)}, u32[]{:S(2)}) collective-permute-start(bf16[128,3584]{1,0:T(8,128)(2,1)S(1)} %add_convert_fusion.2), channel_id=1, source_target_pairs={{0,2},{4,0},{8,4},{12,8},{14,12},{10,14},{6,10},{2,6},{1,3},{5,1},... | collective-permute-start | bytes 2752520 | tf_op jit(solution)/shard_map/ppermute | solution.py:155
  254.9 22.2 %collective-permute-start.12 = (bf16[128,3584]{1,0:T(8,128)(2,1)S(1)}, bf16[128,3584]{1,0:T(8,128)(2,1)S(1)}, u32[]{:S(2)}, u32[]{:S(2)}) collective-permute-start(bf16[128,3584]{1,0:T(8,128)(2,1)S(1)} %add_convert_fusion.5), channel_id=1, source_target_pairs={{0,4},{4,8},{8,12},{12,14},{14,10},{10,6},{6,2},{2,0},{1,5},{5,9},... | collective-permute-start | bytes 2752520 | tf_op jit(solution)/shard_map/ppermute | solution.py:155
  276.8 13.4 %collective-permute-start.17 = (bf16[128,3584]{1,0:T(8,128)(2,1)S(1)}, bf16[128,3584]{1,0:T(8,128)(2,1)S(1)}, u32[]{:S(2)}, u32[]{:S(2)}) collective-permute-start(bf16[128,3584]{1,0:T(8,128)(2,1)S(1)} %add_convert_fusion.1), channel_id=1, source_target_pairs={{0,2},{4,0},{8,4},{12,8},{14,12},{10,14},{6,10},{2,6},{1,3},{5,1},... | collective-permute-start | bytes 2752520 | tf_op jit(solution)/shard_map/ppermute | solution.py:155
  277.3 13.4 %collective-permute-start.13 = (bf16[128,3584]{1,0:T(8,128)(2,1)S(1)}, bf16[128,3584]{1,0:T(8,128)(2,1)S(1)}, u32[]{:S(2)}, u32[]{:S(2)}) collective-permute-start(bf16[128,3584]{1,0:T(8,128)(2,1)S(1)} %add_convert_fusion.4), channel_id=1, source_target_pairs={{0,4},{4,8},{8,12},{12,14},{14,10},{10,6},{6,2},{2,0},{1,5},{5,9},... | collective-permute-start | bytes 2752520 | tf_op jit(solution)/shard_map/ppermute | solution.py:155
  (15 other events, 241.8 us)

commit v2 on v0

v2 whole, which is shorter than its diff:
```python
import functools

import jax
import jax.numpy as jnp
from jax import lax
from jax.experimental import pallas as pl
from jax.experimental.pallas import tpu as pltpu
from jax.sharding import PartitionSpec as P

QB = 128
TILE_F = 256
LANES = 128
VMEM_LIMIT = 56 * 1024 * 1024
CHUNKS = 1
SCALE = 1.0


def cost(flops, bytes_accessed):
    return pl.CostEstimate(
        flops=int(flops * SCALE), bytes_accessed=int(bytes_accessed * SCALE), transcendentals=0
    )


def ring_order(mesh):
    count = mesh.shape["expert"]
    rows = 2 if count == 8 else 1
    first = [i * rows for i in range(count // rows)]
    second = [i * rows + 1 for i in reversed(range(count // rows))] if rows == 2 else []
    return first + second


def dequantize_kernel(in_scale, out_scale, in_raw, out_raw, out_ref):
    f, part = pl.program_id(0), pl.program_id(1)
    chunk = in_raw.shape[1]

    def scaled(block, scale):
        return (block.astype(jnp.float32) * scale).astype(jnp.bfloat16)

    @pl.when(part < 2)
    def _():
        for side in range(2):
            for i in range(chunk // QB):
                for j in range(TILE_F // QB):
                    scale = in_scale[side, part * (chunk // QB) + i, f * (TILE_F // QB) + j]
                    at = side * TILE_F + j * QB
                    out_ref[0, i * QB : (i + 1) * QB, at : at + QB] = scaled(
                        in_raw[side, i * QB : (i + 1) * QB, j * QB : (j + 1) * QB], scale
                    )

    @pl.when(part == 2)
    def _():
        per = 2 * TILE_F // QB
        for i in range(TILE_F // QB):
            for j in range(out_raw.shape[1] // QB):
                scale = out_scale[f * (TILE_F // QB) + i, j]
                row, at = (j // per) * TILE_F + i * QB, (j % per) * QB
                out_ref[0, row : row + QB, at : at + QB] = scaled(
                    out_raw[i * QB : (i + 1) * QB, j * QB : (j + 1) * QB], scale
                )


def dequantize(in_raw, in_scale, out_raw, out_scale):
    width, half = in_raw.shape[1], in_raw.shape[2]
    tiles = half // TILE_F
    chunk = width // 2
    return pl.pallas_call(
        dequantize_kernel,
        grid=(tiles, 3),
        out_shape=jax.ShapeDtypeStruct((tiles, 3 * chunk, 2 * TILE_F), jnp.bfloat16),
        in_specs=[
            pl.BlockSpec(memory_space=pltpu.SMEM),
            pl.BlockSpec(memory_space=pltpu.SMEM),
            pl.BlockSpec((2, chunk, TILE_F), lambda f, p: (0, jnp.minimum(p, 1), f)),
            pl.BlockSpec((TILE_F, width), lambda f, p: (f, 0)),
        ],
        out_specs=pl.BlockSpec((1, chunk, 2 * TILE_F), lambda f, p: (f, p, 0)),
        compiler_params=pltpu.CompilerParams(vmem_limit_bytes=VMEM_LIMIT),
        cost_estimate=cost(6 * width * half, 12 * width * half),
        name="dequantize",
    )(in_scale, out_scale, in_raw, out_raw)


def route_kernel(capacity, owners, hot_ref, ids_ref, combine_ref, tokens_ref, *out_refs):
    picks, rows = ids_ref.shape
    expert = lax.broadcasted_iota(jnp.int32, (owners, rows), 0)
    named = jnp.zeros((owners, rows), jnp.float32)
    weight = jnp.zeros((owners, rows), jnp.float32)
    for k in range(picks):
        here = ids_ref[k : k + 1, :] == expert
        named = named + jnp.where(here, 1.0, 0.0)
        weight = weight + jnp.where(here, combine_ref[k : k + 1, :], 0.0)
    earlier = lax.broadcasted_iota(jnp.int32, (rows, rows), 0)
    later = lax.broadcasted_iota(jnp.int32, (rows, rows), 1)
    before = jnp.where(earlier < later, 1.0, 0.0).astype(jnp.bfloat16)
    rank = jnp.dot(named.astype(jnp.bfloat16), before, preferred_element_type=jnp.float32)
    weight = jnp.where((expert == hot_ref[0]) | (rank < capacity), weight, 0.0)
    pieces = []
    for _ in range(3):
        piece = weight.astype(jnp.bfloat16).astype(jnp.float32)
        weight = weight - piece
        pieces.append(piece)
    pieces.append(jnp.zeros((LANES - 3 * owners, rows), jnp.float32))
    extra = jnp.concatenate(pieces, axis=0).T.astype(jnp.bfloat16)
    width = tokens_ref.shape[1]
    size = rows // len(out_refs)
    for c, out_ref in enumerate(out_refs):
        out_ref[:, :width] = tokens_ref[c * size : (c + 1) * size, :]
        out_ref[:, width:] = extra[c * size : (c + 1) * size, :]


def route(hot_list, expert_ids, combine, tokens, owners, capacity):
    rows, width = tokens.shape
    vmem = pl.BlockSpec(memory_space=pltpu.VMEM)
    return pl.pallas_call(
        functools.partial(route_kernel, capacity, owners),
        out_shape=[jax.ShapeDtypeStruct((rows // CHUNKS, width + LANES), jnp.bfloat16)] * CHUNKS,
        in_specs=[pl.BlockSpec(memory_space=pltpu.SMEM), vmem, vmem, vmem],
        out_specs=[vmem] * CHUNKS,
        name="route",
    )(hot_list, expert_ids.T, combine.T, tokens)


def expert_kernel(sizes, owners, who_ref, own, sib, *refs):
    blocks = len(sizes)
    x_refs, o_refs = refs[:blocks], refs[blocks : 2 * blocks]
    rows, total, held, arrived = refs[2 * blocks :]
    starts = [sum(sizes[:i]) for i in range(blocks)]
    half_tiles, width = own.shape[0], rows.shape[1]
    tiles = 2 * half_tiles
    cut = width // 2

    def copies(ref, at, tile):
        return [
            pltpu.make_async_copy(
                ref.at[at, pl.ds(part * cut, cut)],
                held.at[tile, pl.ds(part * cut, cut)],
                arrived.at[tile, part],
            )
            for part in range(3)
        ]

    landed = []
    for tile in range(tiles):
        half = own if tile < half_tiles else sib
        landed.append(copies(half, tile % half_tiles, tile))
        for copy in landed[-1]:
            copy.start()
    for start, size, x_ref in zip(starts, sizes, x_refs):
        rows[start : start + size, :] = x_ref[:, :width]

    for tile in range(tiles):
        landed[tile][0].wait()
        both = jnp.dot(rows[:, :cut], held[tile, :cut], preferred_element_type=jnp.float32)
        landed[tile][1].wait()
        both += jnp.dot(
            rows[:, cut:], held[tile, cut : 2 * cut], preferred_element_type=jnp.float32
        )
        gate, up = both[:, :TILE_F], both[:, TILE_F:]
        hidden = (gate / (1.0 + jnp.exp(-gate)) * up).astype(jnp.bfloat16)
        landed[tile][2].wait()
        for i in range(width // (2 * TILE_F)):
            at = slice(i * 2 * TILE_F, (i + 1) * 2 * TILE_F)
            term = jnp.dot(
                hidden,
                held[tile, width + i * TILE_F : width + (i + 1) * TILE_F],
                preferred_element_type=jnp.float32,
            )
            total[:, at] = term if tile == 0 else total[:, at] + term
    for start, size, x_ref, o_ref in zip(starts, sizes, x_refs, o_refs):
        lane = lax.broadcasted_iota(jnp.int32, (size, LANES), 1)
        picked = (lax.rem(lane, owners) == who_ref[0]) & (lane < 3 * owners)
        weight = jnp.where(picked, x_ref[:, width:].astype(jnp.float32), 0.0)
        weight = jnp.sum(weight, axis=1, keepdims=True)
        o_ref[...] = (total[start : start + size, :] * weight).astype(jnp.bfloat16)


def run_expert(blocks, owners, who, own, sib):
    tiles, width = own.shape[0], blocks[0].shape[1] - LANES
    sizes = tuple(x.shape[0] for x in blocks)
    m = sum(sizes)
    whole = pl.BlockSpec(memory_space=pltpu.VMEM)
    return pl.pallas_call(
        functools.partial(expert_kernel, sizes, owners),
        out_shape=[jax.ShapeDtypeStruct((size, width), jnp.bfloat16) for size in sizes],
        in_specs=[pl.BlockSpec(memory_space=pltpu.SMEM)]
        + [pl.BlockSpec(memory_space=pl.ANY)] * 2
        + [whole] * len(blocks),
        out_specs=[whole] * len(blocks),
        scratch_shapes=[
            pltpu.VMEM((m, width), jnp.bfloat16),
            pltpu.VMEM((m, width), jnp.float32),
            pltpu.VMEM((2 * tiles,) + own.shape[1:], jnp.bfloat16),
            pltpu.SemaphoreType.DMA((2 * tiles, 3)),
        ],
        compiler_params=pltpu.CompilerParams(vmem_limit_bytes=VMEM_LIMIT),
        cost_estimate=cost(12 * m * width * tiles * TILE_F, 12 * width * tiles * TILE_F),
        name="expert",
    )(who, own, sib, *blocks)


def after(value, *others):
    return lax.optimization_barrier((value, others))[0]


def shards(order, tokens, expert_ids, combine, hot_list, in_weight, in_scale, out_weight, out_scale):
    owners = lax.axis_size("expert")
    halves = lax.axis_size("dp")
    tok_rows, width = tokens.shape
    capacity = tok_rows * expert_ids.shape[1] * 3 // (4 * owners)
    who = lax.axis_index("expert").astype(jnp.int32).reshape(1)
    far = owners // 2
    size = tok_rows // CHUNKS
    mid = size // 2
    chunks = range(CHUNKS)

    def shift(x, by):
        return lax.ppermute(
            x, "expert", [(order[i], order[(i + by) % owners]) for i in range(owners)]
        )

    def add(a, b):
        return (a.astype(jnp.float32) + b.astype(jnp.float32)).astype(jnp.bfloat16)

    have = [{0: x} for x in route(hot_list, expert_ids, combine, tokens, owners, capacity)]
    done = [{} for _ in chunks]

    def gather(c, s):
        if s < far:
            have[c][-s] = shift(have[c][1 - s], 1)
            have[c][s] = shift(have[c][s - 1], -1)
        else:
            have[c]["top"] = shift(have[c][1 - s][:mid], 1)
            have[c]["bottom"] = shift(have[c][s - 1][mid:], -1)

    def expert(*keys):
        blocks = [have[c][key] for c, key in keys]
        for (c, key), out in zip(keys, run_expert(blocks, owners, who, own, sib)):
            done[c][key] = out

    def hold(keys, *others):
        for c, key in keys:
            have[c][key] = after(have[c][key], *others)

    def every(*steps):
        return [(c, key) for s in steps for c in chunks for key in ((s, -s) if s else (0,))]

    for c in chunks:
        gather(c, 1)
    own = dequantize(
        *after((in_weight[0], in_scale[0], out_weight[0], out_scale[0]), have[0][0])
    )
    halved = after(own, [have[c][key] for c, key in every(1)])
    sib = lax.ppermute(halved, "dp", [(i, (i + 1) % halves) for i in range(halves)])
    for c in chunks:
        gather(c, 2)
    for s in range(2, far):
        for c in chunks:
            gather(c, s + 1)
        expert(*every(s))
        if s + 1 < far:
            hold(every(s + 1), done[0][s])
        else:
            hold([(c, key) for c in chunks for key in ("top", "bottom")], done[0][s])
    for c in chunks:
        expert((c, "top"), (c, "bottom"))

    right, left = [None] * CHUNKS, [None] * CHUNKS
    empty = jnp.zeros((mid, width), jnp.bfloat16)
    for c in chunks:
        right[c] = shift(done[c]["top"], 1)
        left[c] = shift(done[c]["bottom"], -1)
    hold(every(0), [done[c]["top"] for c in chunks])
    expert(*every(0))
    hold(every(1), right, left, done[0][0])
    for c in chunks:
        right[c] = jnp.concatenate([right[c], empty], axis=0)
        left[c] = jnp.concatenate([empty, left[c]], axis=0)
    for s in range(far - 1, 0, -1):
        for c in chunks:
            right[c] = shift(add(done[c][s], right[c]), 1)
            left[c] = shift(add(done[c][-s], left[c]), -1)
        if s == far - 1:
            expert(*every(1))
    mixed = [
        (
            done[c][0].astype(jnp.float32)
            + right[c].astype(jnp.float32)
            + left[c].astype(jnp.float32)
        ).astype(jnp.bfloat16)
        for c in chunks
    ]
    return jnp.concatenate(mixed, axis=0) if CHUNKS > 1 else mixed[0]


def solution(mesh):
    placed = (
        P(("group", "expert", "dp"), None),
        P(("group", "expert", "dp"), None),
        P(("group", "expert", "dp"), None),
        P("group"),
        P("expert", None, None, "dp"),
        P("expert", None, None, "dp"),
        P("expert", "dp", None),
        P("expert", "dp", None),
    )
    return jax.shard_map(
        functools.partial(shards, ring_order(mesh)),
        mesh=mesh,
        in_specs=placed,
        out_specs=P(("group", "expert", "dp"), None),
        check_vma=False,
    )
```

time: 843 us -> 176 us (0.21)
  the two profiles are of different devices: /device:TPU:13 before, /device:TPU:0 now
where the time goes in v2:
time: 176 us
  waiting for transfers between devices  81.9 us (47%)
  Pallas kernels  69 us (39%)
  starting transfers between devices  19.6 us (11%)
  local copies, waits for them, and re-layouts  2.44 us (1%)
  other arithmetic  2.32 us (1%)
    ppermute x16, waiting for transfers between devices, shift(): lax.ppermute(x, 'expert', [(order[i], order[(i + by) % owners]) for i in...  81.9 us
    pallas_call x5, Pallas kernels, run_expert(): pl.pallas_call(functools.partial(expert_kernel, sizes, owners), out_shape...  56.8 us
    ppermute x16, starting transfers between devices, shift(): lax.ppermute(x, 'expert', [(order[i], order[(i + by) % owners]) for i in...  19.6 us
    pallas_call x1, Pallas kernels, dequantize(): pl.pallas_call(dequantize_kernel, grid=(tiles, 3), out_shape=jax.ShapeDty...  9.72 us
  transfers between devices with their start and end apart: 17, of which 9 were waited for; matrix products, arithmetic and copies ran while one was open for 1% of the time, Pallas kernels for 32%

profile of v2, /device:TPU:0, one launch (start us, length us, event | category | flops | bytes accessed | tf_op | source)
XLA Modules:
  0.0 176.1 jit_solution(3690282744955666117)
XLA Ops:
  0.7 2.5 %route.1.refs_0_ = bf16[128,3712]{1,0:T(8,128)(2,1)} custom-call(s32[1]{0:T(128)S(6)} %copy.10.hot_ref, s32[4,128]{1,0:T(4,128)} %bitcast.11, f32[4,128]{1,0:T(4,128)} %bitcast.12, bf16[128,3584]{1,0:T(8,128)(2,1)} %tokens_ref.1), custom_call_target="tpu_custom_call" | custom-call | tf_op jit(solution)/shard_map/route/pallas_call | solution.py:114
  3.1 3.0 %collective-permute-start = (bf16[128,3712]{1,0:T(8,128)(2,1)}, bf16[128,3712]{1,0:T(8,128)(2,1)S(1)}, u32[]{:S(2)}, u32[]{:S(2)}) collective-permute-start(bf16[128,3712]{1,0:T(8,128)(2,1)} %route.1.refs_0_), channel_id=1, source_target_pairs={{0,2},{4,0},{8,4},{12,8},{14,12},{10,14},{6,10},{2,6},{1,3},{5,1},... | collective-permute-start | bytes 2850824 | tf_op jit(solution)/shard_map/ppermute | solution.py:217
  6.9 9.7 %dequantize.1.own = bf16[2,5376,512]{2,1,0:T(8,128)(2,1)} custom-call(f32[2,28,4]{2,1,0:T(8,128)} %bitcast.9, f32[4,28]{1,0:T(4,128)} %bitcast.10, bf16[2,3584,512]{2,1,0:T(8,128)(2,1)} %bitcast.7, bf16[512,3584]{1,0:T(8,128)(2,1)} %bitcast.8), custom_call_target="tpu_custom_call" | custom-call | flops 11010048 | bytes 22020096 | tf_op jit(solution)/shard_map/dequantize/pallas_call | solution.py:66
  16.6 10.8 %collective-permute-done.refs_0_ = bf16[128,3712]{1,0:T(8,128)(2,1)S(1)} collective-permute-done((bf16[128,3712]{1,0:T(8,128)(2,1)}, bf16[128,3712]{1,0:T(8,128)(2,1)S(1)}, u32[]{:S(2)}, u32[]{:S(2)}) %collective-permute-start) | collective-permute-done | bytes 950304 | tf_op jit(solution)/shard_map/ppermute | solution.py:217
  27.4 1.4 collective-permute-done.1.refs_1_
  29.3 1.6 collective-permute-start.5
  30.9 21.5 %collective-permute-done.3.refs_1_ = bf16[128,3712]{1,0:T(8,128)(2,1)} collective-permute-done((bf16[128,3712]{1,0:T(8,128)(2,1)S(1)}, bf16[128,3712]{1,0:T(8,128)(2,1)}, u32[]{:S(2)}, u32[]{:S(2)}) %collective-permute-start.3) | collective-permute-done | bytes 950304 | tf_op jit(solution)/shard_map/ppermute | solution.py:217
  52.8 1.6 collective-permute-start.7
  54.4 12.1 %expert.5 = (bf16[128,3584]{1,0:T(8,128)(2,1)}, bf16[128,3584]{1,0:T(8,128)(2,1)}) custom-call(s32[1]{0:T(128)} %bitcast.who_ref, bf16[2,5376,512]{2,1,0:T(8,128)(2,1)} %dequantize.1.own, bf16[2,5376,512]{2,1,0:T(8,128)(2,1)} %collective-permute-done.2.sib, bf16[128,3712]{1,0:T(8,128)(2,1)} %collective-permute-done.5.refs_0_, ...), custom_call_target="tpu_custom_call" | custom-call | flops 5637144576 | bytes 22020096 | tf_op jit(solution)/shard_map/expert/pallas_call | solution.py:182
  66.6 8.7 %collective-permute-done.4.refs_1_ = bf16[128,3712]{1,0:T(8,128)(2,1)S(1)} collective-permute-done((bf16[128,3712]{1,0:T(8,128)(2,1)}, bf16[128,3712]{1,0:T(8,128)(2,1)S(1)}, u32[]{:S(2)}, u32[]{:S(2)}) %collective-permute-start.4) | collective-permute-done | bytes 950304 | tf_op jit(solution)/shard_map/ppermute | solution.py:217
  75.4 1.7 collective-permute-start.8
  77.7 12.2 %expert.6 = (bf16[128,3584]{1,0:T(8,128)(2,1)}, bf16[128,3584]{1,0:T(8,128)(2,1)}) custom-call(s32[1]{0:T(128)} %bitcast.who_ref, bf16[2,5376,512]{2,1,0:T(8,128)(2,1)} %dequantize.1.own, bf16[2,5376,512]{2,1,0:T(8,128)(2,1)} %collective-permute-done.2.sib, bf16[128,3712]{1,0:T(8,128)(2,1)} %copy-done.2, bf16[128,3712]{1,0:T(8,128)(2,1)} %copy-done.1), custom_call_target="tpu_custom_call" | custom-call | flops 5637144576 | bytes 22020096 | tf_op jit(solution)/shard_map/expert/pallas_call | solution.py:182
  91.6 10.1 %expert.7 = (bf16[64,3584]{1,0:T(8,128)(2,1)}, bf16[64,3584]{1,0:T(8,128)(2,1)}) custom-call(s32[1]{0:T(128)} %bitcast.who_ref, bf16[2,5376,512]{2,1,0:T(8,128)(2,1)} %dequantize.1.own, bf16[2,5376,512]{2,1,0:T(8,128)(2,1)} %collective-permute-done.2.sib, bf16[64,3712]{1,0:T(8,128)(2,1)} %copy-done.12, bf16[64,3712]{1,0:T(8,128)(2,1)} %copy-done.11), custom_call_target="tpu_custom_call" | custom-call | flops 2818572288 | bytes 22020096 | tf_op jit(solution)/shard_map/expert/pallas_call | solution.py:182
  101.7 1.8 %collective-permute-start.9 = (bf16[64,3584]{1,0:T(8,128)(2,1)}, bf16[64,3584]{1,0:T(8,128)(2,1)S(1)}, u32[]{:S(2)}, u32[]{:S(2)}) collective-permute-start(bf16[64,3584]{1,0:T(8,128)(2,1)} %get-tuple-element.36), channel_id=1, source_target_pairs={{0,4},{4,8},{8,12},{12,14},{14,10},{10,6},{6,2},{2,0},{1,5},{5,9},... | collective-permute-start | bytes 1376264 | tf_op jit(solution)/shard_map/ppermute | solution.py:217
  103.7 10.2 %expert.8 = bf16[128,3584]{1,0:T(8,128)(2,1)} custom-call(s32[1]{0:T(128)} %bitcast.who_ref, bf16[2,5376,512]{2,1,0:T(8,128)(2,1)} %dequantize.1.own, bf16[2,5376,512]{2,1,0:T(8,128)(2,1)} %collective-permute-done.2.sib, bf16[128,3712]{1,0:T(8,128)(2,1)} %route.1.refs_0_), custom_call_target="tpu_custom_call" | custom-call | flops 2818572288 | bytes 22020096 | tf_op jit(solution)/shard_map/expert/pallas_call | solution.py:182
  114.1 1.8 %collective-permute-start.11 = (bf16[128,3584]{1,0:T(8,128)(2,1)S(1)}, bf16[128,3584]{1,0:T(8,128)(2,1)S(1)}, u32[]{:S(2)}, u32[]{:S(2)}) collective-permute-start(bf16[128,3584]{1,0:T(8,128)(2,1)S(1)} %add_convert_fusion.6), channel_id=1, source_target_pairs={{0,4},{4,8},{8,12},{12,14},{14,10},{10,6},{6,2},{2,0},{1,5},{5,9},... | collective-permute-start | bytes 2752520 | tf_op jit(solution)/shard_map/ppermute | solution.py:217
  117.0 12.2 %expert.9 = (bf16[128,3584]{1,0:T(8,128)(2,1)}, bf16[128,3584]{1,0:T(8,128)(2,1)}) custom-call(s32[1]{0:T(128)} %bitcast.who_ref, bf16[2,5376,512]{2,1,0:T(8,128)(2,1)} %dequantize.1.own, bf16[2,5376,512]{2,1,0:T(8,128)(2,1)} %collective-permute-done.2.sib, bf16[128,3712]{1,0:T(8,128)(2,1)} %copy-done.3, bf16[128,3712]{1,0:T(8,128)(2,1)} %copy-done.4), custom_call_target="tpu_custom_call" | custom-call | flops 5637144576 | bytes 22020096 | tf_op jit(solution)/shard_map/expert/pallas_call | solution.py:182
  129.2 5.2 %collective-permute-done.11 = bf16[128,3584]{1,0:T(8,128)(2,1)S(1)} collective-permute-done((bf16[128,3584]{1,0:T(8,128)(2,1)S(1)}, bf16[128,3584]{1,0:T(8,128)(2,1)S(1)}, u32[]{:S(2)}, u32[]{:S(2)}) %collective-permute-start.11) | collective-permute-done | bytes 917536 | tf_op jit(solution)/shard_map/ppermute | solution.py:217
  134.6 1.8 %collective-permute-start.12 = (bf16[128,3584]{1,0:T(8,128)(2,1)S(1)}, bf16[128,3584]{1,0:T(8,128)(2,1)S(1)}, u32[]{:S(2)}, u32[]{:S(2)}) collective-permute-start(bf16[128,3584]{1,0:T(8,128)(2,1)S(1)} %add_convert_fusion.5), channel_id=1, source_target_pairs={{0,4},{4,8},{8,12},{12,14},{14,10},{10,6},{6,2},{2,0},{1,5},{5,9},... | collective-permute-start | bytes 2752520 | tf_op jit(solution)/shard_map/ppermute | solution.py:217
  137.5 17.4 %collective-permute-done.12 = bf16[128,3584]{1,0:T(8,128)(2,1)S(1)} collective-permute-done((bf16[128,3584]{1,0:T(8,128)(2,1)S(1)}, bf16[128,3584]{1,0:T(8,128)(2,1)S(1)}, u32[]{:S(2)}, u32[]{:S(2)}) %collective-permute-start.12) | collective-permute-done | bytes 917536 | tf_op jit(solution)/shard_map/ppermute | solution.py:217
  155.1 1.8 %collective-permute-start.13 = (bf16[128,3584]{1,0:T(8,128)(2,1)S(1)}, bf16[128,3584]{1,0:T(8,128)(2,1)S(1)}, u32[]{:S(2)}, u32[]{:S(2)}) collective-permute-start(bf16[128,3584]{1,0:T(8,128)(2,1)S(1)} %add_convert_fusion.4), channel_id=1, source_target_pairs={{0,4},{4,8},{8,12},{12,14},{14,10},{10,6},{6,2},{2,0},{1,5},{5,9},... | collective-permute-start | bytes 2752520 | tf_op jit(solution)/shard_map/ppermute | solution.py:217
  158.0 15.5 %collective-permute-done.13 = bf16[128,3584]{1,0:T(8,128)(2,1)S(1)} collective-permute-done((bf16[128,3584]{1,0:T(8,128)(2,1)S(1)}, bf16[128,3584]{1,0:T(8,128)(2,1)S(1)}, u32[]{:S(2)}, u32[]{:S(2)}) %collective-permute-start.13) | collective-permute-done | bytes 917536 | tf_op jit(solution)/shard_map/ppermute | solution.py:217
  173.5 1.4 collective-permute-done.16
  174.9 1.3 add_convert_fusion
  (55 shorter events, 8.1 us)
Async XLA Ops:
  3.1 24.3 %collective-permute-start = (bf16[128,3712]{1,0:T(8,128)(2,1)}, bf16[128,3712]{1,0:T(8,128)(2,1)S(1)}, u32[]{:S(2)}, u32[]{:S(2)}) collective-permute-start(bf16[128,3712]{1,0:T(8,128)(2,1)} %route.1.refs_0_), channel_id=1, source_target_pairs={{0,2},{4,0},{8,4},{12,8},{14,12},{10,14},{6,10},{2,6},{1,3},{5,1},... | collective-permute-start | bytes 2850824 | tf_op jit(solution)/shard_map/ppermute | solution.py:217
  6.1 22.7 %collective-permute-start.1 = (bf16[128,3712]{1,0:T(8,128)(2,1)}, bf16[128,3712]{1,0:T(8,128)(2,1)S(1)}, u32[]{:S(2)}, u32[]{:S(2)}) collective-permute-start(bf16[128,3712]{1,0:T(8,128)(2,1)} %route.1.refs_0_), channel_id=1, source_target_pairs={{0,4},{4,8},{8,12},{12,14},{14,10},{10,6},{6,2},{2,0},{1,5},{5,9},... | collective-permute-start | bytes 2850824 | tf_op jit(solution)/shard_map/ppermute | solution.py:217
  27.4 39.2 %copy-start.3 = (bf16[128,3712]{1,0:T(8,128)(2,1)}, bf16[128,3712]{1,0:T(8,128)(2,1)S(1)}, u32[]{:S(2)}) copy-start(bf16[128,3712]{1,0:T(8,128)(2,1)S(1)} %collective-permute-done.refs_0_) | copy-start | bytes 2850820
  28.8 25.6 %collective-permute-start.2 = (bf16[2,5376,512]{2,1,0:T(8,128)(2,1)}, bf16[2,5376,512]{2,1,0:T(8,128)(2,1)}, u32[]{:S(2)}, u32[]{:S(2)}) collective-permute-start(bf16[2,5376,512]{2,1,0:T(8,128)(2,1)} %dequantize.1.own), channel_id=1, source_target_pairs={{0,1},{1,0},{2,3},{3,2},{4,5},{5,4},{6,7},{7,6},{8,9},{9,8},{10,11... | collective-permute-start | bytes 33030152 | tf_op jit(solution)/shard_map/ppermute | solution.py:253
  28.8 23.6 %collective-permute-start.3 = (bf16[128,3712]{1,0:T(8,128)(2,1)S(1)}, bf16[128,3712]{1,0:T(8,128)(2,1)}, u32[]{:S(2)}, u32[]{:S(2)}) collective-permute-start(bf16[128,3712]{1,0:T(8,128)(2,1)S(1)} %collective-permute-done.1.refs_1_), channel_id=1, source_target_pairs={{0,4},{4,8},{8,12},{12,14},{14,10},{10,6},{6,2},{2,0},{1,5},{5,9},... | collective-permute-start | bytes 2850824 | tf_op jit(solution)/shard_map/ppermute | solution.py:217
  29.3 23.5 %collective-permute-start.5 = (bf16[128,3712]{1,0:T(8,128)(2,1)S(1)}, bf16[128,3712]{1,0:T(8,128)(2,1)}, u32[]{:S(2)}, u32[]{:S(2)}) collective-permute-start(bf16[128,3712]{1,0:T(8,128)(2,1)S(1)} %collective-permute-done.refs_0_), channel_id=1, source_target_pairs={{0,2},{4,0},{8,4},{12,8},{14,12},{10,14},{6,10},{2,6},{1,3},{5,1},... | collective-permute-start | bytes 2850824 | tf_op jit(solution)/shard_map/ppermute | solution.py:217
  52.4 22.9 %collective-permute-start.4 = (bf16[128,3712]{1,0:T(8,128)(2,1)}, bf16[128,3712]{1,0:T(8,128)(2,1)S(1)}, u32[]{:S(2)}, u32[]{:S(2)}) collective-permute-start(bf16[128,3712]{1,0:T(8,128)(2,1)} %collective-permute-done.3.refs_1_), channel_id=1, source_target_pairs={{0,4},{4,8},{8,12},{12,14},{14,10},{10,6},{6,2},{2,0},{1,5},{5,9},... | collective-permute-start | bytes 2850824 | tf_op jit(solution)/shard_map/ppermute | solution.py:217
  52.8 22.6 %collective-permute-start.7 = (bf16[128,3712]{1,0:T(8,128)(2,1)}, bf16[128,3712]{1,0:T(8,128)(2,1)S(1)}, u32[]{:S(2)}, u32[]{:S(2)}) collective-permute-start(bf16[128,3712]{1,0:T(8,128)(2,1)} %collective-permute-done.5.refs_0_), channel_id=1, source_target_pairs={{0,2},{4,0},{8,4},{12,8},{14,12},{10,14},{6,10},{2,6},{1,3},{5,1},... | collective-permute-start | bytes 2850824 | tf_op jit(solution)/shard_map/ppermute | solution.py:217
  75.4 14.6 %collective-permute-start.8 = (bf16[64,3712]{1,0:T(8,128)(2,1)S(1)}, bf16[64,3712]{1,0:T(8,128)(2,1)S(1)}, u32[]{:S(2)}, u32[]{:S(2)}) collective-permute-start(bf16[64,3712]{1,0:T(8,128)(2,1)S(1)} %slice.7), channel_id=1, source_target_pairs={{0,2},{4,0},{8,4},{12,8},{14,12},{10,14},{6,10},{2,6},{1,3},{5,1},... | collective-permute-start | bytes 1425416 | tf_op jit(solution)/shard_map/ppermute | solution.py:217
  77.2 12.8 %collective-permute-start.6 = (bf16[64,3712]{1,0:T(8,128)(2,1)S(1)}, bf16[64,3712]{1,0:T(8,128)(2,1)S(1)}, u32[]{:S(2)}, u32[]{:S(2)}) collective-permute-start(bf16[64,3712]{1,0:T(8,128)(2,1)S(1)} %slice.6), channel_id=1, source_target_pairs={{0,4},{4,8},{8,12},{12,14},{14,10},{10,6},{6,2},{2,0},{1,5},{5,9},... | collective-permute-start | bytes 1425416 | tf_op jit(solution)/shard_map/ppermute | solution.py:217
  101.7 12.3 %collective-permute-start.9 = (bf16[64,3584]{1,0:T(8,128)(2,1)}, bf16[64,3584]{1,0:T(8,128)(2,1)S(1)}, u32[]{:S(2)}, u32[]{:S(2)}) collective-permute-start(bf16[64,3584]{1,0:T(8,128)(2,1)} %get-tuple-element.36), channel_id=1, source_target_pairs={{0,4},{4,8},{8,12},{12,14},{14,10},{10,6},{6,2},{2,0},{1,5},{5,9},... | collective-permute-start | bytes 1376264 | tf_op jit(solution)/shard_map/ppermute | solution.py:217
  103.5 10.5 %copy-start.6 = (bf16[128,3584]{1,0:T(8,128)(2,1)S(1)}, bf16[128,3584]{1,0:T(8,128)(2,1)}, u32[]{:S(2)}) copy-start(bf16[128,3584]{1,0:T(8,128)(2,1)} %get-tuple-element.33) | copy-start | bytes 2752516
  103.5 12.4 %collective-permute-start.10 = (bf16[64,3584]{1,0:T(8,128)(2,1)}, bf16[64,3584]{1,0:T(8,128)(2,1)S(1)}, u32[]{:S(2)}, u32[]{:S(2)}) collective-permute-start(bf16[64,3584]{1,0:T(8,128)(2,1)} %get-tuple-element.38), channel_id=1, source_target_pairs={{0,2},{4,0},{8,4},{12,8},{14,12},{10,14},{6,10},{2,6},{1,3},{5,1},... | collective-permute-start | bytes 1376264 | tf_op jit(solution)/shard_map/ppermute | solution.py:217
  114.1 20.3 %collective-permute-start.11 = (bf16[128,3584]{1,0:T(8,128)(2,1)S(1)}, bf16[128,3584]{1,0:T(8,128)(2,1)S(1)}, u32[]{:S(2)}, u32[]{:S(2)}) collective-permute-start(bf16[128,3584]{1,0:T(8,128)(2,1)S(1)} %add_convert_fusion.6), channel_id=1, source_target_pairs={{0,4},{4,8},{8,12},{12,14},{14,10},{10,6},{6,2},{2,0},{1,5},{5,9},... | collective-permute-start | bytes 2752520 | tf_op jit(solution)/shard_map/ppermute | solution.py:217
  116.0 18.4 %copy-start.8 = (bf16[128,3584]{1,0:T(8,128)(2,1)S(1)}, bf16[128,3584]{1,0:T(8,128)(2,1)}, u32[]{:S(2)}) copy-start(bf16[128,3584]{1,0:T(8,128)(2,1)} %get-tuple-element.30) | copy-start | bytes 2752516
  116.0 20.4 %collective-permute-start.14 = (bf16[128,3584]{1,0:T(8,128)(2,1)S(1)}, bf16[128,3584]{1,0:T(8,128)(2,1)S(1)}, u32[]{:S(2)}, u32[]{:S(2)}) collective-permute-start(bf16[128,3584]{1,0:T(8,128)(2,1)S(1)} %add_convert_fusion.3), channel_id=1, source_target_pairs={{0,2},{4,0},{8,4},{12,8},{14,12},{10,14},{6,10},{2,6},{1,3},{5,1},... | collective-permute-start | bytes 2752520 | tf_op jit(solution)/shard_map/ppermute | solution.py:217
  129.2 7.2 %copy-start.7 = (bf16[128,3584]{1,0:T(8,128)(2,1)S(1)}, bf16[128,3584]{1,0:T(8,128)(2,1)}, u32[]{:S(2)}) copy-start(bf16[128,3584]{1,0:T(8,128)(2,1)} %get-tuple-element.43) | copy-start | bytes 2752516
  134.6 20.3 %copy-start.10 = (bf16[128,3584]{1,0:T(8,128)(2,1)S(1)}, bf16[128,3584]{1,0:T(8,128)(2,1)}, u32[]{:S(2)}) copy-start(bf16[128,3584]{1,0:T(8,128)(2,1)} %get-tuple-element.41) | copy-start | bytes 2752516
  134.6 20.3 %collective-permute-start.12 = (bf16[128,3584]{1,0:T(8,128)(2,1)S(1)}, bf16[128,3584]{1,0:T(8,128)(2,1)S(1)}, u32[]{:S(2)}, u32[]{:S(2)}) collective-permute-start(bf16[128,3584]{1,0:T(8,128)(2,1)S(1)} %add_convert_fusion.5), channel_id=1, source_target_pairs={{0,4},{4,8},{8,12},{12,14},{14,10},{10,6},{6,2},{2,0},{1,5},{5,9},... | collective-permute-start | bytes 2752520 | tf_op jit(solution)/shard_map/ppermute | solution.py:217
  136.6 20.3 %copy-start.9 = (bf16[128,3584]{1,0:T(8,128)(2,1)S(1)}, bf16[128,3584]{1,0:T(8,128)(2,1)}, u32[]{:S(2)}) copy-start(bf16[128,3584]{1,0:T(8,128)(2,1)} %get-tuple-element.42) | copy-start | bytes 2752516
  136.6 20.3 %collective-permute-start.15 = (bf16[128,3584]{1,0:T(8,128)(2,1)S(1)}, bf16[128,3584]{1,0:T(8,128)(2,1)S(1)}, u32[]{:S(2)}, u32[]{:S(2)}) collective-permute-start(bf16[128,3584]{1,0:T(8,128)(2,1)S(1)} %add_convert_fusion.2), channel_id=1, source_target_pairs={{0,2},{4,0},{8,4},{12,8},{14,12},{10,14},{6,10},{2,6},{1,3},{5,1},... | collective-permute-start | bytes 2752520 | tf_op jit(solution)/shard_map/ppermute | solution.py:217
  155.1 19.8 %copy-start = (bf16[128,3584]{1,0:T(8,128)(2,1)S(1)}, bf16[128,3584]{1,0:T(8,128)(2,1)}, u32[]{:S(2)}) copy-start(bf16[128,3584]{1,0:T(8,128)(2,1)} %expert.8) | copy-start | bytes 2752516
  155.1 18.4 %collective-permute-start.13 = (bf16[128,3584]{1,0:T(8,128)(2,1)S(1)}, bf16[128,3584]{1,0:T(8,128)(2,1)S(1)}, u32[]{:S(2)}, u32[]{:S(2)}) collective-permute-start(bf16[128,3584]{1,0:T(8,128)(2,1)S(1)} %add_convert_fusion.4), channel_id=1, source_target_pairs={{0,4},{4,8},{8,12},{12,14},{14,10},{10,6},{6,2},{2,0},{1,5},{5,9},... | collective-permute-start | bytes 2752520 | tf_op jit(solution)/shard_map/ppermute | solution.py:217
  157.1 17.7 %collective-permute-start.16 = (bf16[128,3584]{1,0:T(8,128)(2,1)S(1)}, bf16[128,3584]{1,0:T(8,128)(2,1)S(1)}, u32[]{:S(2)}, u32[]{:S(2)}) collective-permute-start(bf16[128,3584]{1,0:T(8,128)(2,1)S(1)} %add_convert_fusion.1), channel_id=1, source_target_pairs={{0,2},{4,0},{8,4},{12,8},{14,12},{10,14},{6,10},{2,6},{1,3},{5,1},... | collective-permute-start | bytes 2752520 | tf_op jit(solution)/shard_map/ppermute | solution.py:217
  (7 other events, 16.6 us)

commit v3 on v2

--- a/solution.py
+++ b/solution.py
@@ -74,7 +74,7 @@
             pl.BlockSpec((TILE_F, width), lambda f, p: (f, 0)),
         ],
         out_specs=pl.BlockSpec((1, chunk, 2 * TILE_F), lambda f, p: (f, p, 0)),
-        compiler_params=pltpu.CompilerParams(vmem_limit_bytes=VMEM_LIMIT),
+        compiler_params=pltpu.CompilerParams(vmem_limit_bytes=24 * 1024 * 1024),
         cost_estimate=cost(6 * width * half, 12 * width * half),
         name="dequantize",
     )(in_scale, out_scale, in_raw, out_raw)
@@ -123,55 +123,60 @@
 def expert_kernel(sizes, owners, who_ref, own, sib, *refs):
     blocks = len(sizes)
     x_refs, o_refs = refs[:blocks], refs[blocks : 2 * blocks]
-    rows, total, held, arrived = refs[2 * blocks :]
+    rows, total = refs[2 * blocks :]
     starts = [sum(sizes[:i]) for i in range(blocks)]
     half_tiles, width = own.shape[0], rows.shape[1]
     tiles = 2 * half_tiles
-    cut = width // 2
-
-    def copies(ref, at, tile):
-        return [
-            pltpu.make_async_copy(
-                ref.at[at, pl.ds(part * cut, cut)],
-                held.at[tile, pl.ds(part * cut, cut)],
-                arrived.at[tile, part],
-            )
-            for part in range(3)
-        ]
-
-    landed = []
-    for tile in range(tiles):
-        half = own if tile < half_tiles else sib
-        landed.append(copies(half, tile % half_tiles, tile))
-        for copy in landed[-1]:
-            copy.start()
     for start, size, x_ref in zip(starts, sizes, x_refs):
         rows[start : start + size, :] = x_ref[:, :width]
 
     for tile in range(tiles):
-        landed[tile][0].wait()
-        both = jnp.dot(rows[:, :cut], held[tile, :cut], preferred_element_type=jnp.float32)
-        landed[tile][1].wait()
-        both += jnp.dot(
-            rows[:, cut:], held[tile, cut : 2 * cut], preferred_element_type=jnp.float32
-        )
+        held, at = (own, tile) if tile < half_tiles else (sib, tile - half_tiles)
+        both = jnp.dot(rows[...], held[at, :width], preferred_element_type=jnp.float32)
         gate, up = both[:, :TILE_F], both[:, TILE_F:]
         hidden = (gate / (1.0 + jnp.exp(-gate)) * up).astype(jnp.bfloat16)
-        landed[tile][2].wait()
         for i in range(width // (2 * TILE_F)):
-            at = slice(i * 2 * TILE_F, (i + 1) * 2 * TILE_F)
+            to = slice(i * 2 * TILE_F, (i + 1) * 2 * TILE_F)
             term = jnp.dot(
                 hidden,
-                held[tile, width + i * TILE_F : width + (i + 1) * TILE_F],
+                held[at, width + i * TILE_F : width + (i + 1) * TILE_F],
                 preferred_element_type=jnp.float32,
             )
-            total[:, at] = term if tile == 0 else total[:, at] + term
+            total[:, to] = term if tile == 0 else total[:, to] + term
     for start, size, x_ref, o_ref in zip(starts, sizes, x_refs, o_refs):
         lane = lax.broadcasted_iota(jnp.int32, (size, LANES), 1)
         picked = (lax.rem(lane, owners) == who_ref[0]) & (lane < 3 * owners)
         weight = jnp.where(picked, x_ref[:, width:].astype(jnp.float32), 0.0)
         weight = jnp.sum(weight, axis=1, keepdims=True)
         o_ref[...] = (total[start : start + size, :] * weight).astype(jnp.bfloat16)
+
+
+def keep_kernel(own_from, sib_from, own_to, sib_to, arrived):
+    copies = []
+    for side, (from_ref, to_ref) in enumerate(((own_from, own_to), (sib_from, sib_to))):
+        for tile in range(from_ref.shape[0]):
+            copies.append(
+                pltpu.make_async_copy(
+                    from_ref.at[tile], to_ref.at[tile], arrived.at[side, tile]
+                )
+            )
+    for copy in copies:
+        copy.start()
+    for copy in copies:
+        copy.wait()
+
+
+def keep(own, sib):
+    held = pl.pallas_call(
+        keep_kernel,
+        out_shape=[pltpu.VMEM(own.shape, own.dtype)] * 2,
+        in_specs=[pl.BlockSpec(memory_space=pl.ANY)] * 2,
+        out_specs=[pl.BlockSpec(memory_space=pltpu.VMEM)] * 2,
+        scratch_shapes=[pltpu.SemaphoreType.DMA((2, own.shape[0]))],
+        compiler_params=pltpu.CompilerParams(vmem_limit_bytes=2 * 1024 * 1024),
+        name="keep",
+    )(own, sib)
+    return [pltpu.with_memory_space_constraint(h, pltpu.VMEM) for h in held]
 
 
 def run_expert(blocks, owners, who, own, sib):
@@ -183,16 +188,13 @@
         functools.partial(expert_kernel, sizes, owners),
         out_shape=[jax.ShapeDtypeStruct((size, width), jnp.bfloat16) for size in sizes],
         in_specs=[pl.BlockSpec(memory_space=pltpu.SMEM)]
-        + [pl.BlockSpec(memory_space=pl.ANY)] * 2
-        + [whole] * len(blocks),
+        + [whole] * (2 + len(blocks)),
         out_specs=[whole] * len(blocks),
         scratch_shapes=[
             pltpu.VMEM((m, width), jnp.bfloat16),
             pltpu.VMEM((m, width), jnp.float32),
-            pltpu.VMEM((2 * tiles,) + own.shape[1:], jnp.bfloat16),
-            pltpu.SemaphoreType.DMA((2 * tiles, 3)),
         ],
-        compiler_params=pltpu.CompilerParams(vmem_limit_bytes=VMEM_LIMIT),
+        compiler_params=pltpu.CompilerParams(vmem_limit_bytes=24 * 1024 * 1024),
         cost_estimate=cost(12 * m * width * tiles * TILE_F, 12 * width * tiles * TILE_F),
         name="expert",
     )(who, own, sib, *blocks)
@@ -253,6 +255,7 @@
     sib = lax.ppermute(halved, "dp", [(i, (i + 1) % halves) for i in range(halves)])
     for c in chunks:
         gather(c, 2)
+    own, sib = keep(own, sib)
     for s in range(2, far):
         for c in chunks:
             gather(c, s + 1)

time: 176 us -> 163 us (0.926)
  Pallas kernels: 69 us -> 44.2 us
  waiting for transfers between devices: 81.9 us -> 91 us
  local copies, waits for them, and re-layouts: 2.44 us -> 6.27 us
    pallas_call x5, Pallas kernels: 56.8 us -> 27.5 us  [run_expert(): pl.pallas_call(functools.partial(expert_kernel, sizes, owners), out_shape...]
    ppermute x16, waiting for transfers between devices: 81.9 us -> 91 us  [shift(): lax.ppermute(x, 'expert', [(order[i], order[(i + by) % owners]) for i in...]
    pallas_call x0 -> x1, Pallas kernels: none -> 7.36 us  [keep(): pl.pallas_call(keep_kernel, out_shape=[pltpu.VMEM(own.shape, own.dtype)]...]
    unnamed x29 -> x15, local copies, waits for them, and re-layouts: 2.37 us -> 6.2 us
    pallas_call x1, Pallas kernels: 9.72 us -> 6.95 us  [dequantize(): pl.pallas_call(dequantize_kernel, grid=(tiles, 3), out_shape=jax.ShapeDty...]
  transfers between devices with their start and end apart: 17 -> 17, of which waited for: 9 -> 13; matrix products, arithmetic and copies ran while one was open for 1% -> 1% of each run, Pallas kernels for 32% -> 24%
where the time goes in v3:
time: 163 us
  waiting for transfers between devices  91 us (56%)
  Pallas kernels  44.2 us (27%)
  starting transfers between devices  18.1 us (11%)
  local copies, waits for them, and re-layouts  6.27 us (4%)
  other arithmetic  2.4 us (1%)
    ppermute x16, waiting for transfers between devices, shift(): lax.ppermute(x, 'expert', [(order[i], order[(i + by) % owners]) for i in...  91 us
    pallas_call x5, Pallas kernels, run_expert(): pl.pallas_call(functools.partial(expert_kernel, sizes, owners), out_shape...  27.5 us
    ppermute x16, starting transfers between devices, shift(): lax.ppermute(x, 'expert', [(order[i], order[(i + by) % owners]) for i in...  18.1 us
    pallas_call x1, Pallas kernels, keep(): pl.pallas_call(keep_kernel, out_shape=[pltpu.VMEM(own.shape, own.dtype)]...  7.36 us
    pallas_call x1, Pallas kernels, dequantize(): pl.pallas_call(dequantize_kernel, grid=(tiles, 3), out_shape=jax.ShapeDty...  6.95 us
    unnamed x15, local copies, waits for them, and re-layouts  6.2 us
  transfers between devices with their start and end apart: 17, of which 13 were waited for; matrix products, arithmetic and copies ran while one was open for 1% of the time, Pallas kernels for 24%

profile of v3, /device:TPU:0, one launch (start us, length us, event | category | flops | bytes accessed | tf_op | source)
XLA Modules:
  0.0 162.7 jit_solution(13202974841050068827)
XLA Ops:
  0.7 2.4 %route.1.refs_0_ = bf16[128,3712]{1,0:T(8,128)(2,1)} custom-call(s32[1]{0:T(128)S(6)} %copy.10.hot_ref, s32[4,128]{1,0:T(4,128)} %bitcast.11, f32[4,128]{1,0:T(4,128)} %bitcast.12, bf16[128,3584]{1,0:T(8,128)(2,1)} %tokens_ref.1), custom_call_target="tpu_custom_call" | custom-call | tf_op jit(solution)/shard_map/route/pallas_call | solution.py:114
  3.1 3.0 %collective-permute-start = (bf16[128,3712]{1,0:T(8,128)(2,1)}, bf16[128,3712]{1,0:T(8,128)(2,1)S(1)}, u32[]{:S(2)}, u32[]{:S(2)}) collective-permute-start(bf16[128,3712]{1,0:T(8,128)(2,1)} %route.1.refs_0_), channel_id=1, source_target_pairs={{0,2},{4,0},{8,4},{12,8},{14,12},{10,14},{6,10},{2,6},{1,3},{5,1},... | collective-permute-start | bytes 2850824 | tf_op jit(solution)/shard_map/ppermute | solution.py:219
  6.2 3.1 %copy-done = bf16[1,2,3584,512]{3,2,1,0:T(8,128)(2,1)S(1)} copy-done((bf16[1,2,3584,512]{3,2,1,0:T(8,128)(2,1)S(1)}, bf16[1,2,3584,512]{3,2,1,0:T(8,128)(2,1)}, u32[]{:S(2)}) %copy-start) | copy-done | bytes 7340056
  9.3 2.0 %copy-done.2 = bf16[1,512,3584]{2,1,0:T(8,128)(2,1)S(1)} copy-done((bf16[1,512,3584]{2,1,0:T(8,128)(2,1)S(1)}, bf16[1,512,3584]{2,1,0:T(8,128)(2,1)}, u32[]{:S(2)}) %copy-start.2) | copy-done | bytes 3670040
  11.3 7.0 %dequantize.1.own_from = bf16[2,5376,512]{2,1,0:T(8,128)(2,1)} custom-call(f32[2,28,4]{2,1,0:T(8,128)S(1)} %bitcast.9, f32[4,28]{1,0:T(4,128)S(1)} %bitcast.10, bf16[2,3584,512]{2,1,0:T(8,128)(2,1)S(1)} %bitcast.7, bf16[512,3584]{1,0:T(8,128)(2,1)S(1)} %bitcast.8), custom_call_target="tpu_custom_call" | custom-call | flops 11010048 | bytes 22020096 | tf_op jit(solution)/shard_map/dequantize/pallas_call | solution.py:66
  18.3 9.1 %collective-permute-done.refs_0_ = bf16[128,3712]{1,0:T(8,128)(2,1)S(1)} collective-permute-done((bf16[128,3712]{1,0:T(8,128)(2,1)}, bf16[128,3712]{1,0:T(8,128)(2,1)S(1)}, u32[]{:S(2)}, u32[]{:S(2)}) %collective-permute-start) | collective-permute-done | bytes 950304 | tf_op jit(solution)/shard_map/ppermute | solution.py:219
  31.8 20.6 %collective-permute-done.3.refs_1_ = bf16[128,3712]{1,0:T(8,128)(2,1)} collective-permute-done((bf16[128,3712]{1,0:T(8,128)(2,1)S(1)}, bf16[128,3712]{1,0:T(8,128)(2,1)}, u32[]{:S(2)}, u32[]{:S(2)}) %collective-permute-start.3) | collective-permute-done | bytes 950304 | tf_op jit(solution)/shard_map/ppermute | solution.py:219
  55.1 7.4 %keep.1 = (bf16[2,5376,512]{2,1,0:T(8,128)(2,1)S(1)}, bf16[2,5376,512]{2,1,0:T(8,128)(2,1)S(1)}) custom-call(bf16[2,5376,512]{2,1,0:T(8,128)(2,1)} %dequantize.1.own_from, bf16[2,5376,512]{2,1,0:T(8,128)(2,1)} %collective-permute-done.2.sib_from), custom_call_target="tpu_custom_call" | custom-call | tf_op jit(solution)/shard_map/keep/pallas_call | solution.py:170
  62.4 7.7 %expert.5 = (bf16[128,3584]{1,0:T(8,128)(2,1)S(1)}, bf16[128,3584]{1,0:T(8,128)(2,1)S(1)}) custom-call(s32[1]{0:T(128)} %bitcast.who_ref, bf16[2,5376,512]{2,1,0:T(8,128)(2,1)S(1)} %get-tuple-element.32.own, bf16[2,5376,512]{2,1,0:T(8,128)(2,1)S(1)} %get-tuple-element.33.sib, bf16[128,3712]{1,0:T(8,128)(2,1)} %collective-permute-done.5.refs_0_, ...), custom_call_target="tpu_custom_call" | custom-call | flops 5637144576 | bytes 22020096 | tf_op jit(solution)/shard_map/expert/pallas_call | solution.py:187
  70.2 5.1 %collective-permute-done.4.refs_1_ = bf16[128,3712]{1,0:T(8,128)(2,1)S(1)} collective-permute-done((bf16[128,3712]{1,0:T(8,128)(2,1)}, bf16[128,3712]{1,0:T(8,128)(2,1)S(1)}, u32[]{:S(2)}, u32[]{:S(2)}) %collective-permute-start.4) | collective-permute-done | bytes 950304 | tf_op jit(solution)/shard_map/ppermute | solution.py:219
  76.0 1.7 %collective-permute-start.8 = (bf16[64,3712]{1,0:T(8,128)(2,1)S(1)}, bf16[64,3712]{1,0:T(8,128)(2,1)S(1)}, u32[]{:S(2)}, u32[]{:S(2)}) collective-permute-start(bf16[64,3712]{1,0:T(8,128)(2,1)S(1)} %slice.7), channel_id=1, source_target_pairs={{0,2},{4,0},{8,4},{12,8},{14,12},{10,14},{6,10},{2,6},{1,3},{5,1},... | collective-permute-start | bytes 1425416 | tf_op jit(solution)/shard_map/ppermute | solution.py:219
  78.3 6.3 %expert.6 = (bf16[128,3584]{1,0:T(8,128)(2,1)S(1)}, bf16[128,3584]{1,0:T(8,128)(2,1)S(1)}) custom-call(s32[1]{0:T(128)} %bitcast.who_ref, bf16[2,5376,512]{2,1,0:T(8,128)(2,1)S(1)} %get-tuple-element.32.own, bf16[2,5376,512]{2,1,0:T(8,128)(2,1)S(1)} %get-tuple-element.33.sib, bf16[128,3712]{1,0:T(8,128)(2,1)S(1)} %collective-permute-done.7.refs_0_, ...), custom_call_target="tpu_custom_call" | custom-call | flops 5637144576 | bytes 22020096 | tf_op jit(solution)/shard_map/expert/pallas_call | solution.py:187
  84.6 2.7 %collective-permute-done.8.refs_1_ = bf16[64,3712]{1,0:T(8,128)(2,1)S(1)} collective-permute-done((bf16[64,3712]{1,0:T(8,128)(2,1)S(1)}, bf16[64,3712]{1,0:T(8,128)(2,1)S(1)}, u32[]{:S(2)}, u32[]{:S(2)}) %collective-permute-start.8) | collective-permute-done | bytes 475168 | tf_op jit(solution)/shard_map/ppermute | solution.py:219
  89.0 3.6 %expert.7 = (bf16[64,3584]{1,0:T(8,128)(2,1)S(1)}, bf16[64,3584]{1,0:T(8,128)(2,1)S(1)}) custom-call(s32[1]{0:T(128)} %bitcast.who_ref, bf16[2,5376,512]{2,1,0:T(8,128)(2,1)S(1)} %get-tuple-element.32.own, bf16[2,5376,512]{2,1,0:T(8,128)(2,1)S(1)} %get-tuple-element.33.sib, bf16[64,3712]{1,0:T(8,128)(2,1)S(1)} %collective-permute-done.6.refs_0_, ...), custom_call_target="tpu_custom_call" | custom-call | flops 2818572288 | bytes 22020096 | tf_op jit(solution)/shard_map/expert/pallas_call | solution.py:187
  93.0 1.7 %collective-permute-start.10 = (bf16[64,3584]{1,0:T(8,128)(2,1)S(1)}, bf16[64,3584]{1,0:T(8,128)(2,1)S(1)}, u32[]{:S(2)}, u32[]{:S(2)}) collective-permute-start(bf16[64,3584]{1,0:T(8,128)(2,1)S(1)} %get-tuple-element.42), channel_id=1, source_target_pairs={{0,2},{4,0},{8,4},{12,8},{14,12},{10,14},{6,10},{2,6},{1,3},{5,1},... | collective-permute-start | bytes 1376264 | tf_op jit(solution)/shard_map/ppermute | solution.py:219
  94.7 3.7 %expert.8 = bf16[128,3584]{1,0:T(8,128)(2,1)S(1)} custom-call(s32[1]{0:T(128)} %bitcast.who_ref, bf16[2,5376,512]{2,1,0:T(8,128)(2,1)S(1)} %get-tuple-element.32.own, bf16[2,5376,512]{2,1,0:T(8,128)(2,1)S(1)} %get-tuple-element.33.sib, bf16[128,3712]{1,0:T(8,128)(2,1)S(1)} %copy-done.1), custom_call_target="tpu_custom_call" | custom-call | flops 2818572288 | bytes 22020096 | tf_op jit(solution)/shard_map/expert/pallas_call | solution.py:187
  98.3 4.8 %collective-permute-done.9 = bf16[64,3584]{1,0:T(8,128)(2,1)S(1)} collective-permute-done((bf16[64,3584]{1,0:T(8,128)(2,1)S(1)}, bf16[64,3584]{1,0:T(8,128)(2,1)S(1)}, u32[]{:S(2)}, u32[]{:S(2)}) %collective-permute-start.9) | collective-permute-done | bytes 458784 | tf_op jit(solution)/shard_map/ppermute | solution.py:219
  103.8 1.9 %collective-permute-start.14 = (bf16[128,3584]{1,0:T(8,128)(2,1)S(1)}, bf16[128,3584]{1,0:T(8,128)(2,1)S(1)}, u32[]{:S(2)}, u32[]{:S(2)}) collective-permute-start(bf16[128,3584]{1,0:T(8,128)(2,1)S(1)} %add_convert_fusion.3), channel_id=1, source_target_pairs={{0,2},{4,0},{8,4},{12,8},{14,12},{10,14},{6,10},{2,6},{1,3},{5,1},... | collective-permute-start | bytes 2752520 | tf_op jit(solution)/shard_map/ppermute | solution.py:219
  105.7 6.3 %expert.9 = (bf16[128,3584]{1,0:T(8,128)(2,1)S(1)}, bf16[128,3584]{1,0:T(8,128)(2,1)S(1)}) custom-call(s32[1]{0:T(128)} %bitcast.who_ref, bf16[2,5376,512]{2,1,0:T(8,128)(2,1)S(1)} %get-tuple-element.32.own, bf16[2,5376,512]{2,1,0:T(8,128)(2,1)S(1)} %get-tuple-element.33.sib, bf16[128,3712]{1,0:T(8,128)(2,1)S(1)} %collective-permute-done.refs_0_, ...), custom_call_target="tpu_custom_call" | custom-call | flops 5637144576 | bytes 22020096 | tf_op jit(solution)/shard_map/expert/pallas_call | solution.py:187
  112.0 11.6 %collective-permute-done.11 = bf16[128,3584]{1,0:T(8,128)(2,1)S(1)} collective-permute-done((bf16[128,3584]{1,0:T(8,128)(2,1)S(1)}, bf16[128,3584]{1,0:T(8,128)(2,1)S(1)}, u32[]{:S(2)}, u32[]{:S(2)}) %collective-permute-start.11) | collective-permute-done | bytes 917536 | tf_op jit(solution)/shard_map/ppermute | solution.py:219
  124.4 1.7 %collective-permute-start.15 = (bf16[128,3584]{1,0:T(8,128)(2,1)S(1)}, bf16[128,3584]{1,0:T(8,128)(2,1)S(1)}, u32[]{:S(2)}, u32[]{:S(2)}) collective-permute-start(bf16[128,3584]{1,0:T(8,128)(2,1)S(1)} %add_convert_fusion.2), channel_id=1, source_target_pairs={{0,2},{4,0},{8,4},{12,8},{14,12},{10,14},{6,10},{2,6},{1,3},{5,1},... | collective-permute-start | bytes 2752520 | tf_op jit(solution)/shard_map/ppermute | solution.py:219
  126.1 18.0 %collective-permute-done.12 = bf16[128,3584]{1,0:T(8,128)(2,1)S(1)} collective-permute-done((bf16[128,3584]{1,0:T(8,128)(2,1)S(1)}, bf16[128,3584]{1,0:T(8,128)(2,1)S(1)}, u32[]{:S(2)}, u32[]{:S(2)}) %collective-permute-start.12) | collective-permute-done | bytes 917536 | tf_op jit(solution)/shard_map/ppermute | solution.py:219
  144.9 1.7 %collective-permute-start.16 = (bf16[128,3584]{1,0:T(8,128)(2,1)S(1)}, bf16[128,3584]{1,0:T(8,128)(2,1)S(1)}, u32[]{:S(2)}, u32[]{:S(2)}) collective-permute-start(bf16[128,3584]{1,0:T(8,128)(2,1)S(1)} %add_convert_fusion.1), channel_id=1, source_target_pairs={{0,2},{4,0},{8,4},{12,8},{14,12},{10,14},{6,10},{2,6},{1,3},{5,1},... | collective-permute-start | bytes 2752520 | tf_op jit(solution)/shard_map/ppermute | solution.py:219
  146.6 14.7 %collective-permute-done.13 = bf16[128,3584]{1,0:T(8,128)(2,1)S(1)} collective-permute-done((bf16[128,3584]{1,0:T(8,128)(2,1)S(1)}, bf16[128,3584]{1,0:T(8,128)(2,1)S(1)}, u32[]{:S(2)}, u32[]{:S(2)}) %collective-permute-start.13) | collective-permute-done | bytes 917536 | tf_op jit(solution)/shard_map/ppermute | solution.py:219
  (42 shorter events, 14.4 us)
Async XLA Ops:
  0.0 6.1 %copy-start.6 = (f32[1,2,28,4]{2,3,1,0:T(4,128)S(1)}, f32[1,2,28,4]{2,3,1,0:T(4,128)}, u32[]{:S(2)}) copy-start(f32[1,2,28,4]{2,3,1,0:T(4,128)} %param.13) | copy-start | bytes 2692
  0.0 6.2 %copy-start.5 = (f32[1,4,28]{2,1,0:T(4,128)S(1)}, f32[1,4,28]{2,1,0:T(4,128)}, u32[]{:S(2)}) copy-start(f32[1,4,28]{2,1,0:T(4,128)} %param.15) | copy-start | bytes 1348
  3.1 24.3 %collective-permute-start = (bf16[128,3712]{1,0:T(8,128)(2,1)}, bf16[128,3712]{1,0:T(8,128)(2,1)S(1)}, u32[]{:S(2)}, u32[]{:S(2)}) collective-permute-start(bf16[128,3712]{1,0:T(8,128)(2,1)} %route.1.refs_0_), channel_id=1, source_target_pairs={{0,2},{4,0},{8,4},{12,8},{14,12},{10,14},{6,10},{2,6},{1,3},{5,1},... | collective-permute-start | bytes 2850824 | tf_op jit(solution)/shard_map/ppermute | solution.py:219
  6.0 22.7 %collective-permute-start.1 = (bf16[128,3712]{1,0:T(8,128)(2,1)}, bf16[128,3712]{1,0:T(8,128)(2,1)S(1)}, u32[]{:S(2)}, u32[]{:S(2)}) collective-permute-start(bf16[128,3712]{1,0:T(8,128)(2,1)} %route.1.refs_0_), channel_id=1, source_target_pairs={{0,4},{4,8},{8,12},{12,14},{14,10},{10,6},{6,2},{2,0},{1,5},{5,9},... | collective-permute-start | bytes 2850824 | tf_op jit(solution)/shard_map/ppermute | solution.py:219
  6.2 3.1 %copy-start = (bf16[1,2,3584,512]{3,2,1,0:T(8,128)(2,1)S(1)}, bf16[1,2,3584,512]{3,2,1,0:T(8,128)(2,1)}, u32[]{:S(2)}) copy-start(bf16[1,2,3584,512]{3,2,1,0:T(8,128)(2,1)} %param.12) | copy-start | bytes 22020100
  9.3 2.0 %copy-start.2 = (bf16[1,512,3584]{2,1,0:T(8,128)(2,1)S(1)}, bf16[1,512,3584]{2,1,0:T(8,128)(2,1)}, u32[]{:S(2)}) copy-start(bf16[1,512,3584]{2,1,0:T(8,128)(2,1)} %param.14) | copy-start | bytes 11010052
  28.8 26.3 %collective-permute-start.2 = (bf16[2,5376,512]{2,1,0:T(8,128)(2,1)}, bf16[2,5376,512]{2,1,0:T(8,128)(2,1)}, u32[]{:S(2)}, u32[]{:S(2)}) collective-permute-start(bf16[2,5376,512]{2,1,0:T(8,128)(2,1)} %dequantize.1.own_from), channel_id=1, source_target_pairs={{0,1},{1,0},{2,3},{3,2},{4,5},{5,4},{6,7},{7,6},{8,9},{9,8},{10,11... | collective-permute-start | bytes 33030152 | tf_op jit(solution)/shard_map/ppermute | solution.py:255
  28.8 23.6 %collective-permute-start.3 = (bf16[128,3712]{1,0:T(8,128)(2,1)S(1)}, bf16[128,3712]{1,0:T(8,128)(2,1)}, u32[]{:S(2)}, u32[]{:S(2)}) collective-permute-start(bf16[128,3712]{1,0:T(8,128)(2,1)S(1)} %collective-permute-done.1.refs_1_), channel_id=1, source_target_pairs={{0,4},{4,8},{8,12},{12,14},{14,10},{10,6},{6,2},{2,0},{1,5},{5,9},... | collective-permute-start | bytes 2850824 | tf_op jit(solution)/shard_map/ppermute | solution.py:219
  29.1 1.0 copy-start.3
  30.1 23.3 %collective-permute-start.5 = (bf16[128,3712]{1,0:T(8,128)(2,1)S(1)}, bf16[128,3712]{1,0:T(8,128)(2,1)}, u32[]{:S(2)}, u32[]{:S(2)}) collective-permute-start(bf16[128,3712]{1,0:T(8,128)(2,1)S(1)} %collective-permute-done.refs_0_), channel_id=1, source_target_pairs={{0,2},{4,0},{8,4},{12,8},{14,12},{10,14},{6,10},{2,6},{1,3},{5,1},... | collective-permute-start | bytes 2850824 | tf_op jit(solution)/shard_map/ppermute | solution.py:219
  52.3 22.9 %collective-permute-start.4 = (bf16[128,3712]{1,0:T(8,128)(2,1)}, bf16[128,3712]{1,0:T(8,128)(2,1)S(1)}, u32[]{:S(2)}, u32[]{:S(2)}) collective-permute-start(bf16[128,3712]{1,0:T(8,128)(2,1)} %collective-permute-done.3.refs_1_), channel_id=1, source_target_pairs={{0,4},{4,8},{8,12},{12,14},{14,10},{10,6},{6,2},{2,0},{1,5},{5,9},... | collective-permute-start | bytes 2850824 | tf_op jit(solution)/shard_map/ppermute | solution.py:219
  53.4 22.6 %collective-permute-start.7 = (bf16[128,3712]{1,0:T(8,128)(2,1)}, bf16[128,3712]{1,0:T(8,128)(2,1)S(1)}, u32[]{:S(2)}, u32[]{:S(2)}) collective-permute-start(bf16[128,3712]{1,0:T(8,128)(2,1)} %collective-permute-done.5.refs_0_), channel_id=1, source_target_pairs={{0,2},{4,0},{8,4},{12,8},{14,12},{10,14},{6,10},{2,6},{1,3},{5,1},... | collective-permute-start | bytes 2850824 | tf_op jit(solution)/shard_map/ppermute | solution.py:219
  76.0 11.3 %collective-permute-start.8 = (bf16[64,3712]{1,0:T(8,128)(2,1)S(1)}, bf16[64,3712]{1,0:T(8,128)(2,1)S(1)}, u32[]{:S(2)}, u32[]{:S(2)}) collective-permute-start(bf16[64,3712]{1,0:T(8,128)(2,1)S(1)} %slice.7), channel_id=1, source_target_pairs={{0,2},{4,0},{8,4},{12,8},{14,12},{10,14},{6,10},{2,6},{1,3},{5,1},... | collective-permute-start | bytes 1425416 | tf_op jit(solution)/shard_map/ppermute | solution.py:219
  77.8 11.2 %collective-permute-start.6 = (bf16[64,3712]{1,0:T(8,128)(2,1)S(1)}, bf16[64,3712]{1,0:T(8,128)(2,1)S(1)}, u32[]{:S(2)}, u32[]{:S(2)}) collective-permute-start(bf16[64,3712]{1,0:T(8,128)(2,1)S(1)} %slice.6), channel_id=1, source_target_pairs={{0,4},{4,8},{8,12},{12,14},{14,10},{10,6},{6,2},{2,0},{1,5},{5,9},... | collective-permute-start | bytes 1425416 | tf_op jit(solution)/shard_map/ppermute | solution.py:219
  87.3 7.3 %copy-start.1 = (bf16[128,3712]{1,0:T(8,128)(2,1)S(1)}, bf16[128,3712]{1,0:T(8,128)(2,1)}, u32[]{:S(2)}) copy-start(bf16[128,3712]{1,0:T(8,128)(2,1)} %route.1.refs_0_) | copy-start | bytes 2850820
  92.6 10.6 %collective-permute-start.9 = (bf16[64,3584]{1,0:T(8,128)(2,1)S(1)}, bf16[64,3584]{1,0:T(8,128)(2,1)S(1)}, u32[]{:S(2)}, u32[]{:S(2)}) collective-permute-start(bf16[64,3584]{1,0:T(8,128)(2,1)S(1)} %get-tuple-element.40), channel_id=1, source_target_pairs={{0,4},{4,8},{8,12},{12,14},{14,10},{10,6},{6,2},{2,0},{1,5},{5,9},... | collective-permute-start | bytes 1376264 | tf_op jit(solution)/shard_map/ppermute | solution.py:219
  93.0 10.7 %collective-permute-start.10 = (bf16[64,3584]{1,0:T(8,128)(2,1)S(1)}, bf16[64,3584]{1,0:T(8,128)(2,1)S(1)}, u32[]{:S(2)}, u32[]{:S(2)}) collective-permute-start(bf16[64,3584]{1,0:T(8,128)(2,1)S(1)} %get-tuple-element.42), channel_id=1, source_target_pairs={{0,2},{4,0},{8,4},{12,8},{14,12},{10,14},{6,10},{2,6},{1,3},{5,1},... | collective-permute-start | bytes 1376264 | tf_op jit(solution)/shard_map/ppermute | solution.py:219
  98.3 7.4 %copy-start.4 = (bf16[128,3712]{1,0:T(8,128)(2,1)S(1)}, bf16[128,3712]{1,0:T(8,128)(2,1)}, u32[]{:S(2)}) copy-start(bf16[128,3712]{1,0:T(8,128)(2,1)} %copy-done.3) | copy-start | bytes 2850820
  103.3 20.3 %collective-permute-start.11 = (bf16[128,3584]{1,0:T(8,128)(2,1)S(1)}, bf16[128,3584]{1,0:T(8,128)(2,1)S(1)}, u32[]{:S(2)}, u32[]{:S(2)}) collective-permute-start(bf16[128,3584]{1,0:T(8,128)(2,1)S(1)} %add_convert_fusion.6), channel_id=1, source_target_pairs={{0,4},{4,8},{8,12},{12,14},{14,10},{10,6},{6,2},{2,0},{1,5},{5,9},... | collective-permute-start | bytes 2752520 | tf_op jit(solution)/shard_map/ppermute | solution.py:219
  103.8 20.4 %collective-permute-start.14 = (bf16[128,3584]{1,0:T(8,128)(2,1)S(1)}, bf16[128,3584]{1,0:T(8,128)(2,1)S(1)}, u32[]{:S(2)}, u32[]{:S(2)}) collective-permute-start(bf16[128,3584]{1,0:T(8,128)(2,1)S(1)} %add_convert_fusion.3), channel_id=1, source_target_pairs={{0,2},{4,0},{8,4},{12,8},{14,12},{10,14},{6,10},{2,6},{1,3},{5,1},... | collective-permute-start | bytes 2752520 | tf_op jit(solution)/shard_map/ppermute | solution.py:219
  123.8 20.3 %collective-permute-start.12 = (bf16[128,3584]{1,0:T(8,128)(2,1)S(1)}, bf16[128,3584]{1,0:T(8,128)(2,1)S(1)}, u32[]{:S(2)}, u32[]{:S(2)}) collective-permute-start(bf16[128,3584]{1,0:T(8,128)(2,1)S(1)} %add_convert_fusion.5), channel_id=1, source_target_pairs={{0,4},{4,8},{8,12},{12,14},{14,10},{10,6},{6,2},{2,0},{1,5},{5,9},... | collective-permute-start | bytes 2752520 | tf_op jit(solution)/shard_map/ppermute | solution.py:219
  124.4 20.3 %collective-permute-start.15 = (bf16[128,3584]{1,0:T(8,128)(2,1)S(1)}, bf16[128,3584]{1,0:T(8,128)(2,1)S(1)}, u32[]{:S(2)}, u32[]{:S(2)}) collective-permute-start(bf16[128,3584]{1,0:T(8,128)(2,1)S(1)} %add_convert_fusion.2), channel_id=1, source_target_pairs={{0,2},{4,0},{8,4},{12,8},{14,12},{10,14},{6,10},{2,6},{1,3},{5,1},... | collective-permute-start | bytes 2752520 | tf_op jit(solution)/shard_map/ppermute | solution.py:219
  144.3 17.0 %collective-permute-start.13 = (bf16[128,3584]{1,0:T(8,128)(2,1)S(1)}, bf16[128,3584]{1,0:T(8,128)(2,1)S(1)}, u32[]{:S(2)}, u32[]{:S(2)}) collective-permute-start(bf16[128,3584]{1,0:T(8,128)(2,1)S(1)} %add_convert_fusion.4), channel_id=1, source_target_pairs={{0,4},{4,8},{8,12},{12,14},{14,10},{10,6},{6,2},{2,0},{1,5},{5,9},... | collective-permute-start | bytes 2752520 | tf_op jit(solution)/shard_map/ppermute | solution.py:219
  144.9 16.5 %collective-permute-start.16 = (bf16[128,3584]{1,0:T(8,128)(2,1)S(1)}, bf16[128,3584]{1,0:T(8,128)(2,1)S(1)}, u32[]{:S(2)}, u32[]{:S(2)}) collective-permute-start(bf16[128,3584]{1,0:T(8,128)(2,1)S(1)} %add_convert_fusion.1), channel_id=1, source_target_pairs={{0,2},{4,0},{8,4},{12,8},{14,12},{10,14},{6,10},{2,6},{1,3},{5,1},... | collective-permute-start | bytes 2752520 | tf_op jit(solution)/shard_map/ppermute | solution.py:219

commit v4 on v3

--- a/solution.py
+++ b/solution.py
@@ -151,31 +151,81 @@
         o_ref[...] = (total[start : start + size, :] * weight).astype(jnp.bfloat16)
 
 
-def keep_kernel(own_from, sib_from, own_to, sib_to, arrived):
-    copies = []
-    for side, (from_ref, to_ref) in enumerate(((own_from, own_to), (sib_from, sib_to))):
-        for tile in range(from_ref.shape[0]):
-            copies.append(
-                pltpu.make_async_copy(
-                    from_ref.at[tile], to_ref.at[tile], arrived.at[side, tile]
-                )
+def keep_kernel(
+    in_scale, out_scale, own_from, in_raw, out_raw, own_to, sib_to, in_here, out_here, own_sem, in_sem, out_sem
+):
+    tiles, width = own_from.shape[0], in_raw.shape[1]
+    parts = 4
+    chunk = width // parts
+
+    def in_copy(part):
+        rows = pl.ds(pl.multiple_of(part * chunk, QB), chunk)
+        return pltpu.make_async_copy(in_raw.at[:, rows], in_here.at[:, rows], in_sem.at[part])
+
+    out_copy = pltpu.make_async_copy(out_raw, out_here, out_sem)
+    own_copies = [
+        pltpu.make_async_copy(own_from.at[tile], own_to.at[tile], own_sem.at[tile])
+        for tile in range(tiles)
+    ]
+    for part in range(parts):
+        in_copy(part).start()
+    out_copy.start()
+    for copy in own_copies:
+        copy.start()
+
+    def scaled(block, scale):
+        return (block.astype(jnp.float32) * scale).astype(jnp.bfloat16)
+
+    def gate_up(part, carry):
+        in_copy(part).wait()
+        for i in range(chunk // QB):
+            row = part * (chunk // QB) + i
+            rows = pl.ds(pl.multiple_of(row * QB, QB), QB)
+            for side in range(2):
+                for j in range(tiles * TILE_F // QB):
+                    tile, at = (j * QB) // TILE_F, side * TILE_F + (j * QB) % TILE_F
+                    sib_to[tile, rows, at : at + QB] = scaled(
+                        in_here[side, rows, j * QB : (j + 1) * QB], in_scale[side, row, j]
+                    )
+        return carry
+
+    lax.fori_loop(0, parts, gate_up, 0)
+    out_copy.wait()
+    per = 2 * TILE_F // QB
+    below = TILE_F // QB
+
+    def down(i, carry):
+        rows = pl.ds(pl.multiple_of(i * QB, QB), QB)
+        for j in range(width // QB):
+            to = width + (j // per) * TILE_F + lax.rem(i, below) * QB
+            at = (j % per) * QB
+            sib_to[lax.div(i, below), pl.ds(pl.multiple_of(to, QB), QB), at : at + QB] = scaled(
+                out_here[rows, j * QB : (j + 1) * QB], out_scale[i, j]
             )
-    for copy in copies:
-        copy.start()
-    for copy in copies:
+        return carry
+
+    lax.fori_loop(0, tiles * below, down, 0)
+    for copy in own_copies:
         copy.wait()
 
 
-def keep(own, sib):
+def keep(own, in_raw, in_scale, out_raw, out_scale):
+    smem = pl.BlockSpec(memory_space=pltpu.SMEM)
     held = pl.pallas_call(
         keep_kernel,
         out_shape=[pltpu.VMEM(own.shape, own.dtype)] * 2,
-        in_specs=[pl.BlockSpec(memory_space=pl.ANY)] * 2,
+        in_specs=[smem, smem] + [pl.BlockSpec(memory_space=pl.ANY)] * 3,
         out_specs=[pl.BlockSpec(memory_space=pltpu.VMEM)] * 2,
-        scratch_shapes=[pltpu.SemaphoreType.DMA((2, own.shape[0]))],
-        compiler_params=pltpu.CompilerParams(vmem_limit_bytes=2 * 1024 * 1024),
+        scratch_shapes=[
+            pltpu.VMEM(in_raw.shape, in_raw.dtype),
+            pltpu.VMEM(out_raw.shape, out_raw.dtype),
+            pltpu.SemaphoreType.DMA((own.shape[0],)),
+            pltpu.SemaphoreType.DMA((4,)),
+            pltpu.SemaphoreType.DMA(()),
+        ],
+        compiler_params=pltpu.CompilerParams(vmem_limit_bytes=14 * 1024 * 1024),
         name="keep",
-    )(own, sib)
+    )(in_scale, out_scale, own, in_raw, out_raw)
     return [pltpu.with_memory_space_constraint(h, pltpu.VMEM) for h in held]
 
 
@@ -215,10 +265,11 @@
     mid = size // 2
     chunks = range(CHUNKS)
 
-    def shift(x, by):
-        return lax.ppermute(
-            x, "expert", [(order[i], order[(i + by) % owners]) for i in range(owners)]
-        )
+    def shift(x, by, name):
+        with jax.named_scope(name + ("_right" if by > 0 else "_left")):
+            return lax.ppermute(
+                x, "expert", [(order[i], order[(i + by) % owners]) for i in range(owners)]
+            )
 
     def add(a, b):
         return (a.astype(jnp.float32) + b.astype(jnp.float32)).astype(jnp.bfloat16)
@@ -228,11 +279,11 @@
 
     def gather(c, s):
         if s < far:
-            have[c][-s] = shift(have[c][1 - s], 1)
-            have[c][s] = shift(have[c][s - 1], -1)
+            have[c][-s] = shift(have[c][1 - s], 1, f"tokens_{c}_{s}")
+            have[c][s] = shift(have[c][s - 1], -1, f"tokens_{c}_{s}")
         else:
-            have[c]["top"] = shift(have[c][1 - s][:mid], 1)
-            have[c]["bottom"] = shift(have[c][s - 1][mid:], -1)
+            have[c]["top"] = shift(have[c][1 - s][:mid], 1, f"tokens_{c}_{s}")
+            have[c]["bottom"] = shift(have[c][s - 1][mid:], -1, f"tokens_{c}_{s}")
 
     def expert(*keys):
         blocks = [have[c][key] for c, key in keys]
@@ -248,42 +299,48 @@
 
     for c in chunks:
         gather(c, 1)
-    own = dequantize(
-        *after((in_weight[0], in_scale[0], out_weight[0], out_scale[0]), have[0][0])
-    )
-    halved = after(own, [have[c][key] for c, key in every(1)])
-    sib = lax.ppermute(halved, "dp", [(i, (i + 1) % halves) for i in range(halves)])
-    for c in chunks:
-        gather(c, 2)
-    own, sib = keep(own, sib)
+    raw = (in_weight[0], in_scale[0], out_weight[0], out_scale[0])
+    sizes = jnp.concatenate([raw[1].reshape(-1), raw[3].reshape(-1)])
+    in_sib, out_sib, sizes = [
+        lax.ppermute(w, "dp", [(i, (i + 1) % halves) for i in range(halves)])
+        for w in (raw[0], raw[2], sizes)
+    ]
+    own = dequantize(*after(raw, have[0][0]))
     for s in range(2, far):
         for c in chunks:
-            gather(c, s + 1)
-        expert(*every(s))
-        if s + 1 < far:
-            hold(every(s + 1), done[0][s])
-        else:
-            hold([(c, key) for c in chunks for key in ("top", "bottom")], done[0][s])
+            if s == 2:
+                hold([(c, 1), (c, -1)], own)
+            gather(c, s)
+    cut = raw[1].size
+    own, sib = keep(
+        own, in_sib, sizes[:cut].reshape(raw[1].shape), out_sib, sizes[cut:].reshape(raw[3].shape)
+    )
+    hold(every(far - 1), own)
     for c in chunks:
-        expert((c, "top"), (c, "bottom"))
+        gather(c, far)
+        expert((c, far - 1), (c, 1 - far))
+        hold([(c, "top"), (c, "bottom")], done[c][far - 1])
 
     right, left = [None] * CHUNKS, [None] * CHUNKS
     empty = jnp.zeros((mid, width), jnp.bfloat16)
     for c in chunks:
-        right[c] = shift(done[c]["top"], 1)
-        left[c] = shift(done[c]["bottom"], -1)
-    hold(every(0), [done[c]["top"] for c in chunks])
-    expert(*every(0))
-    hold(every(1), right, left, done[0][0])
+        expert((c, "top"), (c, "bottom"))
+        right[c] = shift(done[c]["top"], 1, f"sums_{c}_{far}")
+        left[c] = shift(done[c]["bottom"], -1, f"sums_{c}_{far}")
     for c in chunks:
         right[c] = jnp.concatenate([right[c], empty], axis=0)
         left[c] = jnp.concatenate([empty, left[c]], axis=0)
     for s in range(far - 1, 0, -1):
         for c in chunks:
-            right[c] = shift(add(done[c][s], right[c]), 1)
-            left[c] = shift(add(done[c][-s], left[c]), -1)
-        if s == far - 1:
-            expert(*every(1))
+            keys = [(c, s - 1), (c, 1 - s)] if s > 1 else []
+            if s == 2:
+                keys.append((c, 0))
+            if keys:
+                hold(keys, right[c], left[c])
+            right[c] = shift(add(done[c][s], right[c]), 1, f"sums_{c}_{s}")
+            left[c] = shift(add(done[c][-s], left[c]), -1, f"sums_{c}_{s}")
+            if keys:
+                expert(*keys)
     mixed = [
         (
             done[c][0].astype(jnp.float32)

time: 163 us -> 158 us (0.969)
  waiting for transfers between devices: 91 us -> 83.5 us
  local copies, waits for them, and re-layouts: 6.27 us -> 11.9 us
  Pallas kernels: 44.2 us -> 41.2 us
    ppermute x16, waiting for transfers between devices: 91 us -> 82.3 us  [shift(): lax.ppermute(x, 'expert', [(order[i], order[(i + by) % owners]) for i in...]
    unnamed x15 -> x21, local copies, waits for them, and re-layouts: 6.2 us -> 11.4 us
    pallas_call x1, Pallas kernels: 6.95 us -> 3.99 us  [dequantize(): pl.pallas_call(dequantize_kernel, grid=(tiles, 3), out_shape=jax.ShapeDty...]
    pallas_call x5 -> x4, Pallas kernels: 27.5 us -> 26.3 us  [run_expert(): pl.pallas_call(functools.partial(expert_kernel, sizes, owners), out_shape...]
  transfers between devices with their start and end apart: 17 -> 19, of which waited for: 13 -> 13; matrix products, arithmetic and copies ran while one was open for 1% -> 1% of each run, Pallas kernels for 24% -> 24%
where the time goes in v4:
time: 158 us
  waiting for transfers between devices  83.5 us (53%)
  Pallas kernels  41.2 us (26%)
  starting transfers between devices  18.4 us (12%)
  local copies, waits for them, and re-layouts  11.9 us (8%)
  other arithmetic  2.4 us (2%)
    ppermute x16, waiting for transfers between devices, shift(): lax.ppermute(x, 'expert', [(order[i], order[(i + by) % owners]) for i in...  82.3 us
    pallas_call x4, Pallas kernels, run_expert(): pl.pallas_call(functools.partial(expert_kernel, sizes, owners), out_shape...  26.3 us
    ppermute x16, starting transfers between devices, shift(): lax.ppermute(x, 'expert', [(order[i], order[(i + by) % owners]) for i in...  17.8 us
    unnamed x21, local copies, waits for them, and re-layouts  11.4 us
    pallas_call x1, Pallas kernels, keep(): pl.pallas_call(keep_kernel, out_shape=[pltpu.VMEM(own.shape, own.dtype)]...  8.52 us
    pallas_call x1, Pallas kernels, dequantize(): pl.pallas_call(dequantize_kernel, grid=(tiles, 3), out_shape=jax.ShapeDty...  3.99 us
  transfers between devices with their start and end apart: 19, of which 13 were waited for; matrix products, arithmetic and copies ran while one was open for 1% of the time, Pallas kernels for 24%

profile of v4, /device:TPU:0, one launch (start us, length us, event | category | flops | bytes accessed | tf_op | source)
XLA Modules:
  0.0 158.2 jit_solution(10415455046594222914)
XLA Ops:
  1.2 2.4 %route.1.refs_2_ = bf16[128,3712]{1,0:T(8,128)(2,1)} custom-call(s32[1]{0:T(128)S(6)} %copy.12.hot_ref, s32[4,128]{1,0:T(4,128)} %bitcast.13, f32[4,128]{1,0:T(4,128)} %bitcast.14, bf16[128,3584]{1,0:T(8,128)(2,1)} %tokens_ref.1), custom_call_target="tpu_custom_call" | custom-call | tf_op jit(solution)/shard_map/route/pallas_call | solution.py:114
  3.6 3.0 %collective-permute-start.6 = (bf16[128,3712]{1,0:T(8,128)(2,1)}, bf16[128,3712]{1,0:T(8,128)(2,1)S(1)}, u32[]{:S(2)}, u32[]{:S(2)}) collective-permute-start(bf16[128,3712]{1,0:T(8,128)(2,1)} %route.1.refs_2_), channel_id=1, source_target_pairs={{0,4},{4,8},{8,12},{12,14},{14,10},{10,6},{6,2},{2,0},{1,5},{5,9},... | collective-permute-start | bytes 2850824 | tf_op jit(solution)/shard_map/tokens_0_1_right/ppermute | solution.py:270
  6.7 3.1 %copy-done.1 = bf16[1,2,3584,512]{3,2,1,0:T(8,128)(2,1)S(1)} copy-done((bf16[1,2,3584,512]{3,2,1,0:T(8,128)(2,1)S(1)}, bf16[1,2,3584,512]{3,2,1,0:T(8,128)(2,1)}, u32[]{:S(2)}) %copy-start.1) | copy-done | bytes 7340056
  9.8 2.0 %copy-done.2 = bf16[1,512,3584]{2,1,0:T(8,128)(2,1)S(1)} copy-done((bf16[1,512,3584]{2,1,0:T(8,128)(2,1)S(1)}, bf16[1,512,3584]{2,1,0:T(8,128)(2,1)}, u32[]{:S(2)}) %copy-start.2) | copy-done | bytes 3670040
  11.8 4.0 %dequantize.1.own_from = bf16[2,5376,512]{2,1,0:T(8,128)(2,1)S(1)} custom-call(f32[2,28,4]{2,1,0:T(8,128)S(1)} %bitcast.11, f32[4,28]{1,0:T(4,128)S(1)} %bitcast.12, bf16[2,3584,512]{2,1,0:T(8,128)(2,1)S(1)} %bitcast.8, bf16[512,3584]{1,0:T(8,128)(2,1)S(1)} %bitcast.10), custom_call_target="tpu_custom_call" | custom-call | flops 11010048 | bytes 22020096 | tf_op jit(solution)/shard_map/dequantize/pallas_call | solution.py:66
  15.8 4.2 %copy-done = bf16[2,5376,512]{2,1,0:T(8,128)(2,1)} copy-done((bf16[2,5376,512]{2,1,0:T(8,128)(2,1)}, bf16[2,5376,512]{2,1,0:T(8,128)(2,1)S(1)}, u32[]{:S(2)}) %copy-start) | copy-done | bytes 11010072
  20.0 8.0 %collective-permute-done.6.refs_1_ = bf16[128,3712]{1,0:T(8,128)(2,1)S(1)} collective-permute-done((bf16[128,3712]{1,0:T(8,128)(2,1)}, bf16[128,3712]{1,0:T(8,128)(2,1)S(1)}, u32[]{:S(2)}, u32[]{:S(2)}) %collective-permute-start.6) | collective-permute-done | bytes 950304 | tf_op jit(solution)/shard_map/tokens_0_1_right/ppermute | solution.py:270
  28.0 1.8 %collective-permute-start.7 = (bf16[128,3712]{1,0:T(8,128)(2,1)S(1)}, bf16[128,3712]{1,0:T(8,128)(2,1)S(1)}, u32[]{:S(2)}, u32[]{:S(2)}) collective-permute-start(bf16[128,3712]{1,0:T(8,128)(2,1)S(1)} %collective-permute-done.6.refs_1_), channel_id=1, source_target_pairs={{0,4},{4,8},{8,12},{12,14},{14,10},{10,6},{6,2},{2,0},{1,5},{5,9},... | collective-permute-start | bytes 2850824 | tf_op jit(solution)/shard_map/tokens_0_2_right/ppermute | solution.py:270
  32.0 18.5 %collective-permute-done.7.refs_1_ = bf16[128,3712]{1,0:T(8,128)(2,1)S(1)} collective-permute-done((bf16[128,3712]{1,0:T(8,128)(2,1)S(1)}, bf16[128,3712]{1,0:T(8,128)(2,1)S(1)}, u32[]{:S(2)}, u32[]{:S(2)}) %collective-permute-start.7) | collective-permute-done | bytes 950304 | tf_op jit(solution)/shard_map/tokens_0_2_right/ppermute | solution.py:270
  50.5 1.5 collective-permute-start.8
  55.0 8.5 %keep.1 = (bf16[2,5376,512]{2,1,0:T(8,128)(2,1)S(1)}, bf16[2,5376,512]{2,1,0:T(8,128)(2,1)S(1)}) custom-call(f32[2,28,4]{2,1,0:T(8,128)S(1)} %reshape.26.in_scale, f32[4,28]{1,0:T(4,128)S(1)} %reshape.27.out_scale, bf16[2,5376,512]{2,1,0:T(8,128)(2,1)} %copy-done, bf16[2,3584,512]{2,1,0:T(8,128)(2,1)} %collective-permute-done.1.in_raw, ...), custom_call_target="tpu_custom_call" | custom-call | tf_op jit(solution)/shard_map/keep/pallas_call | solution.py:214
  63.6 8.7 %collective-permute-done.8.refs_1_ = bf16[128,3712]{1,0:T(8,128)(2,1)S(1)} collective-permute-done((bf16[128,3712]{1,0:T(8,128)(2,1)S(1)}, bf16[128,3712]{1,0:T(8,128)(2,1)S(1)}, u32[]{:S(2)}, u32[]{:S(2)}) %collective-permute-start.8) | collective-permute-done | bytes 950304 | tf_op jit(solution)/shard_map/tokens_0_3_right/ppermute | solution.py:270
  72.3 1.9 %collective-permute-done.5.refs_0_ = bf16[128,3712]{1,0:T(8,128)(2,1)S(1)} collective-permute-done((bf16[128,3712]{1,0:T(8,128)(2,1)}, bf16[128,3712]{1,0:T(8,128)(2,1)S(1)}, u32[]{:S(2)}, u32[]{:S(2)}) %collective-permute-start.5) | collective-permute-done | bytes 950304 | tf_op jit(solution)/shard_map/tokens_0_3_left/ppermute | solution.py:270
  75.0 1.3 collective-permute-start.9
  76.3 6.3 %expert.4 = (bf16[128,3584]{1,0:T(8,128)(2,1)S(1)}, bf16[128,3584]{1,0:T(8,128)(2,1)S(1)}) custom-call(s32[1]{0:T(128)} %bitcast.who_ref, bf16[2,5376,512]{2,1,0:T(8,128)(2,1)S(1)} %get-tuple-element.35.own, bf16[2,5376,512]{2,1,0:T(8,128)(2,1)S(1)} %get-tuple-element.36.sib, bf16[128,3712]{1,0:T(8,128)(2,1)S(1)} %collective-permute-done.5.refs_0_, ...), custom_call_target="tpu_custom_call" | custom-call | flops 5637144576 | bytes 22020096 | tf_op jit(solution)/shard_map/expert/pallas_call | solution.py:237
  82.6 1.6 %collective-permute-done.10.refs_1_ = bf16[64,3712]{1,0:T(8,128)(2,1)S(1)} collective-permute-done((bf16[64,3712]{1,0:T(8,128)(2,1)S(1)}, bf16[64,3712]{1,0:T(8,128)(2,1)S(1)}, u32[]{:S(2)}, u32[]{:S(2)}) %collective-permute-start.10) | collective-permute-done | bytes 475168 | tf_op jit(solution)/shard_map/tokens_0_4_left/ppermute | solution.py:270
  85.0 3.6 %expert.5 = (bf16[64,3584]{1,0:T(8,128)(2,1)S(1)}, bf16[64,3584]{1,0:T(8,128)(2,1)S(1)}) custom-call(s32[1]{0:T(128)} %bitcast.who_ref, bf16[2,5376,512]{2,1,0:T(8,128)(2,1)S(1)} %get-tuple-element.35.own, bf16[2,5376,512]{2,1,0:T(8,128)(2,1)S(1)} %get-tuple-element.36.sib, bf16[64,3712]{1,0:T(8,128)(2,1)S(1)} %collective-permute-done.9.refs_0_, ...), custom_call_target="tpu_custom_call" | custom-call | flops 2818572288 | bytes 22020096 | tf_op jit(solution)/shard_map/expert/pallas_call | solution.py:237
  90.7 8.5 %collective-permute-done.11 = bf16[64,3584]{1,0:T(8,128)(2,1)S(1)} collective-permute-done((bf16[64,3584]{1,0:T(8,128)(2,1)S(1)}, bf16[64,3584]{1,0:T(8,128)(2,1)S(1)}, u32[]{:S(2)}, u32[]{:S(2)}) %collective-permute-start.11) | collective-permute-done | bytes 458784 | tf_op jit(solution)/shard_map/sums_0_4_right/ppermute | solution.py:270
  100.3 1.4 collective-permute-start.14
  101.7 7.5 %expert.7 = (bf16[128,3584]{1,0:T(8,128)(2,1)S(1)}, bf16[128,3584]{1,0:T(8,128)(2,1)S(1)}) custom-call(s32[1]{0:T(128)} %bitcast.who_ref, bf16[2,5376,512]{2,1,0:T(8,128)(2,1)S(1)} %get-tuple-element.35.own, bf16[2,5376,512]{2,1,0:T(8,128)(2,1)S(1)} %get-tuple-element.36.sib, bf16[128,3712]{1,0:T(8,128)(2,1)} %collective-permute-done.4.refs_0_, ...), custom_call_target="tpu_custom_call" | custom-call | flops 5637144576 | bytes 22020096 | tf_op jit(solution)/shard_map/expert/pallas_call | solution.py:237
  109.2 10.4 %collective-permute-done.12 = bf16[128,3584]{1,0:T(8,128)(2,1)S(1)} collective-permute-done((bf16[128,3584]{1,0:T(8,128)(2,1)S(1)}, bf16[128,3584]{1,0:T(8,128)(2,1)S(1)}, u32[]{:S(2)}, u32[]{:S(2)}) %collective-permute-start.12) | collective-permute-done | bytes 917536 | tf_op jit(solution)/shard_map/sums_0_3_right/ppermute | solution.py:270
  122.1 9.0 %expert.6 = (bf16[128,3584]{1,0:T(8,128)(2,1)S(1)}, bf16[128,3584]{1,0:T(8,128)(2,1)S(1)}, bf16[128,3584]{1,0:T(8,128)(2,1)S(1)}) custom-call(s32[1]{0:T(128)} %bitcast.who_ref, bf16[2,5376,512]{2,1,0:T(8,128)(2,1)S(1)} %get-tuple-element.35.own, bf16[2,5376,512]{2,1,0:T(8,128)(2,1)S(1)} %get-tuple-element.36.sib, bf16[128,3712]{1,0:T(8,128)(2,1)S(1)} %copy-done.8, ...), custom_call_target="tpu_custom_call" | custom-call | flops 8455716864 | bytes 22020096 | tf_op jit(solution)/shard_map/expert/pallas_call | solution.py:237
  131.2 8.9 %collective-permute-done.15 = bf16[128,3584]{1,0:T(8,128)(2,1)S(1)} collective-permute-done((bf16[128,3584]{1,0:T(8,128)(2,1)S(1)}, bf16[128,3584]{1,0:T(8,128)(2,1)S(1)}, u32[]{:S(2)}, u32[]{:S(2)}) %collective-permute-start.15) | collective-permute-done | bytes 917536 | tf_op jit(solution)/shard_map/sums_0_2_right/ppermute | solution.py:270
  142.6 13.6 %collective-permute-done.16 = bf16[128,3584]{1,0:T(8,128)(2,1)S(1)} collective-permute-done((bf16[128,3584]{1,0:T(8,128)(2,1)S(1)}, bf16[128,3584]{1,0:T(8,128)(2,1)S(1)}, u32[]{:S(2)}, u32[]{:S(2)}) %collective-permute-start.16) | collective-permute-done | bytes 917536 | tf_op jit(solution)/shard_map/sums_0_1_right/ppermute | solution.py:270
  (58 shorter events, 17.7 us)
Async XLA Ops:
  0.0 6.6 %copy-start.9 = (f32[1,2,28,4]{2,3,1,0:T(4,128)S(1)}, f32[1,2,28,4]{2,3,1,0:T(4,128)}, u32[]{:S(2)}) copy-start(f32[1,2,28,4]{2,3,1,0:T(4,128)} %param.13) | copy-start | bytes 2692
  0.0 6.7 %copy-start.4 = (f32[1,4,28]{2,1,0:T(4,128)S(1)}, f32[1,4,28]{2,1,0:T(4,128)}, u32[]{:S(2)}) copy-start(f32[1,4,28]{2,1,0:T(4,128)} %param.15) | copy-start | bytes 1348
  0.0 55.0 %collective-permute-start.1 = (bf16[2,3584,512]{2,1,0:T(8,128)(2,1)}, bf16[2,3584,512]{2,1,0:T(8,128)(2,1)}, u32[]{:S(2)}, u32[]{:S(2)}) collective-permute-start(bf16[2,3584,512]{2,1,0:T(8,128)(2,1)} %bitcast.7), channel_id=1, source_target_pairs={{0,1},{1,0},{2,3},{3,2},{4,5},{5,4},{6,7},{7,6},{8,9},{9,8},{10,11... | collective-permute-start | bytes 22020104 | tf_op jit(solution)/shard_map/ppermute | solution.py:305
  0.5 54.6 %collective-permute-start.2 = (bf16[512,3584]{1,0:T(8,128)(2,1)}, bf16[512,3584]{1,0:T(8,128)(2,1)}, u32[]{:S(2)}, u32[]{:S(2)}) collective-permute-start(bf16[512,3584]{1,0:T(8,128)(2,1)} %bitcast.9), channel_id=1, source_target_pairs={{0,1},{1,0},{2,3},{3,2},{4,5},{5,4},{6,7},{7,6},{8,9},{9,8},{10,11... | collective-permute-start | bytes 11010056 | tf_op jit(solution)/shard_map/ppermute | solution.py:305
  3.6 24.4 %collective-permute-start.6 = (bf16[128,3712]{1,0:T(8,128)(2,1)}, bf16[128,3712]{1,0:T(8,128)(2,1)S(1)}, u32[]{:S(2)}, u32[]{:S(2)}) collective-permute-start(bf16[128,3712]{1,0:T(8,128)(2,1)} %route.1.refs_2_), channel_id=1, source_target_pairs={{0,4},{4,8},{8,12},{12,14},{14,10},{10,6},{6,2},{2,0},{1,5},{5,9},... | collective-permute-start | bytes 2850824 | tf_op jit(solution)/shard_map/tokens_0_1_right/ppermute | solution.py:270
  6.6 24.2 %collective-permute-start.3 = (bf16[128,3712]{1,0:T(8,128)(2,1)}, bf16[128,3712]{1,0:T(8,128)(2,1)S(1)}, u32[]{:S(2)}, u32[]{:S(2)}) collective-permute-start(bf16[128,3712]{1,0:T(8,128)(2,1)} %route.1.refs_2_), channel_id=1, source_target_pairs={{0,2},{4,0},{8,4},{12,8},{14,12},{10,14},{6,10},{2,6},{1,3},{5,1},... | collective-permute-start | bytes 2850824 | tf_op jit(solution)/shard_map/tokens_0_1_left/ppermute | solution.py:270
  6.7 3.1 %copy-start.1 = (bf16[1,2,3584,512]{3,2,1,0:T(8,128)(2,1)S(1)}, bf16[1,2,3584,512]{3,2,1,0:T(8,128)(2,1)}, u32[]{:S(2)}) copy-start(bf16[1,2,3584,512]{3,2,1,0:T(8,128)(2,1)} %param.12) | copy-start | bytes 22020100
  15.8 4.2 %copy-start = (bf16[2,5376,512]{2,1,0:T(8,128)(2,1)}, bf16[2,5376,512]{2,1,0:T(8,128)(2,1)S(1)}, u32[]{:S(2)}) copy-start(bf16[2,5376,512]{2,1,0:T(8,128)(2,1)S(1)} %dequantize.1.own_from) | copy-start | bytes 33030148
  28.0 22.5 %collective-permute-start.7 = (bf16[128,3712]{1,0:T(8,128)(2,1)S(1)}, bf16[128,3712]{1,0:T(8,128)(2,1)S(1)}, u32[]{:S(2)}, u32[]{:S(2)}) collective-permute-start(bf16[128,3712]{1,0:T(8,128)(2,1)S(1)} %collective-permute-done.6.refs_1_), channel_id=1, source_target_pairs={{0,4},{4,8},{8,12},{12,14},{14,10},{10,6},{6,2},{2,0},{1,5},{5,9},... | collective-permute-start | bytes 2850824 | tf_op jit(solution)/shard_map/tokens_0_2_right/ppermute | solution.py:270
  30.8 22.0 %collective-permute-start.4 = (bf16[128,3712]{1,0:T(8,128)(2,1)S(1)}, bf16[128,3712]{1,0:T(8,128)(2,1)}, u32[]{:S(2)}, u32[]{:S(2)}) collective-permute-start(bf16[128,3712]{1,0:T(8,128)(2,1)S(1)} %collective-permute-done.3.refs_0_), channel_id=1, source_target_pairs={{0,2},{4,0},{8,4},{12,8},{14,12},{10,14},{6,10},{2,6},{1,3},{5,1},... | collective-permute-start | bytes 2850824 | tf_op jit(solution)/shard_map/tokens_0_2_left/ppermute | solution.py:270
  50.5 21.7 %collective-permute-start.8 = (bf16[128,3712]{1,0:T(8,128)(2,1)S(1)}, bf16[128,3712]{1,0:T(8,128)(2,1)S(1)}, u32[]{:S(2)}, u32[]{:S(2)}) collective-permute-start(bf16[128,3712]{1,0:T(8,128)(2,1)S(1)} %collective-permute-done.7.refs_1_), channel_id=1, source_target_pairs={{0,4},{4,8},{8,12},{12,14},{14,10},{10,6},{6,2},{2,0},{1,5},{5,9},... | collective-permute-start | bytes 2850824 | tf_op jit(solution)/shard_map/tokens_0_3_right/ppermute | solution.py:270
  52.8 21.3 %collective-permute-start.5 = (bf16[128,3712]{1,0:T(8,128)(2,1)}, bf16[128,3712]{1,0:T(8,128)(2,1)S(1)}, u32[]{:S(2)}, u32[]{:S(2)}) collective-permute-start(bf16[128,3712]{1,0:T(8,128)(2,1)} %collective-permute-done.4.refs_0_), channel_id=1, source_target_pairs={{0,2},{4,0},{8,4},{12,8},{14,12},{10,14},{6,10},{2,6},{1,3},{5,1},... | collective-permute-start | bytes 2850824 | tf_op jit(solution)/shard_map/tokens_0_3_left/ppermute | solution.py:270
  53.6 1.2 collective-permute-start
  74.2 10.0 %collective-permute-start.10 = (bf16[64,3712]{1,0:T(8,128)(2,1)S(1)}, bf16[64,3712]{1,0:T(8,128)(2,1)S(1)}, u32[]{:S(2)}, u32[]{:S(2)}) collective-permute-start(bf16[64,3712]{1,0:T(8,128)(2,1)S(1)} %slice.31), channel_id=1, source_target_pairs={{0,2},{4,0},{8,4},{12,8},{14,12},{10,14},{6,10},{2,6},{1,3},{5,1},... | collective-permute-start | bytes 1425416 | tf_op jit(solution)/shard_map/tokens_0_4_left/ppermute | solution.py:270
  75.0 10.0 %collective-permute-start.9 = (bf16[64,3712]{1,0:T(8,128)(2,1)S(1)}, bf16[64,3712]{1,0:T(8,128)(2,1)S(1)}, u32[]{:S(2)}, u32[]{:S(2)}) collective-permute-start(bf16[64,3712]{1,0:T(8,128)(2,1)S(1)} %slice.30), channel_id=1, source_target_pairs={{0,4},{4,8},{8,12},{12,14},{14,10},{10,6},{6,2},{2,0},{1,5},{5,9},... | collective-permute-start | bytes 1425416 | tf_op jit(solution)/shard_map/tokens_0_4_right/ppermute | solution.py:270
  88.6 10.6 %collective-permute-start.11 = (bf16[64,3584]{1,0:T(8,128)(2,1)S(1)}, bf16[64,3584]{1,0:T(8,128)(2,1)S(1)}, u32[]{:S(2)}, u32[]{:S(2)}) collective-permute-start(bf16[64,3584]{1,0:T(8,128)(2,1)S(1)} %get-tuple-element.44), channel_id=1, source_target_pairs={{0,4},{4,8},{8,12},{12,14},{14,10},{10,6},{6,2},{2,0},{1,5},{5,9},... | collective-permute-start | bytes 1376264 | tf_op jit(solution)/shard_map/sums_0_4_right/ppermute | solution.py:270
  89.5 10.7 %collective-permute-start.13 = (bf16[64,3584]{1,0:T(8,128)(2,1)S(1)}, bf16[64,3584]{1,0:T(8,128)(2,1)S(1)}, u32[]{:S(2)}, u32[]{:S(2)}) collective-permute-start(bf16[64,3584]{1,0:T(8,128)(2,1)S(1)} %get-tuple-element.46), channel_id=1, source_target_pairs={{0,2},{4,0},{8,4},{12,8},{14,12},{10,14},{6,10},{2,6},{1,3},{5,1},... | collective-permute-start | bytes 1376264 | tf_op jit(solution)/shard_map/sums_0_4_left/ppermute | solution.py:270
  99.3 20.3 %collective-permute-start.12 = (bf16[128,3584]{1,0:T(8,128)(2,1)S(1)}, bf16[128,3584]{1,0:T(8,128)(2,1)S(1)}, u32[]{:S(2)}, u32[]{:S(2)}) collective-permute-start(bf16[128,3584]{1,0:T(8,128)(2,1)S(1)} %add_convert_fusion.6), channel_id=1, source_target_pairs={{0,4},{4,8},{8,12},{12,14},{14,10},{10,6},{6,2},{2,0},{1,5},{5,9},... | collective-permute-start | bytes 2752520 | tf_op jit(solution)/shard_map/sums_0_3_right/ppermute | solution.py:270
  100.3 20.4 %collective-permute-start.14 = (bf16[128,3584]{1,0:T(8,128)(2,1)S(1)}, bf16[128,3584]{1,0:T(8,128)(2,1)S(1)}, u32[]{:S(2)}, u32[]{:S(2)}) collective-permute-start(bf16[128,3584]{1,0:T(8,128)(2,1)S(1)} %add_convert_fusion.5), channel_id=1, source_target_pairs={{0,2},{4,0},{8,4},{12,8},{14,12},{10,14},{6,10},{2,6},{1,3},{5,1},... | collective-permute-start | bytes 2752520 | tf_op jit(solution)/shard_map/sums_0_3_left/ppermute | solution.py:270
  119.5 2.6 %copy-start.8 = (bf16[128,3712]{1,0:T(8,128)(2,1)S(1)}, bf16[128,3712]{1,0:T(8,128)(2,1)}, u32[]{:S(2)}) copy-start(bf16[128,3712]{1,0:T(8,128)(2,1)} %copy-done.7) | copy-start | bytes 2850820
  119.8 20.3 %collective-permute-start.15 = (bf16[128,3584]{1,0:T(8,128)(2,1)S(1)}, bf16[128,3584]{1,0:T(8,128)(2,1)S(1)}, u32[]{:S(2)}, u32[]{:S(2)}) collective-permute-start(bf16[128,3584]{1,0:T(8,128)(2,1)S(1)} %add_convert_fusion.4), channel_id=1, source_target_pairs={{0,4},{4,8},{8,12},{12,14},{14,10},{10,6},{6,2},{2,0},{1,5},{5,9},... | collective-permute-start | bytes 2752520 | tf_op jit(solution)/shard_map/sums_0_2_right/ppermute | solution.py:270
  120.9 20.3 %collective-permute-start.17 = (bf16[128,3584]{1,0:T(8,128)(2,1)S(1)}, bf16[128,3584]{1,0:T(8,128)(2,1)S(1)}, u32[]{:S(2)}, u32[]{:S(2)}) collective-permute-start(bf16[128,3584]{1,0:T(8,128)(2,1)S(1)} %add_convert_fusion.2), channel_id=1, source_target_pairs={{0,2},{4,0},{8,4},{12,8},{14,12},{10,14},{6,10},{2,6},{1,3},{5,1},... | collective-permute-start | bytes 2752520 | tf_op jit(solution)/shard_map/sums_0_2_left/ppermute | solution.py:270
  140.3 16.0 %collective-permute-start.16 = (bf16[128,3584]{1,0:T(8,128)(2,1)S(1)}, bf16[128,3584]{1,0:T(8,128)(2,1)S(1)}, u32[]{:S(2)}, u32[]{:S(2)}) collective-permute-start(bf16[128,3584]{1,0:T(8,128)(2,1)S(1)} %add_convert_fusion.3), channel_id=1, source_target_pairs={{0,4},{4,8},{8,12},{12,14},{14,10},{10,6},{6,2},{2,0},{1,5},{5,9},... | collective-permute-start | bytes 2752520 | tf_op jit(solution)/shard_map/sums_0_1_right/ppermute | solution.py:270
  141.4 15.5 %collective-permute-start.18 = (bf16[128,3584]{1,0:T(8,128)(2,1)S(1)}, bf16[128,3584]{1,0:T(8,128)(2,1)S(1)}, u32[]{:S(2)}, u32[]{:S(2)}) collective-permute-start(bf16[128,3584]{1,0:T(8,128)(2,1)S(1)} %add_convert_fusion.1), channel_id=1, source_target_pairs={{0,2},{4,0},{8,4},{12,8},{14,12},{10,14},{6,10},{2,6},{1,3},{5,1},... | collective-permute-start | bytes 2752520 | tf_op jit(solution)/shard_map/sums_0_1_left/ppermute | solution.py:270
  (5 other events, 8.8 us)

commit v5 on v4

--- a/solution.py
+++ b/solution.py
@@ -316,40 +316,44 @@
         own, in_sib, sizes[:cut].reshape(raw[1].shape), out_sib, sizes[cut:].reshape(raw[3].shape)
     )
     hold(every(far - 1), own)
-    for c in chunks:
-        gather(c, far)
-        expert((c, far - 1), (c, 1 - far))
-        hold([(c, "top"), (c, "bottom")], done[c][far - 1])
-
-    right, left = [None] * CHUNKS, [None] * CHUNKS
-    empty = jnp.zeros((mid, width), jnp.bfloat16)
-    for c in chunks:
-        expert((c, "top"), (c, "bottom"))
-        right[c] = shift(done[c]["top"], 1, f"sums_{c}_{far}")
-        left[c] = shift(done[c]["bottom"], -1, f"sums_{c}_{far}")
-    for c in chunks:
-        right[c] = jnp.concatenate([right[c], empty], axis=0)
-        left[c] = jnp.concatenate([empty, left[c]], axis=0)
-    for s in range(far - 1, 0, -1):
-        for c in chunks:
-            keys = [(c, s - 1), (c, 1 - s)] if s > 1 else []
-            if s == 2:
-                keys.append((c, 0))
-            if keys:
-                hold(keys, right[c], left[c])
-            right[c] = shift(add(done[c][s], right[c]), 1, f"sums_{c}_{s}")
-            left[c] = shift(add(done[c][-s], left[c]), -1, f"sums_{c}_{s}")
-            if keys:
-                expert(*keys)
-    mixed = [
-        (
-            done[c][0].astype(jnp.float32)
-            + right[c].astype(jnp.float32)
-            + left[c].astype(jnp.float32)
-        ).astype(jnp.bfloat16)
-        for c in chunks
-    ]
-    return jnp.concatenate(mixed, axis=0) if CHUNKS > 1 else mixed[0]
+    gather(0, far)
+    expert((0, far - 1), (0, 1 - far))
+    hold([(0, "top"), (0, "bottom")], done[0][far - 1])
+    expert((0, "top"), (0, "bottom"))
+
+    part = done[0]
+    right_low = shift(part[far - 1][mid:], 1, f"sums_1_{far - 1}")
+    left_top = shift(part[1 - far][:mid], -1, f"sums_1_{far - 1}")
+    right_top = shift(part["top"], 1, f"sums_0_{far}")
+    left_low = shift(part["bottom"], -1, f"sums_0_{far}")
+    before = part["top"]
+    for s in range(far - 1, 1, -1):
+        keys = [(0, s - 1), (0, 1 - s)] + ([(0, 0)] if s == 2 else [])
+        hold(keys, before)
+        expert(*keys)
+        before = right_top
+        right = jnp.concatenate(
+            [add(part[s][:mid], right_top), add(part[s - 1][mid:], right_low)], axis=0
+        )
+        left = jnp.concatenate(
+            [add(part[1 - s][:mid], left_top), add(part[-s][mid:], left_low)], axis=0
+        )
+        right, left = shift(right, 1, f"sums_0_{s}"), shift(left, -1, f"sums_0_{s}")
+        right_top, right_low = right[:mid], right[mid:]
+        left_top, left_low = left[:mid], left[mid:]
+    right_top = shift(add(part[1][:mid], right_top), 1, "sums_0_1")
+    left_low = shift(add(part[-1][mid:], left_low), -1, "sums_0_1")
+
+    def three(*terms):
+        return sum(t.astype(jnp.float32) for t in terms).astype(jnp.bfloat16)
+
+    return jnp.concatenate(
+        [
+            three(part[0][:mid], right_top, left_top),
+            three(part[0][mid:], right_low, left_low),
+        ],
+        axis=0,
+    )
 
 
 def solution(mesh):

time: 158 us -> 156 us (0.987)
  waiting for transfers between devices: 83.5 us -> 79 us
  starting transfers between devices: 18.4 us -> 20.3 us
    ppermute x16 -> x18, waiting for transfers between devices: 82.3 us -> 77.9 us  [shift(): lax.ppermute(x, 'expert', [(order[i], order[(i + by) % owners]) for i in...]
    ppermute x16 -> x18, starting transfers between devices: 17.8 us -> 19.8 us  [shift(): lax.ppermute(x, 'expert', [(order[i], order[(i + by) % owners]) for i in...]
  transfers between devices with their start and end apart: 19 -> 21, of which waited for: 13 -> 13; matrix products, arithmetic and copies ran while one was open for 1% -> 1% of each run, Pallas kernels for 24% -> 26%
where the time goes in v5:
time: 156 us
  waiting for transfers between devices  79 us (51%)
  Pallas kernels  41.2 us (26%)
  starting transfers between devices  20.3 us (13%)
  local copies, waits for them, and re-layouts  11.9 us (8%)
  other arithmetic  2.72 us (2%)
    ppermute x18, waiting for transfers between devices, shift(): lax.ppermute(x, 'expert', [(order[i], order[(i + by) % owners]) for i in...  77.9 us
    pallas_call x4, Pallas kernels, run_expert(): pl.pallas_call(functools.partial(expert_kernel, sizes, owners), out_shape...  26.3 us
    ppermute x18, starting transfers between devices, shift(): lax.ppermute(x, 'expert', [(order[i], order[(i + by) % owners]) for i in...  19.8 us
    unnamed x21, local copies, waits for them, and re-layouts  11.4 us
    pallas_call x1, Pallas kernels, keep(): pl.pallas_call(keep_kernel, out_shape=[pltpu.VMEM(own.shape, own.dtype)]...  8.52 us
    pallas_call x1, Pallas kernels, dequantize(): pl.pallas_call(dequantize_kernel, grid=(tiles, 3), out_shape=jax.ShapeDty...  3.99 us
  transfers between devices with their start and end apart: 21, of which 13 were waited for; matrix products, arithmetic and copies ran while one was open for 1% of the time, Pallas kernels for 26%

profile of v5, /device:TPU:0, one launch (start us, length us, event | category | flops | bytes accessed | tf_op | source)
XLA Modules:
  0.0 156.1 jit_solution(2316747323349920334)
XLA Ops:
  1.2 2.4 %route.1.refs_2_ = bf16[128,3712]{1,0:T(8,128)(2,1)} custom-call(s32[1]{0:T(128)S(6)} %copy.12.hot_ref, s32[4,128]{1,0:T(4,128)} %bitcast.13, f32[4,128]{1,0:T(4,128)} %bitcast.14, bf16[128,3584]{1,0:T(8,128)(2,1)} %tokens_ref.1), custom_call_target="tpu_custom_call" | custom-call | tf_op jit(solution)/shard_map/route/pallas_call | solution.py:114
  3.6 3.0 %collective-permute-start.4 = (bf16[128,3712]{1,0:T(8,128)(2,1)}, bf16[128,3712]{1,0:T(8,128)(2,1)S(1)}, u32[]{:S(2)}, u32[]{:S(2)}) collective-permute-start(bf16[128,3712]{1,0:T(8,128)(2,1)} %route.1.refs_2_), channel_id=1, source_target_pairs={{0,4},{4,8},{8,12},{12,14},{14,10},{10,6},{6,2},{2,0},{1,5},{5,9},... | collective-permute-start | bytes 2850824 | tf_op jit(solution)/shard_map/tokens_0_1_right/ppermute | solution.py:270
  6.7 3.1 %copy-done.1 = bf16[1,2,3584,512]{3,2,1,0:T(8,128)(2,1)S(1)} copy-done((bf16[1,2,3584,512]{3,2,1,0:T(8,128)(2,1)S(1)}, bf16[1,2,3584,512]{3,2,1,0:T(8,128)(2,1)}, u32[]{:S(2)}) %copy-start.1) | copy-done | bytes 7340056
  9.8 2.0 %copy-done.2 = bf16[1,512,3584]{2,1,0:T(8,128)(2,1)S(1)} copy-done((bf16[1,512,3584]{2,1,0:T(8,128)(2,1)S(1)}, bf16[1,512,3584]{2,1,0:T(8,128)(2,1)}, u32[]{:S(2)}) %copy-start.2) | copy-done | bytes 3670040
  11.8 4.0 %dequantize.1.own_from = bf16[2,5376,512]{2,1,0:T(8,128)(2,1)S(1)} custom-call(f32[2,28,4]{2,1,0:T(8,128)S(1)} %bitcast.11, f32[4,28]{1,0:T(4,128)S(1)} %bitcast.12, bf16[2,3584,512]{2,1,0:T(8,128)(2,1)S(1)} %bitcast.8, bf16[512,3584]{1,0:T(8,128)(2,1)S(1)} %bitcast.10), custom_call_target="tpu_custom_call" | custom-call | flops 11010048 | bytes 22020096 | tf_op jit(solution)/shard_map/dequantize/pallas_call | solution.py:66
  15.8 4.2 %copy-done = bf16[2,5376,512]{2,1,0:T(8,128)(2,1)} copy-done((bf16[2,5376,512]{2,1,0:T(8,128)(2,1)}, bf16[2,5376,512]{2,1,0:T(8,128)(2,1)S(1)}, u32[]{:S(2)}) %copy-start) | copy-done | bytes 11010072
  20.0 8.0 %collective-permute-done.4.refs_1_ = bf16[128,3712]{1,0:T(8,128)(2,1)S(1)} collective-permute-done((bf16[128,3712]{1,0:T(8,128)(2,1)}, bf16[128,3712]{1,0:T(8,128)(2,1)S(1)}, u32[]{:S(2)}, u32[]{:S(2)}) %collective-permute-start.4) | collective-permute-done | bytes 950304 | tf_op jit(solution)/shard_map/tokens_0_1_right/ppermute | solution.py:270
  28.0 1.8 %collective-permute-start.5 = (bf16[128,3712]{1,0:T(8,128)(2,1)S(1)}, bf16[128,3712]{1,0:T(8,128)(2,1)S(1)}, u32[]{:S(2)}, u32[]{:S(2)}) collective-permute-start(bf16[128,3712]{1,0:T(8,128)(2,1)S(1)} %collective-permute-done.4.refs_1_), channel_id=1, source_target_pairs={{0,4},{4,8},{8,12},{12,14},{14,10},{10,6},{6,2},{2,0},{1,5},{5,9},... | collective-permute-start | bytes 2850824 | tf_op jit(solution)/shard_map/tokens_0_2_right/ppermute | solution.py:270
  32.0 18.5 %collective-permute-done.5.refs_1_ = bf16[128,3712]{1,0:T(8,128)(2,1)S(1)} collective-permute-done((bf16[128,3712]{1,0:T(8,128)(2,1)S(1)}, bf16[128,3712]{1,0:T(8,128)(2,1)S(1)}, u32[]{:S(2)}, u32[]{:S(2)}) %collective-permute-start.5) | collective-permute-done | bytes 950304 | tf_op jit(solution)/shard_map/tokens_0_2_right/ppermute | solution.py:270
  50.6 1.5 collective-permute-start.6
  55.0 8.5 %keep.1 = (bf16[2,5376,512]{2,1,0:T(8,128)(2,1)S(1)}, bf16[2,5376,512]{2,1,0:T(8,128)(2,1)S(1)}) custom-call(f32[2,28,4]{2,1,0:T(8,128)S(1)} %reshape.26.in_scale, f32[4,28]{1,0:T(4,128)S(1)} %reshape.27.out_scale, bf16[2,5376,512]{2,1,0:T(8,128)(2,1)} %copy-done, bf16[2,3584,512]{2,1,0:T(8,128)(2,1)} %collective-permute-done.1.in_raw, ...), custom_call_target="tpu_custom_call" | custom-call | tf_op jit(solution)/shard_map/keep/pallas_call | solution.py:214
  63.6 8.7 %collective-permute-done.6.refs_1_ = bf16[128,3712]{1,0:T(8,128)(2,1)S(1)} collective-permute-done((bf16[128,3712]{1,0:T(8,128)(2,1)S(1)}, bf16[128,3712]{1,0:T(8,128)(2,1)S(1)}, u32[]{:S(2)}, u32[]{:S(2)}) %collective-permute-start.6) | collective-permute-done | bytes 950304 | tf_op jit(solution)/shard_map/tokens_0_3_right/ppermute | solution.py:270
  72.3 1.9 %collective-permute-done.9.refs_0_ = bf16[128,3712]{1,0:T(8,128)(2,1)S(1)} collective-permute-done((bf16[128,3712]{1,0:T(8,128)(2,1)}, bf16[128,3712]{1,0:T(8,128)(2,1)S(1)}, u32[]{:S(2)}, u32[]{:S(2)}) %collective-permute-start.9) | collective-permute-done | bytes 950304 | tf_op jit(solution)/shard_map/tokens_0_3_left/ppermute | solution.py:270
  75.0 1.3 collective-permute-start.7
  76.3 6.3 %expert.4 = (bf16[128,3584]{1,0:T(8,128)(2,1)S(1)}, bf16[128,3584]{1,0:T(8,128)(2,1)S(1)}) custom-call(s32[1]{0:T(128)} %bitcast.who_ref, bf16[2,5376,512]{2,1,0:T(8,128)(2,1)S(1)} %get-tuple-element.35.own, bf16[2,5376,512]{2,1,0:T(8,128)(2,1)S(1)} %get-tuple-element.36.sib, bf16[128,3712]{1,0:T(8,128)(2,1)S(1)} %collective-permute-done.9.refs_0_, ...), custom_call_target="tpu_custom_call" | custom-call | flops 5637144576 | bytes 22020096 | tf_op jit(solution)/shard_map/expert/pallas_call | solution.py:237
  83.5 1.4 collective-permute-start.12
  84.8 1.8 %collective-permute-done.10.refs_1_ = bf16[64,3712]{1,0:T(8,128)(2,1)S(1)} collective-permute-done((bf16[64,3712]{1,0:T(8,128)(2,1)S(1)}, bf16[64,3712]{1,0:T(8,128)(2,1)S(1)}, u32[]{:S(2)}, u32[]{:S(2)}) %collective-permute-start.10) | collective-permute-done | bytes 475168 | tf_op jit(solution)/shard_map/tokens_0_4_left/ppermute | solution.py:270
  87.2 3.6 %expert.5 = (bf16[64,3584]{1,0:T(8,128)(2,1)S(1)}, bf16[64,3584]{1,0:T(8,128)(2,1)S(1)}) custom-call(s32[1]{0:T(128)} %bitcast.who_ref, bf16[2,5376,512]{2,1,0:T(8,128)(2,1)S(1)} %get-tuple-element.35.own, bf16[2,5376,512]{2,1,0:T(8,128)(2,1)S(1)} %get-tuple-element.36.sib, bf16[64,3712]{1,0:T(8,128)(2,1)S(1)} %collective-permute-done.7.refs_0_, ...), custom_call_target="tpu_custom_call" | custom-call | flops 2818572288 | bytes 22020096 | tf_op jit(solution)/shard_map/expert/pallas_call | solution.py:237
  92.9 7.5 %expert.7 = (bf16[128,3584]{1,0:T(8,128)(2,1)S(1)}, bf16[128,3584]{1,0:T(8,128)(2,1)S(1)}) custom-call(s32[1]{0:T(128)} %bitcast.who_ref, bf16[2,5376,512]{2,1,0:T(8,128)(2,1)S(1)} %get-tuple-element.35.own, bf16[2,5376,512]{2,1,0:T(8,128)(2,1)S(1)} %get-tuple-element.36.sib, bf16[128,3712]{1,0:T(8,128)(2,1)} %collective-permute-done.8.refs_0_, ...), custom_call_target="tpu_custom_call" | custom-call | flops 5637144576 | bytes 22020096 | tf_op jit(solution)/shard_map/expert/pallas_call | solution.py:237
  100.6 3.3 %collective-permute-done.17 = bf16[64,3584]{1,0:T(8,128)(2,1)S(1)} collective-permute-done((bf16[64,3584]{1,0:T(8,128)(2,1)S(1)}, bf16[64,3584]{1,0:T(8,128)(2,1)S(1)}, u32[]{:S(2)}, u32[]{:S(2)}) %collective-permute-start.17) | collective-permute-done | bytes 458784 | tf_op jit(solution)/shard_map/sums_0_4_left/ppermute | solution.py:270
  106.4 9.0 %expert.6 = (bf16[128,3584]{1,0:T(8,128)(2,1)S(1)}, bf16[128,3584]{1,0:T(8,128)(2,1)S(1)}, bf16[128,3584]{1,0:T(8,128)(2,1)S(1)}) custom-call(s32[1]{0:T(128)} %bitcast.who_ref, bf16[2,5376,512]{2,1,0:T(8,128)(2,1)S(1)} %get-tuple-element.35.own, bf16[2,5376,512]{2,1,0:T(8,128)(2,1)S(1)} %get-tuple-element.36.sib, bf16[128,3712]{1,0:T(8,128)(2,1)S(1)} %copy-done.8, ...), custom_call_target="tpu_custom_call" | custom-call | flops 8455716864 | bytes 22020096 | tf_op jit(solution)/shard_map/expert/pallas_call | solution.py:237
  115.4 8.9 %collective-permute-done.18 = bf16[128,3584]{1,0:T(8,128)(2,1)S(1)} collective-permute-done((bf16[128,3584]{1,0:T(8,128)(2,1)S(1)}, bf16[128,3584]{1,0:T(8,128)(2,1)S(1)}, u32[]{:S(2)}, u32[]{:S(2)}) %collective-permute-start.18) | collective-permute-done | bytes 917536 | tf_op jit(solution)/shard_map/sums_0_3_left/ppermute | solution.py:270
  127.0 18.0 %collective-permute-done.19 = bf16[128,3584]{1,0:T(8,128)(2,1)S(1)} collective-permute-done((bf16[128,3584]{1,0:T(8,128)(2,1)S(1)}, bf16[128,3584]{1,0:T(8,128)(2,1)S(1)}, u32[]{:S(2)}, u32[]{:S(2)}) %collective-permute-start.19) | collective-permute-done | bytes 917536 | tf_op jit(solution)/shard_map/sums_0_2_left/ppermute | solution.py:270
  147.3 6.3 %collective-permute-done.20 = bf16[64,3584]{1,0:T(8,128)(2,1)S(1)} collective-permute-done((bf16[64,3584]{1,0:T(8,128)(2,1)S(1)}, bf16[64,3584]{1,0:T(8,128)(2,1)S(1)}, u32[]{:S(2)}, u32[]{:S(2)}) %collective-permute-start.20) | collective-permute-done | bytes 458784 | tf_op jit(solution)/shard_map/sums_0_1_left/ppermute | solution.py:270
  (71 shorter events, 20.3 us)
Async XLA Ops:
  0.0 6.6 %copy-start.9 = (f32[1,2,28,4]{2,3,1,0:T(4,128)S(1)}, f32[1,2,28,4]{2,3,1,0:T(4,128)}, u32[]{:S(2)}) copy-start(f32[1,2,28,4]{2,3,1,0:T(4,128)} %param.13) | copy-start | bytes 2692
  0.0 6.7 %copy-start.4 = (f32[1,4,28]{2,1,0:T(4,128)S(1)}, f32[1,4,28]{2,1,0:T(4,128)}, u32[]{:S(2)}) copy-start(f32[1,4,28]{2,1,0:T(4,128)} %param.15) | copy-start | bytes 1348
  0.0 55.0 %collective-permute-start.1 = (bf16[2,3584,512]{2,1,0:T(8,128)(2,1)}, bf16[2,3584,512]{2,1,0:T(8,128)(2,1)}, u32[]{:S(2)}, u32[]{:S(2)}) collective-permute-start(bf16[2,3584,512]{2,1,0:T(8,128)(2,1)} %bitcast.7), channel_id=1, source_target_pairs={{0,1},{1,0},{2,3},{3,2},{4,5},{5,4},{6,7},{7,6},{8,9},{9,8},{10,11... | collective-permute-start | bytes 22020104 | tf_op jit(solution)/shard_map/ppermute | solution.py:305
  0.5 54.6 %collective-permute-start.2 = (bf16[512,3584]{1,0:T(8,128)(2,1)}, bf16[512,3584]{1,0:T(8,128)(2,1)}, u32[]{:S(2)}, u32[]{:S(2)}) collective-permute-start(bf16[512,3584]{1,0:T(8,128)(2,1)} %bitcast.9), channel_id=1, source_target_pairs={{0,1},{1,0},{2,3},{3,2},{4,5},{5,4},{6,7},{7,6},{8,9},{9,8},{10,11... | collective-permute-start | bytes 11010056 | tf_op jit(solution)/shard_map/ppermute | solution.py:305
  3.6 24.4 %collective-permute-start.4 = (bf16[128,3712]{1,0:T(8,128)(2,1)}, bf16[128,3712]{1,0:T(8,128)(2,1)S(1)}, u32[]{:S(2)}, u32[]{:S(2)}) collective-permute-start(bf16[128,3712]{1,0:T(8,128)(2,1)} %route.1.refs_2_), channel_id=1, source_target_pairs={{0,4},{4,8},{8,12},{12,14},{14,10},{10,6},{6,2},{2,0},{1,5},{5,9},... | collective-permute-start | bytes 2850824 | tf_op jit(solution)/shard_map/tokens_0_1_right/ppermute | solution.py:270
  6.6 24.2 %collective-permute-start.3 = (bf16[128,3712]{1,0:T(8,128)(2,1)}, bf16[128,3712]{1,0:T(8,128)(2,1)S(1)}, u32[]{:S(2)}, u32[]{:S(2)}) collective-permute-start(bf16[128,3712]{1,0:T(8,128)(2,1)} %route.1.refs_2_), channel_id=1, source_target_pairs={{0,2},{4,0},{8,4},{12,8},{14,12},{10,14},{6,10},{2,6},{1,3},{5,1},... | collective-permute-start | bytes 2850824 | tf_op jit(solution)/shard_map/tokens_0_1_left/ppermute | solution.py:270
  15.8 4.2 %copy-start = (bf16[2,5376,512]{2,1,0:T(8,128)(2,1)}, bf16[2,5376,512]{2,1,0:T(8,128)(2,1)S(1)}, u32[]{:S(2)}) copy-start(bf16[2,5376,512]{2,1,0:T(8,128)(2,1)S(1)} %dequantize.1.own_from) | copy-start | bytes 33030148
  28.0 22.5 %collective-permute-start.5 = (bf16[128,3712]{1,0:T(8,128)(2,1)S(1)}, bf16[128,3712]{1,0:T(8,128)(2,1)S(1)}, u32[]{:S(2)}, u32[]{:S(2)}) collective-permute-start(bf16[128,3712]{1,0:T(8,128)(2,1)S(1)} %collective-permute-done.4.refs_1_), channel_id=1, source_target_pairs={{0,4},{4,8},{8,12},{12,14},{14,10},{10,6},{6,2},{2,0},{1,5},{5,9},... | collective-permute-start | bytes 2850824 | tf_op jit(solution)/shard_map/tokens_0_2_right/ppermute | solution.py:270
  30.8 22.0 %collective-permute-start.8 = (bf16[128,3712]{1,0:T(8,128)(2,1)S(1)}, bf16[128,3712]{1,0:T(8,128)(2,1)}, u32[]{:S(2)}, u32[]{:S(2)}) collective-permute-start(bf16[128,3712]{1,0:T(8,128)(2,1)S(1)} %collective-permute-done.3.refs_0_), channel_id=1, source_target_pairs={{0,2},{4,0},{8,4},{12,8},{14,12},{10,14},{6,10},{2,6},{1,3},{5,1},... | collective-permute-start | bytes 2850824 | tf_op jit(solution)/shard_map/tokens_0_2_left/ppermute | solution.py:270
  50.6 21.7 %collective-permute-start.6 = (bf16[128,3712]{1,0:T(8,128)(2,1)S(1)}, bf16[128,3712]{1,0:T(8,128)(2,1)S(1)}, u32[]{:S(2)}, u32[]{:S(2)}) collective-permute-start(bf16[128,3712]{1,0:T(8,128)(2,1)S(1)} %collective-permute-done.5.refs_1_), channel_id=1, source_target_pairs={{0,4},{4,8},{8,12},{12,14},{14,10},{10,6},{6,2},{2,0},{1,5},{5,9},... | collective-permute-start | bytes 2850824 | tf_op jit(solution)/shard_map/tokens_0_3_right/ppermute | solution.py:270
  52.8 21.3 %collective-permute-start.9 = (bf16[128,3712]{1,0:T(8,128)(2,1)}, bf16[128,3712]{1,0:T(8,128)(2,1)S(1)}, u32[]{:S(2)}, u32[]{:S(2)}) collective-permute-start(bf16[128,3712]{1,0:T(8,128)(2,1)} %collective-permute-done.8.refs_0_), channel_id=1, source_target_pairs={{0,2},{4,0},{8,4},{12,8},{14,12},{10,14},{6,10},{2,6},{1,3},{5,1},... | collective-permute-start | bytes 2850824 | tf_op jit(solution)/shard_map/tokens_0_3_left/ppermute | solution.py:270
  53.6 1.2 collective-permute-start
  74.2 12.4 %collective-permute-start.10 = (bf16[64,3712]{1,0:T(8,128)(2,1)S(1)}, bf16[64,3712]{1,0:T(8,128)(2,1)S(1)}, u32[]{:S(2)}, u32[]{:S(2)}) collective-permute-start(bf16[64,3712]{1,0:T(8,128)(2,1)S(1)} %slice.97), channel_id=1, source_target_pairs={{0,2},{4,0},{8,4},{12,8},{14,12},{10,14},{6,10},{2,6},{1,3},{5,1},... | collective-permute-start | bytes 1425416 | tf_op jit(solution)/shard_map/tokens_0_4_left/ppermute | solution.py:270
  75.0 12.2 %collective-permute-start.7 = (bf16[64,3712]{1,0:T(8,128)(2,1)S(1)}, bf16[64,3712]{1,0:T(8,128)(2,1)S(1)}, u32[]{:S(2)}, u32[]{:S(2)}) collective-permute-start(bf16[64,3712]{1,0:T(8,128)(2,1)S(1)} %slice.96), channel_id=1, source_target_pairs={{0,4},{4,8},{8,12},{12,14},{14,10},{10,6},{6,2},{2,0},{1,5},{5,9},... | collective-permute-start | bytes 1425416 | tf_op jit(solution)/shard_map/tokens_0_4_right/ppermute | solution.py:270
  82.6 17.7 %collective-permute-start.16 = (bf16[64,3584]{1,0:T(8,128)(2,1)S(1)}, bf16[64,3584]{1,0:T(8,128)(2,1)S(1)}, u32[]{:S(2)}, u32[]{:S(2)}) collective-permute-start(bf16[64,3584]{1,0:T(8,128)(2,1)S(1)} %slice.110), channel_id=1, source_target_pairs={{0,2},{4,0},{8,4},{12,8},{14,12},{10,14},{6,10},{2,6},{1,3},{5,1},... | collective-permute-start | bytes 1376264 | tf_op jit(solution)/shard_map/sums_1_3_left/ppermute | solution.py:270
  83.5 17.0 %collective-permute-start.12 = (bf16[64,3584]{1,0:T(8,128)(2,1)S(1)}, bf16[64,3584]{1,0:T(8,128)(2,1)S(1)}, u32[]{:S(2)}, u32[]{:S(2)}) collective-permute-start(bf16[64,3584]{1,0:T(8,128)(2,1)S(1)} %slice.103), channel_id=1, source_target_pairs={{0,4},{4,8},{8,12},{12,14},{14,10},{10,6},{6,2},{2,0},{1,5},{5,9},... | collective-permute-start | bytes 1376264 | tf_op jit(solution)/shard_map/sums_1_3_right/ppermute | solution.py:270
  90.8 14.3 %collective-permute-start.11 = (bf16[64,3584]{1,0:T(8,128)(2,1)S(1)}, bf16[64,3584]{1,0:T(8,128)(2,1)S(1)}, u32[]{:S(2)}, u32[]{:S(2)}) collective-permute-start(bf16[64,3584]{1,0:T(8,128)(2,1)S(1)} %get-tuple-element.44), channel_id=1, source_target_pairs={{0,4},{4,8},{8,12},{12,14},{14,10},{10,6},{6,2},{2,0},{1,5},{5,9},... | collective-permute-start | bytes 1376264 | tf_op jit(solution)/shard_map/sums_0_4_right/ppermute | solution.py:270
  91.8 12.0 %collective-permute-start.17 = (bf16[64,3584]{1,0:T(8,128)(2,1)S(1)}, bf16[64,3584]{1,0:T(8,128)(2,1)S(1)}, u32[]{:S(2)}, u32[]{:S(2)}) collective-permute-start(bf16[64,3584]{1,0:T(8,128)(2,1)S(1)} %get-tuple-element.56), channel_id=1, source_target_pairs={{0,2},{4,0},{8,4},{12,8},{14,12},{10,14},{6,10},{2,6},{1,3},{5,1},... | collective-permute-start | bytes 1376264 | tf_op jit(solution)/shard_map/sums_0_4_left/ppermute | solution.py:270
  104.1 20.2 %collective-permute-start.18 = (bf16[128,3584]{1,0:T(8,128)(2,1)S(1)}, bf16[128,3584]{1,0:T(8,128)(2,1)S(1)}, u32[]{:S(2)}, u32[]{:S(2)}) collective-permute-start(bf16[128,3584]{1,0:T(8,128)(2,1)S(1)} %pad_maximum_fusion.2), channel_id=1, source_target_pairs={{0,2},{4,0},{8,4},{12,8},{14,12},{10,14},{6,10},{2,6},{1,3},{5,1},... | collective-permute-start | bytes 2752520 | tf_op jit(solution)/shard_map/sums_0_3_left/ppermute | solution.py:270
  105.3 20.3 %collective-permute-start.13 = (bf16[128,3584]{1,0:T(8,128)(2,1)S(1)}, bf16[128,3584]{1,0:T(8,128)(2,1)S(1)}, u32[]{:S(2)}, u32[]{:S(2)}) collective-permute-start(bf16[128,3584]{1,0:T(8,128)(2,1)S(1)} %pad_maximum_fusion), channel_id=1, source_target_pairs={{0,4},{4,8},{8,12},{12,14},{14,10},{10,6},{6,2},{2,0},{1,5},{5,9},... | collective-permute-start | bytes 2752520 | tf_op jit(solution)/shard_map/sums_0_3_right/ppermute | solution.py:270
  124.6 20.4 %collective-permute-start.19 = (bf16[128,3584]{1,0:T(8,128)(2,1)S(1)}, bf16[128,3584]{1,0:T(8,128)(2,1)S(1)}, u32[]{:S(2)}, u32[]{:S(2)}) collective-permute-start(bf16[128,3584]{1,0:T(8,128)(2,1)S(1)} %pad_maximum_fusion.3), channel_id=1, source_target_pairs={{0,2},{4,0},{8,4},{12,8},{14,12},{10,14},{6,10},{2,6},{1,3},{5,1},... | collective-permute-start | bytes 2752520 | tf_op jit(solution)/shard_map/sums_0_2_left/ppermute | solution.py:270
  125.9 20.2 %collective-permute-start.14 = (bf16[128,3584]{1,0:T(8,128)(2,1)S(1)}, bf16[128,3584]{1,0:T(8,128)(2,1)S(1)}, u32[]{:S(2)}, u32[]{:S(2)}) collective-permute-start(bf16[128,3584]{1,0:T(8,128)(2,1)S(1)} %pad_maximum_fusion.1), channel_id=1, source_target_pairs={{0,4},{4,8},{8,12},{12,14},{14,10},{10,6},{6,2},{2,0},{1,5},{5,9},... | collective-permute-start | bytes 2752520 | tf_op jit(solution)/shard_map/sums_0_2_right/ppermute | solution.py:270
  145.1 8.5 %collective-permute-start.20 = (bf16[64,3584]{1,0:T(8,128)(2,1)S(1)}, bf16[64,3584]{1,0:T(8,128)(2,1)S(1)}, u32[]{:S(2)}, u32[]{:S(2)}) collective-permute-start(bf16[64,3584]{1,0:T(8,128)(2,1)S(1)} %add_convert_fusion.1), channel_id=1, source_target_pairs={{0,2},{4,0},{8,4},{12,8},{14,12},{10,14},{6,10},{2,6},{1,3},{5,1},... | collective-permute-start | bytes 1376264 | tf_op jit(solution)/shard_map/sums_0_1_left/ppermute | solution.py:270
  146.2 8.5 %collective-permute-start.15 = (bf16[64,3584]{1,0:T(8,128)(2,1)S(1)}, bf16[64,3584]{1,0:T(8,128)(2,1)S(1)}, u32[]{:S(2)}, u32[]{:S(2)}) collective-permute-start(bf16[64,3584]{1,0:T(8,128)(2,1)S(1)} %add_convert_fusion.7), channel_id=1, source_target_pairs={{0,4},{4,8},{8,12},{12,14},{14,10},{10,6},{6,2},{2,0},{1,5},{5,9},... | collective-permute-start | bytes 1376264 | tf_op jit(solution)/shard_map/sums_0_1_right/ppermute | solution.py:270
  (7 other events, 14.1 us)

commit v6 on v5

--- a/solution.py
+++ b/solution.py
@@ -80,7 +80,7 @@
     )(in_scale, out_scale, in_raw, out_raw)
 
 
-def route_kernel(capacity, owners, hot_ref, ids_ref, combine_ref, tokens_ref, *out_refs):
+def route_kernel(capacity, owners, hot_ref, ids_ref, combine_ref, out_ref):
     picks, rows = ids_ref.shape
     expert = lax.broadcasted_iota(jnp.int32, (owners, rows), 0)
     named = jnp.zeros((owners, rows), jnp.float32)
@@ -101,23 +101,19 @@
         pieces.append(piece)
     pieces.append(jnp.zeros((LANES - 3 * owners, rows), jnp.float32))
     extra = jnp.concatenate(pieces, axis=0).T.astype(jnp.bfloat16)
-    width = tokens_ref.shape[1]
-    size = rows // len(out_refs)
-    for c, out_ref in enumerate(out_refs):
-        out_ref[:, :width] = tokens_ref[c * size : (c + 1) * size, :]
-        out_ref[:, width:] = extra[c * size : (c + 1) * size, :]
-
-
-def route(hot_list, expert_ids, combine, tokens, owners, capacity):
-    rows, width = tokens.shape
+    out_ref[...] = extra
+
+
+def route(hot_list, expert_ids, combine, owners, capacity):
+    rows = expert_ids.shape[0]
     vmem = pl.BlockSpec(memory_space=pltpu.VMEM)
     return pl.pallas_call(
         functools.partial(route_kernel, capacity, owners),
-        out_shape=[jax.ShapeDtypeStruct((rows // CHUNKS, width + LANES), jnp.bfloat16)] * CHUNKS,
-        in_specs=[pl.BlockSpec(memory_space=pltpu.SMEM), vmem, vmem, vmem],
-        out_specs=[vmem] * CHUNKS,
+        out_shape=jax.ShapeDtypeStruct((rows, LANES), jnp.bfloat16),
+        in_specs=[pl.BlockSpec(memory_space=pltpu.SMEM), vmem, vmem],
+        out_specs=vmem,
         name="route",
-    )(hot_list, expert_ids.T, combine.T, tokens)
+    )(hot_list, expert_ids.T, combine.T)
 
 
 def expert_kernel(sizes, owners, who_ref, own, sib, *refs):
@@ -274,7 +270,7 @@
     def add(a, b):
         return (a.astype(jnp.float32) + b.astype(jnp.float32)).astype(jnp.bfloat16)
 
-    have = [{0: x} for x in route(hot_list, expert_ids, combine, tokens, owners, capacity)]
+    have = [{}]
     done = [{} for _ in chunks]
 
     def gather(c, s):
@@ -297,15 +293,22 @@
     def every(*steps):
         return [(c, key) for s in steps for c in chunks for key in ((s, -s) if s else (0,))]
 
-    for c in chunks:
-        gather(c, 1)
+    bare = {0: tokens, -1: shift(tokens, 1, "tokens_0_1"), 1: shift(tokens, -1, "tokens_0_1")}
+    extra = {0: route(hot_list, expert_ids, combine, owners, capacity)}
+    extra[-1] = shift(extra[0], 1, "weights_0_1")
+    extra[1] = shift(extra[0], -1, "weights_0_1")
+    for s in bare:
+        have[0][s] = jnp.concatenate([bare[s], extra[s]], axis=1)
     raw = (in_weight[0], in_scale[0], out_weight[0], out_scale[0])
     sizes = jnp.concatenate([raw[1].reshape(-1), raw[3].reshape(-1)])
-    in_sib, out_sib, sizes = [
-        lax.ppermute(w, "dp", [(i, (i + 1) % halves) for i in range(halves)])
-        for w in (raw[0], raw[2], sizes)
-    ]
-    own = dequantize(*after(raw, have[0][0]))
+
+    def swap(w):
+        return lax.ppermute(w, "dp", [(i, (i + 1) % halves) for i in range(halves)])
+
+    sizes = swap(sizes)
+    in_sib = swap(raw[0])
+    own = dequantize(*after(raw, extra[0]))
+    out_sib = swap(raw[2])
     for s in range(2, far):
         for c in chunks:
             if s == 2:

time: 156 us -> 155 us (level)
  waiting for transfers between devices: 79 us -> 71.4 us
  starting transfers between devices: 20.3 us -> 23.9 us
  other arithmetic: 2.72 us -> 5.11 us
    ppermute x18 -> x20, waiting for transfers between devices: 77.9 us -> 71.4 us  [shift(): lax.ppermute(x, 'expert', [(order[i], order[(i + by) % owners]) for i in...]
    ppermute x18 -> x20, starting transfers between devices: 19.8 us -> 23.2 us  [shift(): lax.ppermute(x, 'expert', [(order[i], order[(i + by) % owners]) for i in...]
    concatenate x0 -> x3, other arithmetic: none -> 2.4 us  [shards(): have[0][s] = jnp.concatenate([bare[s], extra[s]], axis=1)]
    unnamed x21 -> x19, local copies, waits for them, and re-layouts: 11.4 us -> 11.8 us
  transfers between devices with their start and end apart: 21 -> 23, of which waited for: 13 -> 13; matrix products, arithmetic and copies ran while one was open for 1% -> 3% of each run, Pallas kernels for 26% -> 26%
where the time goes in v6:
time: 155 us; the launch traced here: 154 us
  waiting for transfers between devices  71.4 us (46%)
  Pallas kernels  40.6 us (26%)
  starting transfers between devices  23.9 us (15%)
  local copies, waits for them, and re-layouts  12.4 us (8%)
  other arithmetic  5.11 us (3%)
    ppermute x20, waiting for transfers between devices, shift(): lax.ppermute(x, 'expert', [(order[i], order[(i + by) % owners]) for i in...  71.4 us
    pallas_call x4, Pallas kernels, run_expert(): pl.pallas_call(functools.partial(expert_kernel, sizes, owners), out_shape...  26.5 us
    ppermute x20, starting transfers between devices, shift(): lax.ppermute(x, 'expert', [(order[i], order[(i + by) % owners]) for i in...  23.2 us
    unnamed x19, local copies, waits for them, and re-layouts  11.8 us
    pallas_call x1, Pallas kernels, keep(): pl.pallas_call(keep_kernel, out_shape=[pltpu.VMEM(own.shape, own.dtype)]...  8.52 us
    pallas_call x1, Pallas kernels, dequantize(): pl.pallas_call(dequantize_kernel, grid=(tiles, 3), out_shape=jax.ShapeDty...  3.99 us
  transfers between devices with their start and end apart: 23, of which 13 were waited for; matrix products, arithmetic and copies ran while one was open for 3% of the time, Pallas kernels for 26%

profile of v6, /device:TPU:0, one launch (start us, length us, event | category | flops | bytes accessed | tf_op | source)
XLA Modules:
  0.0 154.2 jit_solution(18322618174963524820)
XLA Ops:
  0.5 2.6 %collective-permute-start.5 = (bf16[128,3584]{1,0:T(8,128)(2,1)}, bf16[128,3584]{1,0:T(8,128)(2,1)S(1)}, u32[]{:S(2)}, u32[]{:S(2)}) collective-permute-start(bf16[128,3584]{1,0:T(8,128)(2,1)} %param.8), channel_id=1, source_target_pairs={{0,4},{4,8},{8,12},{12,14},{14,10},{10,6},{6,2},{2,0},{1,5},{5,9},... | collective-permute-start | bytes 2752520 | tf_op jit(solution)/shard_map/tokens_0_1_right/ppermute | solution.py:266
  4.1 1.6 %route.1 = bf16[128,128]{1,0:T(8,128)(2,1)} custom-call(s32[1]{0:T(128)S(6)} %copy.12.hot_ref, s32[4,128]{1,0:T(4,128)} %bitcast.13, f32[4,128]{1,0:T(4,128)} %bitcast.14), custom_call_target="tpu_custom_call" | custom-call | tf_op jit(solution)/shard_map/route/pallas_call | solution.py:110
  5.7 1.8 %collective-permute-start.6 = (bf16[128,128]{1,0:T(8,128)(2,1)}, bf16[128,128]{1,0:T(8,128)(2,1)S(1)}, u32[]{:S(2)}, u32[]{:S(2)}) collective-permute-start(bf16[128,128]{1,0:T(8,128)(2,1)} %route.1), channel_id=1, source_target_pairs={{0,4},{4,8},{8,12},{12,14},{14,10},{10,6},{6,2},{2,0},{1,5},{5,9},... | collective-permute-start | bytes 98312 | tf_op jit(solution)/shard_map/weights_0_1_right/ppermute | solution.py:266
  8.3 3.1 %copy-done.1 = bf16[1,2,3584,512]{3,2,1,0:T(8,128)(2,1)S(1)} copy-done((bf16[1,2,3584,512]{3,2,1,0:T(8,128)(2,1)S(1)}, bf16[1,2,3584,512]{3,2,1,0:T(8,128)(2,1)}, u32[]{:S(2)}) %copy-start.1) | copy-done | bytes 7340056
  11.4 2.0 %copy-done.2 = bf16[1,512,3584]{2,1,0:T(8,128)(2,1)S(1)} copy-done((bf16[1,512,3584]{2,1,0:T(8,128)(2,1)S(1)}, bf16[1,512,3584]{2,1,0:T(8,128)(2,1)}, u32[]{:S(2)}) %copy-start.2) | copy-done | bytes 3670040
  14.1 4.0 %dequantize.1.own_from = bf16[2,5376,512]{2,1,0:T(8,128)(2,1)S(1)} custom-call(f32[2,28,4]{2,1,0:T(8,128)S(1)} %bitcast.11, f32[4,28]{1,0:T(4,128)S(1)} %bitcast.12, bf16[2,3584,512]{2,1,0:T(8,128)(2,1)S(1)} %bitcast.8, bf16[512,3584]{1,0:T(8,128)(2,1)S(1)} %bitcast.10), custom_call_target="tpu_custom_call" | custom-call | flops 11010048 | bytes 22020096 | tf_op jit(solution)/shard_map/dequantize/pallas_call | solution.py:66
  18.1 4.2 %copy-done = bf16[2,5376,512]{2,1,0:T(8,128)(2,1)} copy-done((bf16[2,5376,512]{2,1,0:T(8,128)(2,1)}, bf16[2,5376,512]{2,1,0:T(8,128)(2,1)S(1)}, u32[]{:S(2)}) %copy-start) | copy-done | bytes 11010072
  22.3 2.6 %collective-permute-done.6 = bf16[128,128]{1,0:T(8,128)(2,1)S(1)} collective-permute-done((bf16[128,128]{1,0:T(8,128)(2,1)}, bf16[128,128]{1,0:T(8,128)(2,1)S(1)}, u32[]{:S(2)}, u32[]{:S(2)}) %collective-permute-start.6) | collective-permute-done | bytes 32800 | tf_op jit(solution)/shard_map/weights_0_1_right/ppermute | solution.py:266
  24.9 1.7 %collective-permute-start.4 = (bf16[128,128]{1,0:T(8,128)(2,1)S(1)}, bf16[128,128]{1,0:T(8,128)(2,1)S(1)}, u32[]{:S(2)}, u32[]{:S(2)}) collective-permute-start(bf16[128,128]{1,0:T(8,128)(2,1)S(1)} %copy-done.8), channel_id=1, source_target_pairs={{0,2},{4,0},{8,4},{12,8},{14,12},{10,14},{6,10},{2,6},{1,3},{5,1},... | collective-permute-start | bytes 98312 | tf_op jit(solution)/shard_map/weights_0_1_left/ppermute | solution.py:266
  27.1 1.8 %collective-permute-done.4 = bf16[128,128]{1,0:T(8,128)(2,1)S(1)} collective-permute-done((bf16[128,128]{1,0:T(8,128)(2,1)S(1)}, bf16[128,128]{1,0:T(8,128)(2,1)S(1)}, u32[]{:S(2)}, u32[]{:S(2)}) %collective-permute-start.4) | collective-permute-done | bytes 32800 | tf_op jit(solution)/shard_map/weights_0_1_left/ppermute | solution.py:266
  28.9 1.8 %collective-permute-start.10 = (bf16[128,3712]{1,0:T(8,128)(2,1)S(1)}, bf16[128,3712]{1,0:T(8,128)(2,1)}, u32[]{:S(2)}, u32[]{:S(2)}) collective-permute-start(bf16[128,3712]{1,0:T(8,128)(2,1)S(1)} %pad_maximum_fusion.refs_0_), channel_id=1, source_target_pairs={{0,2},{4,0},{8,4},{12,8},{14,12},{10,14},{6,10},{2,6},{1,3},{5,1},... | collective-permute-start | bytes 2850824 | tf_op jit(solution)/shard_map/tokens_0_2_left/ppermute | solution.py:266
  31.7 17.6 %collective-permute-done.7.refs_1_ = bf16[128,3712]{1,0:T(8,128)(2,1)} collective-permute-done((bf16[128,3712]{1,0:T(8,128)(2,1)S(1)}, bf16[128,3712]{1,0:T(8,128)(2,1)}, u32[]{:S(2)}, u32[]{:S(2)}) %collective-permute-start.7) | collective-permute-done | bytes 950304 | tf_op jit(solution)/shard_map/tokens_0_2_right/ppermute | solution.py:266
  52.6 2.3 %pad_maximum_fusion.2.refs_2_ = bf16[128,3712]{1,0:T(8,128)(2,1)} fusion(bf16[128,128]{1,0:T(8,128)(2,1)S(1)} %copy-done.8, bf16[128,3584]{1,0:T(8,128)(2,1)} %param.8), kind=kLoop, calls=%fused_computation.2 | loop fusion | flops 1900544 | bytes 1900544 | tf_op jit(solution)/shard_map/concatenate | solution.py:301
  55.2 8.5 %keep.1 = (bf16[2,5376,512]{2,1,0:T(8,128)(2,1)S(1)}, bf16[2,5376,512]{2,1,0:T(8,128)(2,1)S(1)}) custom-call(f32[2,28,4]{2,1,0:T(8,128)S(1)} %reshape.26.in_scale, f32[4,28]{1,0:T(4,128)S(1)} %reshape.27.out_scale, bf16[2,5376,512]{2,1,0:T(8,128)(2,1)} %copy-done, bf16[2,3584,512]{2,1,0:T(8,128)(2,1)} %collective-permute-done.1.in_raw, ...), custom_call_target="tpu_custom_call" | custom-call | tf_op jit(solution)/shard_map/keep/pallas_call | solution.py:210
  63.7 7.3 %collective-permute-done.8.refs_1_ = bf16[128,3712]{1,0:T(8,128)(2,1)S(1)} collective-permute-done((bf16[128,3712]{1,0:T(8,128)(2,1)}, bf16[128,3712]{1,0:T(8,128)(2,1)S(1)}, u32[]{:S(2)}, u32[]{:S(2)}) %collective-permute-start.8) | collective-permute-done | bytes 950304 | tf_op jit(solution)/shard_map/tokens_0_3_right/ppermute | solution.py:266
  74.3 6.3 %expert.4 = (bf16[128,3584]{1,0:T(8,128)(2,1)S(1)}, bf16[128,3584]{1,0:T(8,128)(2,1)S(1)}) custom-call(s32[1]{0:T(128)} %bitcast.who_ref, bf16[2,5376,512]{2,1,0:T(8,128)(2,1)S(1)} %get-tuple-element.35.own, bf16[2,5376,512]{2,1,0:T(8,128)(2,1)S(1)} %get-tuple-element.36.sib, bf16[128,3712]{1,0:T(8,128)(2,1)S(1)} %collective-permute-done.11.refs_0_, ...), custom_call_target="tpu_custom_call" | custom-call | flops 5637144576 | bytes 22020096 | tf_op jit(solution)/shard_map/expert/pallas_call | solution.py:233
  82.8 1.8 %collective-permute-done.12.refs_1_ = bf16[64,3712]{1,0:T(8,128)(2,1)S(1)} collective-permute-done((bf16[64,3712]{1,0:T(8,128)(2,1)S(1)}, bf16[64,3712]{1,0:T(8,128)(2,1)S(1)}, u32[]{:S(2)}, u32[]{:S(2)}) %collective-permute-start.12) | collective-permute-done | bytes 475168 | tf_op jit(solution)/shard_map/tokens_0_4_left/ppermute | solution.py:266
  85.0 3.5 %expert.5 = (bf16[64,3584]{1,0:T(8,128)(2,1)S(1)}, bf16[64,3584]{1,0:T(8,128)(2,1)S(1)}) custom-call(s32[1]{0:T(128)} %bitcast.who_ref, bf16[2,5376,512]{2,1,0:T(8,128)(2,1)S(1)} %get-tuple-element.35.own, bf16[2,5376,512]{2,1,0:T(8,128)(2,1)S(1)} %get-tuple-element.36.sib, bf16[64,3712]{1,0:T(8,128)(2,1)S(1)} %collective-permute-done.9.refs_0_, ...), custom_call_target="tpu_custom_call" | custom-call | flops 2818572288 | bytes 22020096 | tf_op jit(solution)/shard_map/expert/pallas_call | solution.py:233
  90.7 7.7 %expert.7 = (bf16[128,3584]{1,0:T(8,128)(2,1)S(1)}, bf16[128,3584]{1,0:T(8,128)(2,1)S(1)}) custom-call(s32[1]{0:T(128)} %bitcast.who_ref, bf16[2,5376,512]{2,1,0:T(8,128)(2,1)S(1)} %get-tuple-element.35.own, bf16[2,5376,512]{2,1,0:T(8,128)(2,1)S(1)} %get-tuple-element.36.sib, bf16[128,3712]{1,0:T(8,128)(2,1)} %collective-permute-done.10.refs_0_, ...), custom_call_target="tpu_custom_call" | custom-call | flops 5637144576 | bytes 22020096 | tf_op jit(solution)/shard_map/expert/pallas_call | solution.py:233
  98.7 3.0 %collective-permute-done.19 = bf16[64,3584]{1,0:T(8,128)(2,1)S(1)} collective-permute-done((bf16[64,3584]{1,0:T(8,128)(2,1)S(1)}, bf16[64,3584]{1,0:T(8,128)(2,1)S(1)}, u32[]{:S(2)}, u32[]{:S(2)}) %collective-permute-start.19) | collective-permute-done | bytes 458784 | tf_op jit(solution)/shard_map/sums_0_4_left/ppermute | solution.py:266
  104.2 9.0 %expert.6 = (bf16[128,3584]{1,0:T(8,128)(2,1)S(1)}, bf16[128,3584]{1,0:T(8,128)(2,1)S(1)}, bf16[128,3584]{1,0:T(8,128)(2,1)S(1)}) custom-call(s32[1]{0:T(128)} %bitcast.who_ref, bf16[2,5376,512]{2,1,0:T(8,128)(2,1)S(1)} %get-tuple-element.35.own, bf16[2,5376,512]{2,1,0:T(8,128)(2,1)S(1)} %get-tuple-element.36.sib, bf16[128,3712]{1,0:T(8,128)(2,1)S(1)} %copy-done.4, ...), custom_call_target="tpu_custom_call" | custom-call | flops 8455716864 | bytes 22020096 | tf_op jit(solution)/shard_map/expert/pallas_call | solution.py:233
  113.2 8.9 %collective-permute-done.20 = bf16[128,3584]{1,0:T(8,128)(2,1)S(1)} collective-permute-done((bf16[128,3584]{1,0:T(8,128)(2,1)S(1)}, bf16[128,3584]{1,0:T(8,128)(2,1)S(1)}, u32[]{:S(2)}, u32[]{:S(2)}) %collective-permute-start.20) | collective-permute-done | bytes 917536 | tf_op jit(solution)/shard_map/sums_0_3_left/ppermute | solution.py:266
  124.8 18.0 %collective-permute-done.21 = bf16[128,3584]{1,0:T(8,128)(2,1)S(1)} collective-permute-done((bf16[128,3584]{1,0:T(8,128)(2,1)S(1)}, bf16[128,3584]{1,0:T(8,128)(2,1)S(1)}, u32[]{:S(2)}, u32[]{:S(2)}) %collective-permute-start.21) | collective-permute-done | bytes 917536 | tf_op jit(solution)/shard_map/sums_0_2_left/ppermute | solution.py:266
  145.1 6.3 %collective-permute-done.22 = bf16[64,3584]{1,0:T(8,128)(2,1)S(1)} collective-permute-done((bf16[64,3584]{1,0:T(8,128)(2,1)S(1)}, bf16[64,3584]{1,0:T(8,128)(2,1)S(1)}, u32[]{:S(2)}, u32[]{:S(2)}) %collective-permute-start.22) | collective-permute-done | bytes 458784 | tf_op jit(solution)/shard_map/sums_0_1_left/ppermute | solution.py:266
  (76 shorter events, 26.1 us)
Async XLA Ops:
  0.0 55.2 %collective-permute-start.1 = (bf16[2,3584,512]{2,1,0:T(8,128)(2,1)}, bf16[2,3584,512]{2,1,0:T(8,128)(2,1)}, u32[]{:S(2)}, u32[]{:S(2)}) collective-permute-start(bf16[2,3584,512]{2,1,0:T(8,128)(2,1)} %bitcast.7), channel_id=1, source_target_pairs={{0,1},{1,0},{2,3},{3,2},{4,5},{5,4},{6,7},{7,6},{8,9},{9,8},{10,11... | collective-permute-start | bytes 22020104 | tf_op jit(solution)/shard_map/ppermute | solution.py:306
  0.5 26.2 %collective-permute-start.5 = (bf16[128,3584]{1,0:T(8,128)(2,1)}, bf16[128,3584]{1,0:T(8,128)(2,1)S(1)}, u32[]{:S(2)}, u32[]{:S(2)}) collective-permute-start(bf16[128,3584]{1,0:T(8,128)(2,1)} %param.8), channel_id=1, source_target_pairs={{0,4},{4,8},{8,12},{12,14},{14,10},{10,6},{6,2},{2,0},{1,5},{5,9},... | collective-permute-start | bytes 2752520 | tf_op jit(solution)/shard_map/tokens_0_1_right/ppermute | solution.py:266
  3.0 52.1 %collective-permute-start.2 = (bf16[512,3584]{1,0:T(8,128)(2,1)}, bf16[512,3584]{1,0:T(8,128)(2,1)}, u32[]{:S(2)}, u32[]{:S(2)}) collective-permute-start(bf16[512,3584]{1,0:T(8,128)(2,1)} %bitcast.9), channel_id=1, source_target_pairs={{0,1},{1,0},{2,3},{3,2},{4,5},{5,4},{6,7},{7,6},{8,9},{9,8},{10,11... | collective-permute-start | bytes 11010056 | tf_op jit(solution)/shard_map/ppermute | solution.py:306
  3.3 25.6 %collective-permute-start.3 = (bf16[128,3584]{1,0:T(8,128)(2,1)}, bf16[128,3584]{1,0:T(8,128)(2,1)S(1)}, u32[]{:S(2)}, u32[]{:S(2)}) collective-permute-start(bf16[128,3584]{1,0:T(8,128)(2,1)} %param.8), channel_id=1, source_target_pairs={{0,2},{4,0},{8,4},{12,8},{14,12},{10,14},{6,10},{2,6},{1,3},{5,1},... | collective-permute-start | bytes 2752520 | tf_op jit(solution)/shard_map/tokens_0_1_left/ppermute | solution.py:266
  5.7 19.2 %collective-permute-start.6 = (bf16[128,128]{1,0:T(8,128)(2,1)}, bf16[128,128]{1,0:T(8,128)(2,1)S(1)}, u32[]{:S(2)}, u32[]{:S(2)}) collective-permute-start(bf16[128,128]{1,0:T(8,128)(2,1)} %route.1), channel_id=1, source_target_pairs={{0,4},{4,8},{8,12},{12,14},{14,10},{10,6},{6,2},{2,0},{1,5},{5,9},... | collective-permute-start | bytes 98312 | tf_op jit(solution)/shard_map/weights_0_1_right/ppermute | solution.py:266
  22.3 30.2 %copy-start.7 = (f32[1,4,28]{2,1,0:T(4,128)S(1)}, f32[1,4,28]{2,1,0:T(4,128)}, u32[]{:S(2)}) copy-start(f32[1,4,28]{2,1,0:T(4,128)} %param.15) | copy-start | bytes 1348
  24.9 3.9 %collective-permute-start.4 = (bf16[128,128]{1,0:T(8,128)(2,1)S(1)}, bf16[128,128]{1,0:T(8,128)(2,1)S(1)}, u32[]{:S(2)}, u32[]{:S(2)}) collective-permute-start(bf16[128,128]{1,0:T(8,128)(2,1)S(1)} %copy-done.8), channel_id=1, source_target_pairs={{0,2},{4,0},{8,4},{12,8},{14,12},{10,14},{6,10},{2,6},{1,3},{5,1},... | collective-permute-start | bytes 98312 | tf_op jit(solution)/shard_map/weights_0_1_left/ppermute | solution.py:266
  26.7 22.6 %collective-permute-start.7 = (bf16[128,3712]{1,0:T(8,128)(2,1)S(1)}, bf16[128,3712]{1,0:T(8,128)(2,1)}, u32[]{:S(2)}, u32[]{:S(2)}) collective-permute-start(bf16[128,3712]{1,0:T(8,128)(2,1)S(1)} %pad_maximum_fusion.1.refs_1_), channel_id=1, source_target_pairs={{0,4},{4,8},{8,12},{12,14},{14,10},{10,6},{6,2},{2,0},{1,5},{5,9},... | collective-permute-start | bytes 2850824 | tf_op jit(solution)/shard_map/tokens_0_2_right/ppermute | solution.py:266
  28.9 21.9 %collective-permute-start.10 = (bf16[128,3712]{1,0:T(8,128)(2,1)S(1)}, bf16[128,3712]{1,0:T(8,128)(2,1)}, u32[]{:S(2)}, u32[]{:S(2)}) collective-permute-start(bf16[128,3712]{1,0:T(8,128)(2,1)S(1)} %pad_maximum_fusion.refs_0_), channel_id=1, source_target_pairs={{0,2},{4,0},{8,4},{12,8},{14,12},{10,14},{6,10},{2,6},{1,3},{5,1},... | collective-permute-start | bytes 2850824 | tf_op jit(solution)/shard_map/tokens_0_2_left/ppermute | solution.py:266
  49.3 21.7 %collective-permute-start.8 = (bf16[128,3712]{1,0:T(8,128)(2,1)}, bf16[128,3712]{1,0:T(8,128)(2,1)S(1)}, u32[]{:S(2)}, u32[]{:S(2)}) collective-permute-start(bf16[128,3712]{1,0:T(8,128)(2,1)} %collective-permute-done.7.refs_1_), channel_id=1, source_target_pairs={{0,4},{4,8},{8,12},{12,14},{14,10},{10,6},{6,2},{2,0},{1,5},{5,9},... | collective-permute-start | bytes 2850824 | tf_op jit(solution)/shard_map/tokens_0_3_right/ppermute | solution.py:266
  50.8 21.3 %collective-permute-start.11 = (bf16[128,3712]{1,0:T(8,128)(2,1)}, bf16[128,3712]{1,0:T(8,128)(2,1)S(1)}, u32[]{:S(2)}, u32[]{:S(2)}) collective-permute-start(bf16[128,3712]{1,0:T(8,128)(2,1)} %collective-permute-done.10.refs_0_), channel_id=1, source_target_pairs={{0,2},{4,0},{8,4},{12,8},{14,12},{10,14},{6,10},{2,6},{1,3},{5,1},... | collective-permute-start | bytes 2850824 | tf_op jit(solution)/shard_map/tokens_0_3_left/ppermute | solution.py:266
  52.6 2.3 %collective-permute-start = (f32[336]{0:T(512)S(1)}, f32[336]{0:T(512)S(1)}, u32[]{:S(2)}, u32[]{:S(2)}) collective-permute-start(f32[336]{0:T(512)S(1)} %pad_maximum_fusion.8), channel_id=1, source_target_pairs={{0,1},{1,0},{2,3},{3,2},{4,5},{5,4},{6,7},{7,6},{8,9},{9,8},{10,11... | collective-permute-start | bytes 4040 | tf_op jit(solution)/shard_map/ppermute | solution.py:306
  72.2 12.4 %collective-permute-start.12 = (bf16[64,3712]{1,0:T(8,128)(2,1)S(1)}, bf16[64,3712]{1,0:T(8,128)(2,1)S(1)}, u32[]{:S(2)}, u32[]{:S(2)}) collective-permute-start(bf16[64,3712]{1,0:T(8,128)(2,1)S(1)} %slice.97), channel_id=1, source_target_pairs={{0,2},{4,0},{8,4},{12,8},{14,12},{10,14},{6,10},{2,6},{1,3},{5,1},... | collective-permute-start | bytes 1425416 | tf_op jit(solution)/shard_map/tokens_0_4_left/ppermute | solution.py:266
  73.5 11.5 %collective-permute-start.9 = (bf16[64,3712]{1,0:T(8,128)(2,1)S(1)}, bf16[64,3712]{1,0:T(8,128)(2,1)S(1)}, u32[]{:S(2)}, u32[]{:S(2)}) collective-permute-start(bf16[64,3712]{1,0:T(8,128)(2,1)S(1)} %slice.96), channel_id=1, source_target_pairs={{0,4},{4,8},{8,12},{12,14},{14,10},{10,6},{6,2},{2,0},{1,5},{5,9},... | collective-permute-start | bytes 1425416 | tf_op jit(solution)/shard_map/tokens_0_4_right/ppermute | solution.py:266
  80.6 17.8 %collective-permute-start.18 = (bf16[64,3584]{1,0:T(8,128)(2,1)S(1)}, bf16[64,3584]{1,0:T(8,128)(2,1)S(1)}, u32[]{:S(2)}, u32[]{:S(2)}) collective-permute-start(bf16[64,3584]{1,0:T(8,128)(2,1)S(1)} %slice.110), channel_id=1, source_target_pairs={{0,2},{4,0},{8,4},{12,8},{14,12},{10,14},{6,10},{2,6},{1,3},{5,1},... | collective-permute-start | bytes 1376264 | tf_op jit(solution)/shard_map/sums_1_3_left/ppermute | solution.py:266
  82.0 16.5 %collective-permute-start.14 = (bf16[64,3584]{1,0:T(8,128)(2,1)S(1)}, bf16[64,3584]{1,0:T(8,128)(2,1)S(1)}, u32[]{:S(2)}, u32[]{:S(2)}) collective-permute-start(bf16[64,3584]{1,0:T(8,128)(2,1)S(1)} %slice.103), channel_id=1, source_target_pairs={{0,4},{4,8},{8,12},{12,14},{14,10},{10,6},{6,2},{2,0},{1,5},{5,9},... | collective-permute-start | bytes 1376264 | tf_op jit(solution)/shard_map/sums_1_3_right/ppermute | solution.py:266
  88.6 14.7 %collective-permute-start.13 = (bf16[64,3584]{1,0:T(8,128)(2,1)S(1)}, bf16[64,3584]{1,0:T(8,128)(2,1)S(1)}, u32[]{:S(2)}, u32[]{:S(2)}) collective-permute-start(bf16[64,3584]{1,0:T(8,128)(2,1)S(1)} %get-tuple-element.44), channel_id=1, source_target_pairs={{0,4},{4,8},{8,12},{12,14},{14,10},{10,6},{6,2},{2,0},{1,5},{5,9},... | collective-permute-start | bytes 1376264 | tf_op jit(solution)/shard_map/sums_0_4_right/ppermute | solution.py:266
  89.8 11.9 %collective-permute-start.19 = (bf16[64,3584]{1,0:T(8,128)(2,1)S(1)}, bf16[64,3584]{1,0:T(8,128)(2,1)S(1)}, u32[]{:S(2)}, u32[]{:S(2)}) collective-permute-start(bf16[64,3584]{1,0:T(8,128)(2,1)S(1)} %get-tuple-element.56), channel_id=1, source_target_pairs={{0,2},{4,0},{8,4},{12,8},{14,12},{10,14},{6,10},{2,6},{1,3},{5,1},... | collective-permute-start | bytes 1376264 | tf_op jit(solution)/shard_map/sums_0_4_left/ppermute | solution.py:266
  101.9 20.2 %collective-permute-start.20 = (bf16[128,3584]{1,0:T(8,128)(2,1)S(1)}, bf16[128,3584]{1,0:T(8,128)(2,1)S(1)}, u32[]{:S(2)}, u32[]{:S(2)}) collective-permute-start(bf16[128,3584]{1,0:T(8,128)(2,1)S(1)} %pad_maximum_fusion.5), channel_id=1, source_target_pairs={{0,2},{4,0},{8,4},{12,8},{14,12},{10,14},{6,10},{2,6},{1,3},{5,1},... | collective-permute-start | bytes 2752520 | tf_op jit(solution)/shard_map/sums_0_3_left/ppermute | solution.py:266
  103.4 20.3 %collective-permute-start.15 = (bf16[128,3584]{1,0:T(8,128)(2,1)S(1)}, bf16[128,3584]{1,0:T(8,128)(2,1)S(1)}, u32[]{:S(2)}, u32[]{:S(2)}) collective-permute-start(bf16[128,3584]{1,0:T(8,128)(2,1)S(1)} %pad_maximum_fusion.3), channel_id=1, source_target_pairs={{0,4},{4,8},{8,12},{12,14},{14,10},{10,6},{6,2},{2,0},{1,5},{5,9},... | collective-permute-start | bytes 2752520 | tf_op jit(solution)/shard_map/sums_0_3_right/ppermute | solution.py:266
  122.4 20.4 %collective-permute-start.21 = (bf16[128,3584]{1,0:T(8,128)(2,1)S(1)}, bf16[128,3584]{1,0:T(8,128)(2,1)S(1)}, u32[]{:S(2)}, u32[]{:S(2)}) collective-permute-start(bf16[128,3584]{1,0:T(8,128)(2,1)S(1)} %pad_maximum_fusion.6), channel_id=1, source_target_pairs={{0,2},{4,0},{8,4},{12,8},{14,12},{10,14},{6,10},{2,6},{1,3},{5,1},... | collective-permute-start | bytes 2752520 | tf_op jit(solution)/shard_map/sums_0_2_left/ppermute | solution.py:266
  124.0 20.2 %collective-permute-start.16 = (bf16[128,3584]{1,0:T(8,128)(2,1)S(1)}, bf16[128,3584]{1,0:T(8,128)(2,1)S(1)}, u32[]{:S(2)}, u32[]{:S(2)}) collective-permute-start(bf16[128,3584]{1,0:T(8,128)(2,1)S(1)} %pad_maximum_fusion.4), channel_id=1, source_target_pairs={{0,4},{4,8},{8,12},{12,14},{14,10},{10,6},{6,2},{2,0},{1,5},{5,9},... | collective-permute-start | bytes 2752520 | tf_op jit(solution)/shard_map/sums_0_2_right/ppermute | solution.py:266
  142.9 8.5 %collective-permute-start.22 = (bf16[64,3584]{1,0:T(8,128)(2,1)S(1)}, bf16[64,3584]{1,0:T(8,128)(2,1)S(1)}, u32[]{:S(2)}, u32[]{:S(2)}) collective-permute-start(bf16[64,3584]{1,0:T(8,128)(2,1)S(1)} %add_convert_fusion.1), channel_id=1, source_target_pairs={{0,2},{4,0},{8,4},{12,8},{14,12},{10,14},{6,10},{2,6},{1,3},{5,1},... | collective-permute-start | bytes 1376264 | tf_op jit(solution)/shard_map/sums_0_1_left/ppermute | solution.py:266
  144.4 8.5 %collective-permute-start.17 = (bf16[64,3584]{1,0:T(8,128)(2,1)S(1)}, bf16[64,3584]{1,0:T(8,128)(2,1)S(1)}, u32[]{:S(2)}, u32[]{:S(2)}) collective-permute-start(bf16[64,3584]{1,0:T(8,128)(2,1)S(1)} %add_convert_fusion.7), channel_id=1, source_target_pairs={{0,4},{4,8},{8,12},{12,14},{14,10},{10,6},{6,2},{2,0},{1,5},{5,9},... | collective-permute-start | bytes 1376264 | tf_op jit(solution)/shard_map/sums_0_1_right/ppermute | solution.py:266
  (8 other events, 26.5 us)

commit v7 on v6

--- a/solution.py
+++ b/solution.py
@@ -311,8 +311,8 @@
     out_sib = swap(raw[2])
     for s in range(2, far):
         for c in chunks:
-            if s == 2:
-                hold([(c, 1), (c, -1)], own)
+            if s == 3:
+                hold([(c, 2), (c, -2)], own)
             gather(c, s)
     cut = raw[1].size
     own, sib = keep(

time: 155 us -> 154 us (level)
  local copies, waits for them, and re-layouts: 12.4 us -> 10.1 us
    unnamed x19 -> x23, local copies, waits for them, and re-layouts: 11.8 us -> 9.56 us
  transfers between devices with their start and end apart: 23 -> 23, of which waited for: 13 -> 13; matrix products, arithmetic and copies ran while one was open for 3% -> 2% of each run, Pallas kernels for 26% -> 27%
where the time goes in v7:
time: 154 us; the launch traced here: 153 us
  waiting for transfers between devices  72.8 us (47%)
  Pallas kernels  40.6 us (26%)
  starting transfers between devices  24.8 us (16%)
  local copies, waits for them, and re-layouts  10.1 us (7%)
  other arithmetic  3.95 us (3%)
    ppermute x20, waiting for transfers between devices, shift(): lax.ppermute(x, 'expert', [(order[i], order[(i + by) % owners]) for i in...  72.8 us
    pallas_call x4, Pallas kernels, run_expert(): pl.pallas_call(functools.partial(expert_kernel, sizes, owners), out_shape...  26.5 us
    ppermute x20, starting transfers between devices, shift(): lax.ppermute(x, 'expert', [(order[i], order[(i + by) % owners]) for i in...  24.1 us
    unnamed x23, local copies, waits for them, and re-layouts  9.56 us
    pallas_call x1, Pallas kernels, keep(): pl.pallas_call(keep_kernel, out_shape=[pltpu.VMEM(own.shape, own.dtype)]...  8.52 us
    pallas_call x1, Pallas kernels, dequantize(): pl.pallas_call(dequantize_kernel, grid=(tiles, 3), out_shape=jax.ShapeDty...  3.99 us
  transfers between devices with their start and end apart: 23, of which 13 were waited for; matrix products, arithmetic and copies ran while one was open for 2% of the time, Pallas kernels for 27%

profile of v7, /device:TPU:0, one launch (start us, length us, event | category | flops | bytes accessed | tf_op | source)
XLA Modules:
  0.0 153.2 jit_solution(988117850628168800)
XLA Ops:
  0.5 2.6 %collective-permute-start.5 = (bf16[128,3584]{1,0:T(8,128)(2,1)}, bf16[128,3584]{1,0:T(8,128)(2,1)S(1)}, u32[]{:S(2)}, u32[]{:S(2)}) collective-permute-start(bf16[128,3584]{1,0:T(8,128)(2,1)} %param.8), channel_id=1, source_target_pairs={{0,4},{4,8},{8,12},{12,14},{14,10},{10,6},{6,2},{2,0},{1,5},{5,9},... | collective-permute-start | bytes 2752520 | tf_op jit(solution)/shard_map/tokens_0_1_right/ppermute | solution.py:266
  4.1 1.6 %route.1 = bf16[128,128]{1,0:T(8,128)(2,1)} custom-call(s32[1]{0:T(128)S(6)} %copy.14.hot_ref, s32[4,128]{1,0:T(4,128)} %bitcast.13, f32[4,128]{1,0:T(4,128)} %bitcast.14), custom_call_target="tpu_custom_call" | custom-call | tf_op jit(solution)/shard_map/route/pallas_call | solution.py:110
  5.7 1.8 %collective-permute-start.6 = (bf16[128,128]{1,0:T(8,128)(2,1)}, bf16[128,128]{1,0:T(8,128)(2,1)S(1)}, u32[]{:S(2)}, u32[]{:S(2)}) collective-permute-start(bf16[128,128]{1,0:T(8,128)(2,1)} %route.1), channel_id=1, source_target_pairs={{0,4},{4,8},{8,12},{12,14},{14,10},{10,6},{6,2},{2,0},{1,5},{5,9},... | collective-permute-start | bytes 98312 | tf_op jit(solution)/shard_map/weights_0_1_right/ppermute | solution.py:266
  7.5 16.9 %collective-permute-done.5 = bf16[128,3584]{1,0:T(8,128)(2,1)S(1)} collective-permute-done((bf16[128,3584]{1,0:T(8,128)(2,1)}, bf16[128,3584]{1,0:T(8,128)(2,1)S(1)}, u32[]{:S(2)}, u32[]{:S(2)}) %collective-permute-start.5) | collective-permute-done | bytes 917536 | tf_op jit(solution)/shard_map/tokens_0_1_right/ppermute | solution.py:266
  24.4 1.9 %collective-permute-start.4 = (bf16[128,128]{1,0:T(8,128)(2,1)}, bf16[128,128]{1,0:T(8,128)(2,1)S(1)}, u32[]{:S(2)}, u32[]{:S(2)}) collective-permute-start(bf16[128,128]{1,0:T(8,128)(2,1)} %route.1), channel_id=1, source_target_pairs={{0,2},{4,0},{8,4},{12,8},{14,12},{10,14},{6,10},{2,6},{1,3},{5,1},... | collective-permute-start | bytes 98312 | tf_op jit(solution)/shard_map/weights_0_1_left/ppermute | solution.py:266
  26.8 1.7 %collective-permute-done.4 = bf16[128,128]{1,0:T(8,128)(2,1)S(1)} collective-permute-done((bf16[128,128]{1,0:T(8,128)(2,1)}, bf16[128,128]{1,0:T(8,128)(2,1)S(1)}, u32[]{:S(2)}, u32[]{:S(2)}) %collective-permute-start.4) | collective-permute-done | bytes 32800 | tf_op jit(solution)/shard_map/weights_0_1_left/ppermute | solution.py:266
  28.5 2.0 %collective-permute-start.10 = (bf16[128,3712]{1,0:T(8,128)(2,1)S(1)}, bf16[128,3712]{1,0:T(8,128)(2,1)}, u32[]{:S(2)}, u32[]{:S(2)}) collective-permute-start(bf16[128,3712]{1,0:T(8,128)(2,1)S(1)} %constant_dynamic-update-slice_fusion.refs_0_), channel_id=1, source_target_pairs={{0,2},{4,0},{8,4},{12,8},{14,12},{10,14},{6,10},{2,6},{1,3},{5,1},... | collective-permute-start | bytes 2850824 | tf_op jit(solution)/shard_map/tokens_0_2_left/ppermute | solution.py:266
  30.6 3.1 %copy-done.1 = bf16[1,2,3584,512]{3,2,1,0:T(8,128)(2,1)S(1)} copy-done((bf16[1,2,3584,512]{3,2,1,0:T(8,128)(2,1)S(1)}, bf16[1,2,3584,512]{3,2,1,0:T(8,128)(2,1)}, u32[]{:S(2)}) %copy-start.1) | copy-done | bytes 7340056
  33.7 2.0 %copy-done.2 = bf16[1,512,3584]{2,1,0:T(8,128)(2,1)S(1)} copy-done((bf16[1,512,3584]{2,1,0:T(8,128)(2,1)S(1)}, bf16[1,512,3584]{2,1,0:T(8,128)(2,1)}, u32[]{:S(2)}) %copy-start.2) | copy-done | bytes 3670040
  35.7 4.0 %dequantize.1.own_from = bf16[2,5376,512]{2,1,0:T(8,128)(2,1)S(1)} custom-call(f32[2,28,4]{2,1,0:T(8,128)S(1)} %bitcast.11, f32[4,28]{1,0:T(4,128)S(1)} %bitcast.12, bf16[2,3584,512]{2,1,0:T(8,128)(2,1)S(1)} %bitcast.8, bf16[512,3584]{1,0:T(8,128)(2,1)S(1)} %bitcast.10), custom_call_target="tpu_custom_call" | custom-call | flops 11010048 | bytes 22020096 | tf_op jit(solution)/shard_map/dequantize/pallas_call | solution.py:66
  39.8 4.2 %copy-done = bf16[2,5376,512]{2,1,0:T(8,128)(2,1)} copy-done((bf16[2,5376,512]{2,1,0:T(8,128)(2,1)}, bf16[2,5376,512]{2,1,0:T(8,128)(2,1)S(1)}, u32[]{:S(2)}) %copy-start) | copy-done | bytes 11010072
  43.9 4.7 %collective-permute-done.7.refs_1_ = bf16[128,3712]{1,0:T(8,128)(2,1)} collective-permute-done((bf16[128,3712]{1,0:T(8,128)(2,1)S(1)}, bf16[128,3712]{1,0:T(8,128)(2,1)}, u32[]{:S(2)}, u32[]{:S(2)}) %collective-permute-start.7) | collective-permute-done | bytes 950304 | tf_op jit(solution)/shard_map/tokens_0_2_right/ppermute | solution.py:266
  53.6 8.5 %keep.1 = (bf16[2,5376,512]{2,1,0:T(8,128)(2,1)S(1)}, bf16[2,5376,512]{2,1,0:T(8,128)(2,1)S(1)}) custom-call(f32[2,28,4]{2,1,0:T(8,128)S(1)} %reshape.26.in_scale, f32[4,28]{1,0:T(4,128)S(1)} %reshape.27.out_scale, bf16[2,5376,512]{2,1,0:T(8,128)(2,1)} %copy-done, bf16[2,3584,512]{2,1,0:T(8,128)(2,1)} %collective-permute-done.1.in_raw, ...), custom_call_target="tpu_custom_call" | custom-call | tf_op jit(solution)/shard_map/keep/pallas_call | solution.py:210
  62.1 7.8 %collective-permute-done.8.refs_1_ = bf16[128,3712]{1,0:T(8,128)(2,1)S(1)} collective-permute-done((bf16[128,3712]{1,0:T(8,128)(2,1)}, bf16[128,3712]{1,0:T(8,128)(2,1)S(1)}, u32[]{:S(2)}, u32[]{:S(2)}) %collective-permute-start.8) | collective-permute-done | bytes 950304 | tf_op jit(solution)/shard_map/tokens_0_3_right/ppermute | solution.py:266
  69.9 1.6 %collective-permute-done.11.refs_0_ = bf16[128,3712]{1,0:T(8,128)(2,1)S(1)} collective-permute-done((bf16[128,3712]{1,0:T(8,128)(2,1)}, bf16[128,3712]{1,0:T(8,128)(2,1)S(1)}, u32[]{:S(2)}, u32[]{:S(2)}) %collective-permute-start.11) | collective-permute-done | bytes 950304 | tf_op jit(solution)/shard_map/tokens_0_3_left/ppermute | solution.py:266
  73.8 6.3 %expert.4 = (bf16[128,3584]{1,0:T(8,128)(2,1)S(1)}, bf16[128,3584]{1,0:T(8,128)(2,1)S(1)}) custom-call(s32[1]{0:T(128)} %bitcast.who_ref, bf16[2,5376,512]{2,1,0:T(8,128)(2,1)S(1)} %get-tuple-element.35.own, bf16[2,5376,512]{2,1,0:T(8,128)(2,1)S(1)} %get-tuple-element.36.sib, bf16[128,3712]{1,0:T(8,128)(2,1)S(1)} %collective-permute-done.11.refs_0_, ...), custom_call_target="tpu_custom_call" | custom-call | flops 5637144576 | bytes 22020096 | tf_op jit(solution)/shard_map/expert/pallas_call | solution.py:233
  82.3 1.8 %collective-permute-done.12.refs_1_ = bf16[64,3712]{1,0:T(8,128)(2,1)S(1)} collective-permute-done((bf16[64,3712]{1,0:T(8,128)(2,1)S(1)}, bf16[64,3712]{1,0:T(8,128)(2,1)S(1)}, u32[]{:S(2)}, u32[]{:S(2)}) %collective-permute-start.12) | collective-permute-done | bytes 475168 | tf_op jit(solution)/shard_map/tokens_0_4_left/ppermute | solution.py:266
  84.4 3.5 %expert.5 = (bf16[64,3584]{1,0:T(8,128)(2,1)S(1)}, bf16[64,3584]{1,0:T(8,128)(2,1)S(1)}) custom-call(s32[1]{0:T(128)} %bitcast.who_ref, bf16[2,5376,512]{2,1,0:T(8,128)(2,1)S(1)} %get-tuple-element.35.own, bf16[2,5376,512]{2,1,0:T(8,128)(2,1)S(1)} %get-tuple-element.36.sib, bf16[64,3712]{1,0:T(8,128)(2,1)S(1)} %collective-permute-done.9.refs_0_, ...), custom_call_target="tpu_custom_call" | custom-call | flops 2818572288 | bytes 22020096 | tf_op jit(solution)/shard_map/expert/pallas_call | solution.py:233
  90.0 7.7 %expert.7 = (bf16[128,3584]{1,0:T(8,128)(2,1)S(1)}, bf16[128,3584]{1,0:T(8,128)(2,1)S(1)}) custom-call(s32[1]{0:T(128)} %bitcast.who_ref, bf16[2,5376,512]{2,1,0:T(8,128)(2,1)S(1)} %get-tuple-element.35.own, bf16[2,5376,512]{2,1,0:T(8,128)(2,1)S(1)} %get-tuple-element.36.sib, bf16[128,3712]{1,0:T(8,128)(2,1)} %collective-permute-done.10.refs_0_, ...), custom_call_target="tpu_custom_call" | custom-call | flops 5637144576 | bytes 22020096 | tf_op jit(solution)/shard_map/expert/pallas_call | solution.py:233
  98.0 3.1 %collective-permute-done.19 = bf16[64,3584]{1,0:T(8,128)(2,1)S(1)} collective-permute-done((bf16[64,3584]{1,0:T(8,128)(2,1)S(1)}, bf16[64,3584]{1,0:T(8,128)(2,1)S(1)}, u32[]{:S(2)}, u32[]{:S(2)}) %collective-permute-start.19) | collective-permute-done | bytes 458784 | tf_op jit(solution)/shard_map/sums_0_4_left/ppermute | solution.py:266
  103.7 9.0 %expert.6 = (bf16[128,3584]{1,0:T(8,128)(2,1)S(1)}, bf16[128,3584]{1,0:T(8,128)(2,1)S(1)}, bf16[128,3584]{1,0:T(8,128)(2,1)S(1)}) custom-call(s32[1]{0:T(128)} %bitcast.who_ref, bf16[2,5376,512]{2,1,0:T(8,128)(2,1)S(1)} %get-tuple-element.35.own, bf16[2,5376,512]{2,1,0:T(8,128)(2,1)S(1)} %get-tuple-element.36.sib, bf16[128,3712]{1,0:T(8,128)(2,1)S(1)} %copy-done.6, ...), custom_call_target="tpu_custom_call" | custom-call | flops 8455716864 | bytes 22020096 | tf_op jit(solution)/shard_map/expert/pallas_call | solution.py:233
  112.7 8.9 %collective-permute-done.20 = bf16[128,3584]{1,0:T(8,128)(2,1)S(1)} collective-permute-done((bf16[128,3584]{1,0:T(8,128)(2,1)S(1)}, bf16[128,3584]{1,0:T(8,128)(2,1)S(1)}, u32[]{:S(2)}, u32[]{:S(2)}) %collective-permute-start.20) | collective-permute-done | bytes 917536 | tf_op jit(solution)/shard_map/sums_0_3_left/ppermute | solution.py:266
  124.3 18.0 %collective-permute-done.21 = bf16[128,3584]{1,0:T(8,128)(2,1)S(1)} collective-permute-done((bf16[128,3584]{1,0:T(8,128)(2,1)S(1)}, bf16[128,3584]{1,0:T(8,128)(2,1)S(1)}, u32[]{:S(2)}, u32[]{:S(2)}) %collective-permute-start.21) | collective-permute-done | bytes 917536 | tf_op jit(solution)/shard_map/sums_0_2_left/ppermute | solution.py:266
  144.6 6.3 %collective-permute-done.22 = bf16[64,3584]{1,0:T(8,128)(2,1)S(1)} collective-permute-done((bf16[64,3584]{1,0:T(8,128)(2,1)S(1)}, bf16[64,3584]{1,0:T(8,128)(2,1)S(1)}, u32[]{:S(2)}, u32[]{:S(2)}) %collective-permute-start.22) | collective-permute-done | bytes 458784 | tf_op jit(solution)/shard_map/sums_0_1_left/ppermute | solution.py:266
  (80 shorter events, 23.4 us)
Async XLA Ops:
  0.0 53.6 %collective-permute-start.1 = (bf16[2,3584,512]{2,1,0:T(8,128)(2,1)}, bf16[2,3584,512]{2,1,0:T(8,128)(2,1)}, u32[]{:S(2)}, u32[]{:S(2)}) collective-permute-start(bf16[2,3584,512]{2,1,0:T(8,128)(2,1)} %bitcast.7), channel_id=1, source_target_pairs={{0,1},{1,0},{2,3},{3,2},{4,5},{5,4},{6,7},{7,6},{8,9},{9,8},{10,11... | collective-permute-start | bytes 22020104 | tf_op jit(solution)/shard_map/ppermute | solution.py:306
  0.5 23.9 %collective-permute-start.5 = (bf16[128,3584]{1,0:T(8,128)(2,1)}, bf16[128,3584]{1,0:T(8,128)(2,1)S(1)}, u32[]{:S(2)}, u32[]{:S(2)}) collective-permute-start(bf16[128,3584]{1,0:T(8,128)(2,1)} %param.8), channel_id=1, source_target_pairs={{0,4},{4,8},{8,12},{12,14},{14,10},{10,6},{6,2},{2,0},{1,5},{5,9},... | collective-permute-start | bytes 2752520 | tf_op jit(solution)/shard_map/tokens_0_1_right/ppermute | solution.py:266
  3.0 50.6 %collective-permute-start.2 = (bf16[512,3584]{1,0:T(8,128)(2,1)}, bf16[512,3584]{1,0:T(8,128)(2,1)}, u32[]{:S(2)}, u32[]{:S(2)}) collective-permute-start(bf16[512,3584]{1,0:T(8,128)(2,1)} %bitcast.9), channel_id=1, source_target_pairs={{0,1},{1,0},{2,3},{3,2},{4,5},{5,4},{6,7},{7,6},{8,9},{9,8},{10,11... | collective-permute-start | bytes 11010056 | tf_op jit(solution)/shard_map/ppermute | solution.py:306
  3.3 23.5 %collective-permute-start.3 = (bf16[128,3584]{1,0:T(8,128)(2,1)}, bf16[128,3584]{1,0:T(8,128)(2,1)S(1)}, u32[]{:S(2)}, u32[]{:S(2)}) collective-permute-start(bf16[128,3584]{1,0:T(8,128)(2,1)} %param.8), channel_id=1, source_target_pairs={{0,2},{4,0},{8,4},{12,8},{14,12},{10,14},{6,10},{2,6},{1,3},{5,1},... | collective-permute-start | bytes 2752520 | tf_op jit(solution)/shard_map/tokens_0_1_left/ppermute | solution.py:266
  5.7 24.9 %copy-start.7 = (f32[1,4,28]{2,1,0:T(4,128)S(1)}, f32[1,4,28]{2,1,0:T(4,128)}, u32[]{:S(2)}) copy-start(f32[1,4,28]{2,1,0:T(4,128)} %param.15) | copy-start | bytes 1348
  5.7 20.7 %collective-permute-start.6 = (bf16[128,128]{1,0:T(8,128)(2,1)}, bf16[128,128]{1,0:T(8,128)(2,1)S(1)}, u32[]{:S(2)}, u32[]{:S(2)}) collective-permute-start(bf16[128,128]{1,0:T(8,128)(2,1)} %route.1), channel_id=1, source_target_pairs={{0,4},{4,8},{8,12},{12,14},{14,10},{10,6},{6,2},{2,0},{1,5},{5,9},... | collective-permute-start | bytes 98312 | tf_op jit(solution)/shard_map/weights_0_1_right/ppermute | solution.py:266
  24.4 4.1 %collective-permute-start.4 = (bf16[128,128]{1,0:T(8,128)(2,1)}, bf16[128,128]{1,0:T(8,128)(2,1)S(1)}, u32[]{:S(2)}, u32[]{:S(2)}) collective-permute-start(bf16[128,128]{1,0:T(8,128)(2,1)} %route.1), channel_id=1, source_target_pairs={{0,2},{4,0},{8,4},{12,8},{14,12},{10,14},{6,10},{2,6},{1,3},{5,1},... | collective-permute-start | bytes 98312 | tf_op jit(solution)/shard_map/weights_0_1_left/ppermute | solution.py:266
  26.4 22.2 %collective-permute-start.7 = (bf16[128,3712]{1,0:T(8,128)(2,1)S(1)}, bf16[128,3712]{1,0:T(8,128)(2,1)}, u32[]{:S(2)}, u32[]{:S(2)}) collective-permute-start(bf16[128,3712]{1,0:T(8,128)(2,1)S(1)} %constant_dynamic-update-slice_fusion.2.refs_1_), channel_id=1, source_target_pairs={{0,4},{4,8},{8,12},{12,14},{14,10},{10,6},{6,2},{2,0},{1,5},{5,9},... | collective-permute-start | bytes 2850824 | tf_op jit(solution)/shard_map/tokens_0_2_right/ppermute | solution.py:266
  28.5 21.7 %collective-permute-start.10 = (bf16[128,3712]{1,0:T(8,128)(2,1)S(1)}, bf16[128,3712]{1,0:T(8,128)(2,1)}, u32[]{:S(2)}, u32[]{:S(2)}) collective-permute-start(bf16[128,3712]{1,0:T(8,128)(2,1)S(1)} %constant_dynamic-update-slice_fusion.refs_0_), channel_id=1, source_target_pairs={{0,2},{4,0},{8,4},{12,8},{14,12},{10,14},{6,10},{2,6},{1,3},{5,1},... | collective-permute-start | bytes 2850824 | tf_op jit(solution)/shard_map/tokens_0_2_left/ppermute | solution.py:266
  48.6 21.3 %collective-permute-start.8 = (bf16[128,3712]{1,0:T(8,128)(2,1)}, bf16[128,3712]{1,0:T(8,128)(2,1)S(1)}, u32[]{:S(2)}, u32[]{:S(2)}) collective-permute-start(bf16[128,3712]{1,0:T(8,128)(2,1)} %collective-permute-done.7.refs_1_), channel_id=1, source_target_pairs={{0,4},{4,8},{8,12},{12,14},{14,10},{10,6},{6,2},{2,0},{1,5},{5,9},... | collective-permute-start | bytes 2850824 | tf_op jit(solution)/shard_map/tokens_0_3_right/ppermute | solution.py:266
  50.2 21.3 %collective-permute-start.11 = (bf16[128,3712]{1,0:T(8,128)(2,1)}, bf16[128,3712]{1,0:T(8,128)(2,1)S(1)}, u32[]{:S(2)}, u32[]{:S(2)}) collective-permute-start(bf16[128,3712]{1,0:T(8,128)(2,1)} %collective-permute-done.10.refs_0_), channel_id=1, source_target_pairs={{0,2},{4,0},{8,4},{12,8},{14,12},{10,14},{6,10},{2,6},{1,3},{5,1},... | collective-permute-start | bytes 2850824 | tf_op jit(solution)/shard_map/tokens_0_3_left/ppermute | solution.py:266
  52.0 1.3 collective-permute-start
  71.6 12.4 %collective-permute-start.12 = (bf16[64,3712]{1,0:T(8,128)(2,1)S(1)}, bf16[64,3712]{1,0:T(8,128)(2,1)S(1)}, u32[]{:S(2)}, u32[]{:S(2)}) collective-permute-start(bf16[64,3712]{1,0:T(8,128)(2,1)S(1)} %slice.97), channel_id=1, source_target_pairs={{0,2},{4,0},{8,4},{12,8},{14,12},{10,14},{6,10},{2,6},{1,3},{5,1},... | collective-permute-start | bytes 1425416 | tf_op jit(solution)/shard_map/tokens_0_4_left/ppermute | solution.py:266
  73.1 11.3 %collective-permute-start.9 = (bf16[64,3712]{1,0:T(8,128)(2,1)S(1)}, bf16[64,3712]{1,0:T(8,128)(2,1)S(1)}, u32[]{:S(2)}, u32[]{:S(2)}) collective-permute-start(bf16[64,3712]{1,0:T(8,128)(2,1)S(1)} %slice.96), channel_id=1, source_target_pairs={{0,4},{4,8},{8,12},{12,14},{14,10},{10,6},{6,2},{2,0},{1,5},{5,9},... | collective-permute-start | bytes 1425416 | tf_op jit(solution)/shard_map/tokens_0_4_right/ppermute | solution.py:266
  80.1 17.6 %collective-permute-start.18 = (bf16[64,3584]{1,0:T(8,128)(2,1)S(1)}, bf16[64,3584]{1,0:T(8,128)(2,1)S(1)}, u32[]{:S(2)}, u32[]{:S(2)}) collective-permute-start(bf16[64,3584]{1,0:T(8,128)(2,1)S(1)} %slice.110), channel_id=1, source_target_pairs={{0,2},{4,0},{8,4},{12,8},{14,12},{10,14},{6,10},{2,6},{1,3},{5,1},... | collective-permute-start | bytes 1376264 | tf_op jit(solution)/shard_map/sums_1_3_left/ppermute | solution.py:266
  81.6 16.3 %collective-permute-start.14 = (bf16[64,3584]{1,0:T(8,128)(2,1)S(1)}, bf16[64,3584]{1,0:T(8,128)(2,1)S(1)}, u32[]{:S(2)}, u32[]{:S(2)}) collective-permute-start(bf16[64,3584]{1,0:T(8,128)(2,1)S(1)} %slice.103), channel_id=1, source_target_pairs={{0,4},{4,8},{8,12},{12,14},{14,10},{10,6},{6,2},{2,0},{1,5},{5,9},... | collective-permute-start | bytes 1376264 | tf_op jit(solution)/shard_map/sums_1_3_right/ppermute | solution.py:266
  87.9 14.4 %collective-permute-start.13 = (bf16[64,3584]{1,0:T(8,128)(2,1)S(1)}, bf16[64,3584]{1,0:T(8,128)(2,1)S(1)}, u32[]{:S(2)}, u32[]{:S(2)}) collective-permute-start(bf16[64,3584]{1,0:T(8,128)(2,1)S(1)} %get-tuple-element.44), channel_id=1, source_target_pairs={{0,4},{4,8},{8,12},{12,14},{14,10},{10,6},{6,2},{2,0},{1,5},{5,9},... | collective-permute-start | bytes 1376264 | tf_op jit(solution)/shard_map/sums_0_4_right/ppermute | solution.py:266
  89.1 12.0 %collective-permute-start.19 = (bf16[64,3584]{1,0:T(8,128)(2,1)S(1)}, bf16[64,3584]{1,0:T(8,128)(2,1)S(1)}, u32[]{:S(2)}, u32[]{:S(2)}) collective-permute-start(bf16[64,3584]{1,0:T(8,128)(2,1)S(1)} %get-tuple-element.56), channel_id=1, source_target_pairs={{0,2},{4,0},{8,4},{12,8},{14,12},{10,14},{6,10},{2,6},{1,3},{5,1},... | collective-permute-start | bytes 1376264 | tf_op jit(solution)/shard_map/sums_0_4_left/ppermute | solution.py:266
  101.3 20.2 %collective-permute-start.20 = (bf16[128,3584]{1,0:T(8,128)(2,1)S(1)}, bf16[128,3584]{1,0:T(8,128)(2,1)S(1)}, u32[]{:S(2)}, u32[]{:S(2)}) collective-permute-start(bf16[128,3584]{1,0:T(8,128)(2,1)S(1)} %pad_maximum_fusion.3), channel_id=1, source_target_pairs={{0,2},{4,0},{8,4},{12,8},{14,12},{10,14},{6,10},{2,6},{1,3},{5,1},... | collective-permute-start | bytes 2752520 | tf_op jit(solution)/shard_map/sums_0_3_left/ppermute | solution.py:266
  102.5 20.2 %collective-permute-start.15 = (bf16[128,3584]{1,0:T(8,128)(2,1)S(1)}, bf16[128,3584]{1,0:T(8,128)(2,1)S(1)}, u32[]{:S(2)}, u32[]{:S(2)}) collective-permute-start(bf16[128,3584]{1,0:T(8,128)(2,1)S(1)} %pad_maximum_fusion.1), channel_id=1, source_target_pairs={{0,4},{4,8},{8,12},{12,14},{14,10},{10,6},{6,2},{2,0},{1,5},{5,9},... | collective-permute-start | bytes 2752520 | tf_op jit(solution)/shard_map/sums_0_3_right/ppermute | solution.py:266
  121.9 20.4 %collective-permute-start.21 = (bf16[128,3584]{1,0:T(8,128)(2,1)S(1)}, bf16[128,3584]{1,0:T(8,128)(2,1)S(1)}, u32[]{:S(2)}, u32[]{:S(2)}) collective-permute-start(bf16[128,3584]{1,0:T(8,128)(2,1)S(1)} %pad_maximum_fusion.4), channel_id=1, source_target_pairs={{0,2},{4,0},{8,4},{12,8},{14,12},{10,14},{6,10},{2,6},{1,3},{5,1},... | collective-permute-start | bytes 2752520 | tf_op jit(solution)/shard_map/sums_0_2_left/ppermute | solution.py:266
  123.0 20.2 %collective-permute-start.16 = (bf16[128,3584]{1,0:T(8,128)(2,1)S(1)}, bf16[128,3584]{1,0:T(8,128)(2,1)S(1)}, u32[]{:S(2)}, u32[]{:S(2)}) collective-permute-start(bf16[128,3584]{1,0:T(8,128)(2,1)S(1)} %pad_maximum_fusion.2), channel_id=1, source_target_pairs={{0,4},{4,8},{8,12},{12,14},{14,10},{10,6},{6,2},{2,0},{1,5},{5,9},... | collective-permute-start | bytes 2752520 | tf_op jit(solution)/shard_map/sums_0_2_right/ppermute | solution.py:266
  142.4 8.5 %collective-permute-start.22 = (bf16[64,3584]{1,0:T(8,128)(2,1)S(1)}, bf16[64,3584]{1,0:T(8,128)(2,1)S(1)}, u32[]{:S(2)}, u32[]{:S(2)}) collective-permute-start(bf16[64,3584]{1,0:T(8,128)(2,1)S(1)} %add_convert_fusion.1), channel_id=1, source_target_pairs={{0,2},{4,0},{8,4},{12,8},{14,12},{10,14},{6,10},{2,6},{1,3},{5,1},... | collective-permute-start | bytes 1376264 | tf_op jit(solution)/shard_map/sums_0_1_left/ppermute | solution.py:266
  143.4 8.5 %collective-permute-start.17 = (bf16[64,3584]{1,0:T(8,128)(2,1)S(1)}, bf16[64,3584]{1,0:T(8,128)(2,1)S(1)}, u32[]{:S(2)}, u32[]{:S(2)}) collective-permute-start(bf16[64,3584]{1,0:T(8,128)(2,1)S(1)} %add_convert_fusion.7), channel_id=1, source_target_pairs={{0,4},{4,8},{8,12},{12,14},{14,10},{10,6},{6,2},{2,0},{1,5},{5,9},... | collective-permute-start | bytes 1376264 | tf_op jit(solution)/shard_map/sums_0_1_right/ppermute | solution.py:266
  (9 other events, 79.7 us)

commit v8 on v7

--- a/solution.py
+++ b/solution.py
@@ -331,7 +331,7 @@
     left_low = shift(part["bottom"], -1, f"sums_0_{far}")
     before = part["top"]
     for s in range(far - 1, 1, -1):
-        keys = [(0, s - 1), (0, 1 - s)] + ([(0, 0)] if s == 2 else [])
+        keys = [(0, s - 1), (0, 1 - s)]
         hold(keys, before)
         expert(*keys)
         before = right_top
@@ -344,6 +344,8 @@
         right, left = shift(right, 1, f"sums_0_{s}"), shift(left, -1, f"sums_0_{s}")
         right_top, right_low = right[:mid], right[mid:]
         left_top, left_low = left[:mid], left[mid:]
+    hold([(0, 0)], right_top)
+    expert((0, 0))
     right_top = shift(add(part[1][:mid], right_top), 1, "sums_0_1")
     left_low = shift(add(part[-1][mid:], left_low), -1, "sums_0_1")
 

time: 154 us -> 155 us (level)
  Pallas kernels: 40.6 us -> 42.6 us
    pallas_call x4 -> x5, Pallas kernels: 26.5 us -> 28.5 us  [run_expert(): pl.pallas_call(functools.partial(expert_kernel, sizes, owners), out_shape...]
    unnamed x23 -> x17, local copies, waits for them, and re-layouts: 9.56 us -> 9.54 us
  transfers between devices with their start and end apart: 23 -> 23, of which waited for: 13 -> 15; matrix products, arithmetic and copies ran while one was open for 2% -> 2% of each run, Pallas kernels for 27% -> 27%
where the time goes in v8:
time: 155 us
  waiting for transfers between devices  72.6 us (47%)
  Pallas kernels  42.6 us (27%)
  starting transfers between devices  24.9 us (16%)
  local copies, waits for them, and re-layouts  11.2 us (7%)
  other arithmetic  2.77 us (2%)
    ppermute x20, waiting for transfers between devices, shift(): lax.ppermute(x, 'expert', [(order[i], order[(i + by) % owners]) for i in...  71.5 us
    pallas_call x5, Pallas kernels, run_expert(): pl.pallas_call(functools.partial(expert_kernel, sizes, owners), out_shape...  28.5 us
    ppermute x20, starting transfers between devices, shift(): lax.ppermute(x, 'expert', [(order[i], order[(i + by) % owners]) for i in...  24.2 us
    unnamed x17, local copies, waits for them, and re-layouts  9.54 us
    pallas_call x1, Pallas kernels, keep(): pl.pallas_call(keep_kernel, out_shape=[pltpu.VMEM(own.shape, own.dtype)]...  8.52 us
    pallas_call x1, Pallas kernels, dequantize(): pl.pallas_call(dequantize_kernel, grid=(tiles, 3), out_shape=jax.ShapeDty...  3.99 us
  transfers between devices with their start and end apart: 23, of which 15 were waited for; matrix products, arithmetic and copies ran while one was open for 2% of the time, Pallas kernels for 27%

profile of v8, /device:TPU:0, one launch (start us, length us, event | category | flops | bytes accessed | tf_op | source)
XLA Modules:
  0.0 154.9 jit_solution(17386541420578130849)
XLA Ops:
  0.5 2.5 %collective-permute-start.3 = (bf16[128,3584]{1,0:T(8,128)(2,1)}, bf16[128,3584]{1,0:T(8,128)(2,1)S(1)}, u32[]{:S(2)}, u32[]{:S(2)}) collective-permute-start(bf16[128,3584]{1,0:T(8,128)(2,1)} %param.8), channel_id=1, source_target_pairs={{0,2},{4,0},{8,4},{12,8},{14,12},{10,14},{6,10},{2,6},{1,3},{5,1},... | collective-permute-start | bytes 2752520 | tf_op jit(solution)/shard_map/tokens_0_1_left/ppermute | solution.py:266
  4.2 1.6 %route.1 = bf16[128,128]{1,0:T(8,128)(2,1)} custom-call(s32[1]{0:T(128)S(6)} %copy.14.hot_ref, s32[4,128]{1,0:T(4,128)} %bitcast.13, f32[4,128]{1,0:T(4,128)} %bitcast.14), custom_call_target="tpu_custom_call" | custom-call | tf_op jit(solution)/shard_map/route/pallas_call | solution.py:110
  5.7 1.7 %collective-permute-start.4 = (bf16[128,128]{1,0:T(8,128)(2,1)}, bf16[128,128]{1,0:T(8,128)(2,1)S(1)}, u32[]{:S(2)}, u32[]{:S(2)}) collective-permute-start(bf16[128,128]{1,0:T(8,128)(2,1)} %route.1), channel_id=1, source_target_pairs={{0,2},{4,0},{8,4},{12,8},{14,12},{10,14},{6,10},{2,6},{1,3},{5,1},... | collective-permute-start | bytes 98312 | tf_op jit(solution)/shard_map/weights_0_1_left/ppermute | solution.py:266
  7.4 17.0 %collective-permute-done.3 = bf16[128,3584]{1,0:T(8,128)(2,1)S(1)} collective-permute-done((bf16[128,3584]{1,0:T(8,128)(2,1)}, bf16[128,3584]{1,0:T(8,128)(2,1)S(1)}, u32[]{:S(2)}, u32[]{:S(2)}) %collective-permute-start.3) | collective-permute-done | bytes 917536 | tf_op jit(solution)/shard_map/tokens_0_1_left/ppermute | solution.py:266
  24.4 1.9 %collective-permute-start.7 = (bf16[128,128]{1,0:T(8,128)(2,1)}, bf16[128,128]{1,0:T(8,128)(2,1)S(1)}, u32[]{:S(2)}, u32[]{:S(2)}) collective-permute-start(bf16[128,128]{1,0:T(8,128)(2,1)} %route.1), channel_id=1, source_target_pairs={{0,4},{4,8},{8,12},{12,14},{14,10},{10,6},{6,2},{2,0},{1,5},{5,9},... | collective-permute-start | bytes 98312 | tf_op jit(solution)/shard_map/weights_0_1_right/ppermute | solution.py:266
  26.8 1.8 %collective-permute-done.7 = bf16[128,128]{1,0:T(8,128)(2,1)S(1)} collective-permute-done((bf16[128,128]{1,0:T(8,128)(2,1)}, bf16[128,128]{1,0:T(8,128)(2,1)S(1)}, u32[]{:S(2)}, u32[]{:S(2)}) %collective-permute-start.7) | collective-permute-done | bytes 32800 | tf_op jit(solution)/shard_map/weights_0_1_right/ppermute | solution.py:266
  28.6 2.0 %collective-permute-start.8 = (bf16[128,3712]{1,0:T(8,128)(2,1)S(1)}, bf16[128,3712]{1,0:T(8,128)(2,1)}, u32[]{:S(2)}, u32[]{:S(2)}) collective-permute-start(bf16[128,3712]{1,0:T(8,128)(2,1)S(1)} %constant_dynamic-update-slice_fusion.2.refs_1_), channel_id=1, source_target_pairs={{0,4},{4,8},{8,12},{12,14},{14,10},{10,6},{6,2},{2,0},{1,5},{5,9},... | collective-permute-start | bytes 2850824 | tf_op jit(solution)/shard_map/tokens_0_2_right/ppermute | solution.py:266
  30.7 3.1 %copy-done.1 = bf16[1,2,3584,512]{3,2,1,0:T(8,128)(2,1)S(1)} copy-done((bf16[1,2,3584,512]{3,2,1,0:T(8,128)(2,1)S(1)}, bf16[1,2,3584,512]{3,2,1,0:T(8,128)(2,1)}, u32[]{:S(2)}) %copy-start.1) | copy-done | bytes 7340056
  33.7 2.0 %copy-done.2 = bf16[1,512,3584]{2,1,0:T(8,128)(2,1)S(1)} copy-done((bf16[1,512,3584]{2,1,0:T(8,128)(2,1)S(1)}, bf16[1,512,3584]{2,1,0:T(8,128)(2,1)}, u32[]{:S(2)}) %copy-start.2) | copy-done | bytes 3670040
  35.8 4.0 %dequantize.1.own_from = bf16[2,5376,512]{2,1,0:T(8,128)(2,1)S(1)} custom-call(f32[2,28,4]{2,1,0:T(8,128)S(1)} %bitcast.11, f32[4,28]{1,0:T(4,128)S(1)} %bitcast.12, bf16[2,3584,512]{2,1,0:T(8,128)(2,1)S(1)} %bitcast.8, bf16[512,3584]{1,0:T(8,128)(2,1)S(1)} %bitcast.10), custom_call_target="tpu_custom_call" | custom-call | flops 11010048 | bytes 22020096 | tf_op jit(solution)/shard_map/dequantize/pallas_call | solution.py:66
  39.8 4.2 %copy-done = bf16[2,5376,512]{2,1,0:T(8,128)(2,1)} copy-done((bf16[2,5376,512]{2,1,0:T(8,128)(2,1)}, bf16[2,5376,512]{2,1,0:T(8,128)(2,1)S(1)}, u32[]{:S(2)}) %copy-start) | copy-done | bytes 11010072
  44.0 4.7 %collective-permute-done.5.refs_0_ = bf16[128,3712]{1,0:T(8,128)(2,1)} collective-permute-done((bf16[128,3712]{1,0:T(8,128)(2,1)S(1)}, bf16[128,3712]{1,0:T(8,128)(2,1)}, u32[]{:S(2)}, u32[]{:S(2)}) %collective-permute-start.5) | collective-permute-done | bytes 950304 | tf_op jit(solution)/shard_map/tokens_0_2_left/ppermute | solution.py:266
  53.5 8.5 %keep.1 = (bf16[2,5376,512]{2,1,0:T(8,128)(2,1)S(1)}, bf16[2,5376,512]{2,1,0:T(8,128)(2,1)S(1)}) custom-call(f32[2,28,4]{2,1,0:T(8,128)S(1)} %reshape.26.in_scale, f32[4,28]{1,0:T(4,128)S(1)} %reshape.27.out_scale, bf16[2,5376,512]{2,1,0:T(8,128)(2,1)} %copy-done, bf16[2,3584,512]{2,1,0:T(8,128)(2,1)} %collective-permute-done.1.in_raw, ...), custom_call_target="tpu_custom_call" | custom-call | tf_op jit(solution)/shard_map/keep/pallas_call | solution.py:210
  62.1 7.9 %collective-permute-done.11.refs_0_ = bf16[128,3712]{1,0:T(8,128)(2,1)S(1)} collective-permute-done((bf16[128,3712]{1,0:T(8,128)(2,1)}, bf16[128,3712]{1,0:T(8,128)(2,1)S(1)}, u32[]{:S(2)}, u32[]{:S(2)}) %collective-permute-start.11) | collective-permute-done | bytes 950304 | tf_op jit(solution)/shard_map/tokens_0_3_left/ppermute | solution.py:266
  74.6 7.5 %expert.5 = (bf16[128,3584]{1,0:T(8,128)(2,1)S(1)}, bf16[128,3584]{1,0:T(8,128)(2,1)S(1)}) custom-call(s32[1]{0:T(128)} %bitcast.who_ref, bf16[2,5376,512]{2,1,0:T(8,128)(2,1)S(1)} %get-tuple-element.34.own, bf16[2,5376,512]{2,1,0:T(8,128)(2,1)S(1)} %get-tuple-element.35.sib, bf16[128,3712]{1,0:T(8,128)(2,1)S(1)} %collective-permute-done.11.refs_0_, ...), custom_call_target="tpu_custom_call" | custom-call | flops 5637144576 | bytes 22020096 | tf_op jit(solution)/shard_map/expert/pallas_call | solution.py:233
  84.2 3.5 %expert.6 = (bf16[64,3584]{1,0:T(8,128)(2,1)S(1)}, bf16[64,3584]{1,0:T(8,128)(2,1)S(1)}) custom-call(s32[1]{0:T(128)} %bitcast.who_ref, bf16[2,5376,512]{2,1,0:T(8,128)(2,1)S(1)} %get-tuple-element.34.own, bf16[2,5376,512]{2,1,0:T(8,128)(2,1)S(1)} %get-tuple-element.35.sib, bf16[64,3712]{1,0:T(8,128)(2,1)S(1)} %collective-permute-done.10.refs_0_, ...), custom_call_target="tpu_custom_call" | custom-call | flops 2818572288 | bytes 22020096 | tf_op jit(solution)/shard_map/expert/pallas_call | solution.py:233
  89.8 7.7 %expert.7 = (bf16[128,3584]{1,0:T(8,128)(2,1)S(1)}, bf16[128,3584]{1,0:T(8,128)(2,1)S(1)}) custom-call(s32[1]{0:T(128)} %bitcast.who_ref, bf16[2,5376,512]{2,1,0:T(8,128)(2,1)S(1)} %get-tuple-element.34.own, bf16[2,5376,512]{2,1,0:T(8,128)(2,1)S(1)} %get-tuple-element.35.sib, bf16[128,3712]{1,0:T(8,128)(2,1)} %collective-permute-done.5.refs_0_, ...), custom_call_target="tpu_custom_call" | custom-call | flops 5637144576 | bytes 22020096 | tf_op jit(solution)/shard_map/expert/pallas_call | solution.py:233
  97.8 4.1 %collective-permute-done.19 = bf16[64,3584]{1,0:T(8,128)(2,1)S(1)} collective-permute-done((bf16[64,3584]{1,0:T(8,128)(2,1)S(1)}, bf16[64,3584]{1,0:T(8,128)(2,1)S(1)}, u32[]{:S(2)}, u32[]{:S(2)}) %collective-permute-start.19) | collective-permute-done | bytes 458784 | tf_op jit(solution)/shard_map/sums_0_4_left/ppermute | solution.py:266
  104.7 6.3 %expert.8 = (bf16[128,3584]{1,0:T(8,128)(2,1)S(1)}, bf16[128,3584]{1,0:T(8,128)(2,1)S(1)}) custom-call(s32[1]{0:T(128)} %bitcast.who_ref, bf16[2,5376,512]{2,1,0:T(8,128)(2,1)S(1)} %get-tuple-element.34.own, bf16[2,5376,512]{2,1,0:T(8,128)(2,1)S(1)} %get-tuple-element.35.sib, bf16[128,3712]{1,0:T(8,128)(2,1)S(1)} %constant_dynamic-update-slice_fusion.refs_0_, ...), custom_call_target="tpu_custom_call" | custom-call | flops 5637144576 | bytes 22020096 | tf_op jit(solution)/shard_map/expert/pallas_call | solution.py:233
  111.0 11.4 %collective-permute-done.20 = bf16[128,3584]{1,0:T(8,128)(2,1)S(1)} collective-permute-done((bf16[128,3584]{1,0:T(8,128)(2,1)S(1)}, bf16[128,3584]{1,0:T(8,128)(2,1)S(1)}, u32[]{:S(2)}, u32[]{:S(2)}) %collective-permute-start.20) | collective-permute-done | bytes 917536 | tf_op jit(solution)/shard_map/sums_0_3_left/ppermute | solution.py:266
  125.3 17.8 %collective-permute-done.21 = bf16[128,3584]{1,0:T(8,128)(2,1)S(1)} collective-permute-done((bf16[128,3584]{1,0:T(8,128)(2,1)S(1)}, bf16[128,3584]{1,0:T(8,128)(2,1)S(1)}, u32[]{:S(2)}, u32[]{:S(2)}) %collective-permute-start.21) | collective-permute-done | bytes 917536 | tf_op jit(solution)/shard_map/sums_0_2_left/ppermute | solution.py:266
  145.8 3.5 %expert.9 = bf16[128,3584]{1,0:T(8,128)(2,1)S(1)} custom-call(s32[1]{0:T(128)} %bitcast.who_ref, bf16[2,5376,512]{2,1,0:T(8,128)(2,1)S(1)} %get-tuple-element.34.own, bf16[2,5376,512]{2,1,0:T(8,128)(2,1)S(1)} %get-tuple-element.35.sib, bf16[128,3712]{1,0:T(8,128)(2,1)S(1)} %pad_maximum_fusion.refs_0_), custom_call_target="tpu_custom_call" | custom-call | flops 2818572288 | bytes 22020096 | tf_op jit(solution)/shard_map/expert/pallas_call | solution.py:233
  149.4 2.3 %collective-permute-done.22 = bf16[64,3584]{1,0:T(8,128)(2,1)S(1)} collective-permute-done((bf16[64,3584]{1,0:T(8,128)(2,1)S(1)}, bf16[64,3584]{1,0:T(8,128)(2,1)S(1)}, u32[]{:S(2)}, u32[]{:S(2)}) %collective-permute-start.22) | collective-permute-done | bytes 458784 | tf_op jit(solution)/shard_map/sums_0_1_left/ppermute | solution.py:266
  151.7 1.9 %collective-permute-done.17 = bf16[64,3584]{1,0:T(8,128)(2,1)S(1)} collective-permute-done((bf16[64,3584]{1,0:T(8,128)(2,1)S(1)}, bf16[64,3584]{1,0:T(8,128)(2,1)S(1)}, u32[]{:S(2)}, u32[]{:S(2)}) %collective-permute-start.17) | collective-permute-done | bytes 458784 | tf_op jit(solution)/shard_map/sums_0_1_right/ppermute | solution.py:266
  (75 shorter events, 25.2 us)
Async XLA Ops:
  0.0 53.5 %collective-permute-start.1 = (bf16[2,3584,512]{2,1,0:T(8,128)(2,1)}, bf16[2,3584,512]{2,1,0:T(8,128)(2,1)}, u32[]{:S(2)}, u32[]{:S(2)}) collective-permute-start(bf16[2,3584,512]{2,1,0:T(8,128)(2,1)} %bitcast.7), channel_id=1, source_target_pairs={{0,1},{1,0},{2,3},{3,2},{4,5},{5,4},{6,7},{7,6},{8,9},{9,8},{10,11... | collective-permute-start | bytes 22020104 | tf_op jit(solution)/shard_map/ppermute | solution.py:306
  0.5 24.0 %collective-permute-start.3 = (bf16[128,3584]{1,0:T(8,128)(2,1)}, bf16[128,3584]{1,0:T(8,128)(2,1)S(1)}, u32[]{:S(2)}, u32[]{:S(2)}) collective-permute-start(bf16[128,3584]{1,0:T(8,128)(2,1)} %param.8), channel_id=1, source_target_pairs={{0,2},{4,0},{8,4},{12,8},{14,12},{10,14},{6,10},{2,6},{1,3},{5,1},... | collective-permute-start | bytes 2752520 | tf_op jit(solution)/shard_map/tokens_0_1_left/ppermute | solution.py:266
  3.0 50.6 %collective-permute-start.2 = (bf16[512,3584]{1,0:T(8,128)(2,1)}, bf16[512,3584]{1,0:T(8,128)(2,1)}, u32[]{:S(2)}, u32[]{:S(2)}) collective-permute-start(bf16[512,3584]{1,0:T(8,128)(2,1)} %bitcast.9), channel_id=1, source_target_pairs={{0,1},{1,0},{2,3},{3,2},{4,5},{5,4},{6,7},{7,6},{8,9},{9,8},{10,11... | collective-permute-start | bytes 11010056 | tf_op jit(solution)/shard_map/ppermute | solution.py:306
  3.2 23.5 %collective-permute-start.6 = (bf16[128,3584]{1,0:T(8,128)(2,1)}, bf16[128,3584]{1,0:T(8,128)(2,1)S(1)}, u32[]{:S(2)}, u32[]{:S(2)}) collective-permute-start(bf16[128,3584]{1,0:T(8,128)(2,1)} %param.8), channel_id=1, source_target_pairs={{0,4},{4,8},{8,12},{12,14},{14,10},{10,6},{6,2},{2,0},{1,5},{5,9},... | collective-permute-start | bytes 2752520 | tf_op jit(solution)/shard_map/tokens_0_1_right/ppermute | solution.py:266
  5.7 24.9 %copy-start.3 = (f32[1,4,28]{2,1,0:T(4,128)S(1)}, f32[1,4,28]{2,1,0:T(4,128)}, u32[]{:S(2)}) copy-start(f32[1,4,28]{2,1,0:T(4,128)} %param.15) | copy-start | bytes 1348
  5.7 20.7 %collective-permute-start.4 = (bf16[128,128]{1,0:T(8,128)(2,1)}, bf16[128,128]{1,0:T(8,128)(2,1)S(1)}, u32[]{:S(2)}, u32[]{:S(2)}) collective-permute-start(bf16[128,128]{1,0:T(8,128)(2,1)} %route.1), channel_id=1, source_target_pairs={{0,2},{4,0},{8,4},{12,8},{14,12},{10,14},{6,10},{2,6},{1,3},{5,1},... | collective-permute-start | bytes 98312 | tf_op jit(solution)/shard_map/weights_0_1_left/ppermute | solution.py:266
  24.4 4.1 %collective-permute-start.7 = (bf16[128,128]{1,0:T(8,128)(2,1)}, bf16[128,128]{1,0:T(8,128)(2,1)S(1)}, u32[]{:S(2)}, u32[]{:S(2)}) collective-permute-start(bf16[128,128]{1,0:T(8,128)(2,1)} %route.1), channel_id=1, source_target_pairs={{0,4},{4,8},{8,12},{12,14},{14,10},{10,6},{6,2},{2,0},{1,5},{5,9},... | collective-permute-start | bytes 98312 | tf_op jit(solution)/shard_map/weights_0_1_right/ppermute | solution.py:266
  26.4 22.2 %collective-permute-start.5 = (bf16[128,3712]{1,0:T(8,128)(2,1)S(1)}, bf16[128,3712]{1,0:T(8,128)(2,1)}, u32[]{:S(2)}, u32[]{:S(2)}) collective-permute-start(bf16[128,3712]{1,0:T(8,128)(2,1)S(1)} %constant_dynamic-update-slice_fusion.refs_0_), channel_id=1, source_target_pairs={{0,2},{4,0},{8,4},{12,8},{14,12},{10,14},{6,10},{2,6},{1,3},{5,1},... | collective-permute-start | bytes 2850824 | tf_op jit(solution)/shard_map/tokens_0_2_left/ppermute | solution.py:266
  28.6 21.7 %collective-permute-start.8 = (bf16[128,3712]{1,0:T(8,128)(2,1)S(1)}, bf16[128,3712]{1,0:T(8,128)(2,1)}, u32[]{:S(2)}, u32[]{:S(2)}) collective-permute-start(bf16[128,3712]{1,0:T(8,128)(2,1)S(1)} %constant_dynamic-update-slice_fusion.2.refs_1_), channel_id=1, source_target_pairs={{0,4},{4,8},{8,12},{12,14},{14,10},{10,6},{6,2},{2,0},{1,5},{5,9},... | collective-permute-start | bytes 2850824 | tf_op jit(solution)/shard_map/tokens_0_2_right/ppermute | solution.py:266
  48.7 21.3 %collective-permute-start.11 = (bf16[128,3712]{1,0:T(8,128)(2,1)}, bf16[128,3712]{1,0:T(8,128)(2,1)S(1)}, u32[]{:S(2)}, u32[]{:S(2)}) collective-permute-start(bf16[128,3712]{1,0:T(8,128)(2,1)} %collective-permute-done.5.refs_0_), channel_id=1, source_target_pairs={{0,2},{4,0},{8,4},{12,8},{14,12},{10,14},{6,10},{2,6},{1,3},{5,1},... | collective-permute-start | bytes 2850824 | tf_op jit(solution)/shard_map/tokens_0_3_left/ppermute | solution.py:266
  50.3 21.0 %collective-permute-start.9 = (bf16[128,3712]{1,0:T(8,128)(2,1)}, bf16[128,3712]{1,0:T(8,128)(2,1)}, u32[]{:S(2)}, u32[]{:S(2)}) collective-permute-start(bf16[128,3712]{1,0:T(8,128)(2,1)} %collective-permute-done.8.refs_1_), channel_id=1, source_target_pairs={{0,4},{4,8},{8,12},{12,14},{14,10},{10,6},{6,2},{2,0},{1,5},{5,9},... | collective-permute-start | bytes 2850824 | tf_op jit(solution)/shard_map/tokens_0_3_right/ppermute | solution.py:266
  52.1 1.2 collective-permute-start
  71.4 12.9 %collective-permute-start.12 = (bf16[64,3712]{1,0:T(8,128)(2,1)S(1)}, bf16[64,3712]{1,0:T(8,128)(2,1)S(1)}, u32[]{:S(2)}, u32[]{:S(2)}) collective-permute-start(bf16[64,3712]{1,0:T(8,128)(2,1)S(1)} %slice.97), channel_id=1, source_target_pairs={{0,2},{4,0},{8,4},{12,8},{14,12},{10,14},{6,10},{2,6},{1,3},{5,1},... | collective-permute-start | bytes 1425416 | tf_op jit(solution)/shard_map/tokens_0_4_left/ppermute | solution.py:266
  73.9 10.4 %collective-permute-start.10 = (bf16[64,3712]{1,0:T(8,128)(2,1)S(1)}, bf16[64,3712]{1,0:T(8,128)(2,1)S(1)}, u32[]{:S(2)}, u32[]{:S(2)}) collective-permute-start(bf16[64,3712]{1,0:T(8,128)(2,1)S(1)} %slice.96), channel_id=1, source_target_pairs={{0,4},{4,8},{8,12},{12,14},{14,10},{10,6},{6,2},{2,0},{1,5},{5,9},... | collective-permute-start | bytes 1425416 | tf_op jit(solution)/shard_map/tokens_0_4_right/ppermute | solution.py:266
  82.1 15.5 %collective-permute-start.18 = (bf16[64,3584]{1,0:T(8,128)(2,1)S(1)}, bf16[64,3584]{1,0:T(8,128)(2,1)S(1)}, u32[]{:S(2)}, u32[]{:S(2)}) collective-permute-start(bf16[64,3584]{1,0:T(8,128)(2,1)S(1)} %slice.110), channel_id=1, source_target_pairs={{0,2},{4,0},{8,4},{12,8},{14,12},{10,14},{6,10},{2,6},{1,3},{5,1},... | collective-permute-start | bytes 1376264 | tf_op jit(solution)/shard_map/sums_1_3_left/ppermute | solution.py:266
  83.5 14.2 %collective-permute-start.14 = (bf16[64,3584]{1,0:T(8,128)(2,1)S(1)}, bf16[64,3584]{1,0:T(8,128)(2,1)S(1)}, u32[]{:S(2)}, u32[]{:S(2)}) collective-permute-start(bf16[64,3584]{1,0:T(8,128)(2,1)S(1)} %slice.101), channel_id=1, source_target_pairs={{0,4},{4,8},{8,12},{12,14},{14,10},{10,6},{6,2},{2,0},{1,5},{5,9},... | collective-permute-start | bytes 1376264 | tf_op jit(solution)/shard_map/sums_1_3_right/ppermute | solution.py:266
  87.8 16.1 %collective-permute-start.13 = (bf16[64,3584]{1,0:T(8,128)(2,1)S(1)}, bf16[64,3584]{1,0:T(8,128)(2,1)S(1)}, u32[]{:S(2)}, u32[]{:S(2)}) collective-permute-start(bf16[64,3584]{1,0:T(8,128)(2,1)S(1)} %get-tuple-element.43), channel_id=1, source_target_pairs={{0,4},{4,8},{8,12},{12,14},{14,10},{10,6},{6,2},{2,0},{1,5},{5,9},... | collective-permute-start | bytes 1376264 | tf_op jit(solution)/shard_map/sums_0_4_right/ppermute | solution.py:266
  88.9 13.0 %collective-permute-start.19 = (bf16[64,3584]{1,0:T(8,128)(2,1)S(1)}, bf16[64,3584]{1,0:T(8,128)(2,1)S(1)}, u32[]{:S(2)}, u32[]{:S(2)}) collective-permute-start(bf16[64,3584]{1,0:T(8,128)(2,1)S(1)} %get-tuple-element.54), channel_id=1, source_target_pairs={{0,2},{4,0},{8,4},{12,8},{14,12},{10,14},{6,10},{2,6},{1,3},{5,1},... | collective-permute-start | bytes 1376264 | tf_op jit(solution)/shard_map/sums_0_4_left/ppermute | solution.py:266
  102.1 20.2 %collective-permute-start.20 = (bf16[128,3584]{1,0:T(8,128)(2,1)S(1)}, bf16[128,3584]{1,0:T(8,128)(2,1)S(1)}, u32[]{:S(2)}, u32[]{:S(2)}) collective-permute-start(bf16[128,3584]{1,0:T(8,128)(2,1)S(1)} %pad_maximum_fusion.3), channel_id=1, source_target_pairs={{0,2},{4,0},{8,4},{12,8},{14,12},{10,14},{6,10},{2,6},{1,3},{5,1},... | collective-permute-start | bytes 2752520 | tf_op jit(solution)/shard_map/sums_0_3_left/ppermute | solution.py:266
  104.0 20.2 %collective-permute-start.15 = (bf16[128,3584]{1,0:T(8,128)(2,1)S(1)}, bf16[128,3584]{1,0:T(8,128)(2,1)S(1)}, u32[]{:S(2)}, u32[]{:S(2)}) collective-permute-start(bf16[128,3584]{1,0:T(8,128)(2,1)S(1)} %pad_maximum_fusion.1), channel_id=1, source_target_pairs={{0,4},{4,8},{8,12},{12,14},{14,10},{10,6},{6,2},{2,0},{1,5},{5,9},... | collective-permute-start | bytes 2752520 | tf_op jit(solution)/shard_map/sums_0_3_right/ppermute | solution.py:266
  122.6 20.4 %collective-permute-start.21 = (bf16[128,3584]{1,0:T(8,128)(2,1)S(1)}, bf16[128,3584]{1,0:T(8,128)(2,1)S(1)}, u32[]{:S(2)}, u32[]{:S(2)}) collective-permute-start(bf16[128,3584]{1,0:T(8,128)(2,1)S(1)} %pad_maximum_fusion.4), channel_id=1, source_target_pairs={{0,2},{4,0},{8,4},{12,8},{14,12},{10,14},{6,10},{2,6},{1,3},{5,1},... | collective-permute-start | bytes 2752520 | tf_op jit(solution)/shard_map/sums_0_2_left/ppermute | solution.py:266
  124.6 20.2 %collective-permute-start.16 = (bf16[128,3584]{1,0:T(8,128)(2,1)S(1)}, bf16[128,3584]{1,0:T(8,128)(2,1)S(1)}, u32[]{:S(2)}, u32[]{:S(2)}) collective-permute-start(bf16[128,3584]{1,0:T(8,128)(2,1)S(1)} %pad_maximum_fusion.2), channel_id=1, source_target_pairs={{0,4},{4,8},{8,12},{12,14},{14,10},{10,6},{6,2},{2,0},{1,5},{5,9},... | collective-permute-start | bytes 2752520 | tf_op jit(solution)/shard_map/sums_0_2_right/ppermute | solution.py:266
  143.2 8.5 %collective-permute-start.22 = (bf16[64,3584]{1,0:T(8,128)(2,1)S(1)}, bf16[64,3584]{1,0:T(8,128)(2,1)S(1)}, u32[]{:S(2)}, u32[]{:S(2)}) collective-permute-start(bf16[64,3584]{1,0:T(8,128)(2,1)S(1)} %add_convert_fusion.1), channel_id=1, source_target_pairs={{0,2},{4,0},{8,4},{12,8},{14,12},{10,14},{6,10},{2,6},{1,3},{5,1},... | collective-permute-start | bytes 1376264 | tf_op jit(solution)/shard_map/sums_0_1_left/ppermute | solution.py:266
  144.9 8.8 %collective-permute-start.17 = (bf16[64,3584]{1,0:T(8,128)(2,1)S(1)}, bf16[64,3584]{1,0:T(8,128)(2,1)S(1)}, u32[]{:S(2)}, u32[]{:S(2)}) collective-permute-start(bf16[64,3584]{1,0:T(8,128)(2,1)S(1)} %add_convert_fusion.7), channel_id=1, source_target_pairs={{0,4},{4,8},{8,12},{12,14},{14,10},{10,6},{6,2},{2,0},{1,5},{5,9},... | collective-permute-start | bytes 1376264 | tf_op jit(solution)/shard_map/sums_0_1_right/ppermute | solution.py:266
  (6 other events, 76.7 us)
